TPU v7x, 32 devices: a whole 2x2x4 slice. The times are simulated.
32 devices in a mesh: path: 8 (over z, y), dim: 4 (over x, core).
Axes of the slice: x: 2, y: 2, z: 4, core: 2. Of those that a mesh axis runs over, the one named last changes fastest.
Arguments:
- inner_noise: bfloat16 [64, 1000, 512], P('path', 'dim'), may hold values from -6 to 6
- outer_noise: bfloat16 [1000, 512], P('dim'), may hold values from -6 to 6
- start: float32 [1000], P('dim'), may hold values from 0.8 to 1.25
- vol: float32 [1000], P('dim'), may hold values from 0.1 to 0.4
- times: float32 [512], replicated, may hold values from 0.1 to 0.9
Outputs:
- root_value: float32 [1], replicated
- root_grad: float32 [1000], P('dim')
- point_value: float32 [512], P('path')
- point_grad: float32 [1000, 512], P('dim', 'path')
All inputs are finite; a program needn't handle non-finite values.
Results may differ from a plain program's by a relative error of at most 0.0003.
Values sent between devices are 32-bit elements; how exact they have to be, the bound alone decides.
No kernel may reach another device: no remote copies, remote signals or barrier semaphores. Data moves between devices by JAX's collectives and lax.ppermute only.
A program may use at most 64 MiB of HBM per device.

v0:
```python
import jax
import jax.numpy as jnp
from jax import lax
from jax.sharding import PartitionSpec as P

drift = 0.02
delta = 2.0 / 3.0
rate_free = 0.02
gamma_high = 0.2
gamma_low = 0.02
value_high = 0.4
value_low = 0.7


def driver_of(value):
    slope = jnp.clip((value - value_high) / (value_low - value_high), 0.0, 1.0)
    quota = gamma_high + (gamma_low - gamma_high) * slope
    return -(1.0 - delta) * quota * value - rate_free * value


def per_device(inner_noise, outer_noise, start, vol, times):
    paths_here = inner_noise.shape[0]
    points = times.shape[0]
    groups = lax.axis_size("path")
    inner_total = paths_here * groups
    owned = points // groups
    tau = 1.0 - times
    outer = outer_noise.astype(jnp.float32)
    mean_rate = (drift - 0.5 * vol * vol)[:, None]
    outer_state = start[:, None] * jnp.exp(
        mean_rate * times[None, :] + vol[:, None] * jnp.sqrt(times)[None, :] * outer
    )
    shock = inner_noise.astype(jnp.float32)
    level = outer_state[None] * jnp.exp(
        (mean_rate * tau[None, :])[None] + (vol[:, None] * jnp.sqrt(tau)[None, :])[None] * shock
    )
    local_min = jnp.min(level, axis=1)
    payoff = lax.pmin(local_min, "dim")
    totals = jnp.sum(payoff, axis=0)
    moments = jnp.sum(payoff[:, None, :] * shock, axis=0)
    start_index = lax.axis_index("path") * owned
    totals, moments = lax.psum((totals, moments), "path")
    point_value = totals / inner_total
    point_grad_all = moments / (inner_total * vol[:, None] * outer_state * jnp.sqrt(tau)[None, :])
    driver = driver_of(point_value)
    root_value = jnp.sum(totals) / (points * inner_total) + jnp.sum(driver) / points
    terminal = jnp.sum(
        jnp.sqrt(times)[None, :] * outer * totals[None, :] + jnp.sqrt(tau)[None, :] * moments,
        axis=1,
    )
    integral = jnp.sum(driver[None, :] * outer / jnp.sqrt(times)[None, :], axis=1)
    root_grad = terminal / (points * inner_total * vol * start) + integral / (points * vol * start)
    own_value = lax.dynamic_slice_in_dim(point_value, start_index, owned, 0)
    own_grad = lax.dynamic_slice_in_dim(point_grad_all, start_index, owned, 1)
    return (jnp.reshape(root_value, (1,)), root_grad, own_value, own_grad)


def solution(mesh):
    in_specs = (P("path", "dim", None), P("dim", None), P("dim"), P("dim"), P())
    out_specs = (P(), P("dim"), P("path"), P("dim", "path"))
    return jax.shard_map(
        per_device, mesh=mesh, in_specs=in_specs, out_specs=out_specs, check_vma=False
    )
```

profile of v0, /device:TPU:0, one launch (start us, length us, event | category | flops | bytes accessed | tf_op | source)
XLA Modules:
  0.0 111.8 jit_solution(717918163029792968)
XLA Ops:
  7.2 0.0 all-reduce.2.cloned.1.call-start
  7.2 0.7 fusion.17
  7.9 0.7 broadcast_multiply_fusion.3
  8.6 1.2 %fusion.7 = (f32[250,512]{1,0:T(8,128)S(1)}, f32[250,512]{1,0:T(8,128)S(1)}, f32[250,512]{1,0:T(8,128)S(1)}) fusion(bf16[250,512]{1,0:T(8,128)(2,1)} %param.6, f32[512]{0:T(512)S(1)} %get-tuple-element.14, f32[250]{0:T(256)} %param.8, f32[512]{0:T(512)} %param.9, f32[250]{0:T(256)S(1)} %get-tuple-element.18, f32[250]{0:T(256)} %param.7, ...), kind=kLoop, calls=%fused_computation.12 | loop fusion | flops 1024000 | bytes 1803192 | tf_op jit(solution)/shard_map/mul | solution.py:30
  9.8 0.0 copy-start
  9.8 2.4 %fusion.3 = f32[8,512]{1,0:T(8,128)S(1)} fusion(bf16[8,250,512]{2,0,1:T(8,128)(2,1)} %param.5, f32[250,512]{1,0:T(8,128)S(1)} %get-tuple-element.21, f32[250,512]{1,0:T(8,128)S(1)} %get-tuple-element.20, f32[250,512]{1,0:T(8,128)S(1)} %get-tuple-element.19), kind=kLoop, calls=%fused_computation.5 | loop fusion | flops 5115904 | bytes 3600384 | tf_op jit(solution)/shard_map/reduce_min | solution.py:37
  12.2 0.0 copy-start.1
  12.2 12.8 %pmin.7 = f32[8,512]{1,0:T(8,128)S(1)} all-reduce(f32[8,512]{1,0:T(8,128)S(1)} %fusion.3), channel_id=1, replica_groups=mesh['path'=8,'dim'=4] {'dim'}, use_global_device_ids=true, to_apply=%region_1.0 | all-reduce | flops 4096 | bytes 32768 | tf_op jit(solution)/shard_map/pmin | solution.py:38
  25.0 0.0 copy-done
  25.0 0.0 copy-start.2
  25.0 0.0 copy-start.3
  25.0 2.2 %fusion.4 = f32[250,512]{1,0:T(8,128)} fusion(bf16[8,250,512]{2,0,1:T(8,128)(2,1)S(1)} %copy-done, f32[8,512]{1,0:T(8,128)S(1)} %pmin.7), kind=kLoop, calls=%fused_computation.6 | loop fusion | flops 2944000 | bytes 2576384 | tf_op jit(solution)/shard_map/reduce_sum | solution.py:40
  27.2 0.0 all-reduce.2.cloned.1.call-update
  27.3 0.1 dynamic-slice
  27.3 22.0 %psum.14 = f32[512]{0:T(512)S(1)} all-reduce(f32[512]{0:T(512)S(1)} %reduce_sum.54), channel_id=1, replica_groups=mesh['path'=8,'dim'=4] {'path'}, use_global_device_ids=true, to_apply=%region_3.0 | all-reduce | flops 512 | bytes 4096 | tf_op jit(solution)/shard_map/psum | solution.py:42
  49.3 0.6 fusion.16
  49.9 0.6 dynamic_slice.6
  51.8 48.3 %all-reduce.2.cloned.1.call-done = f32[250,512]{1,0:T(8,128)} async-done(((f32[250,512]{1,0:T(8,128)}), f32[250,512]{1,0:T(8,128)}) %all-reduce.2.cloned.1.call-update) | async-done | bytes 512016 | tf_op jit(solution)/shard_map/psum | solution.py:42
  100.2 1.1 dynamic-slice_divide_fusion
  101.2 0.7 copy.13
  101.9 0.0 copy-done.1
  101.9 1.3 %fusion.10 = (f32[250]{0:T(256)S(1)}, f32[250]{0:T(256)S(1)}) fusion(bf16[250,512]{1,0:T(8,128)(2,1)S(1)} %copy-done.1, f32[250,512]{1,0:T(8,128)} %all-reduce.2.cloned.1.call-done, f32[512]{0:T(512)S(1)} %psum.14, f32[512]{0:T(512)S(1)} %get-tuple-element.15, f32[512]{0:T(512)S(1)} %get-tuple-element.14, f32[512]{0:T(512)S(1)} %get-tuple-element.11), kind=kLoop, calls=%fused_computation.15 | loop fusion | flops 1151500 | bytes 778192 | tf_op jit(solution)/shard_map/reduce_sum | solution.py:47
  103.3 0.0 copy-done.2
  103.3 0.0 copy-done.3
  103.3 0.6 divide_add_fusion
  (1 shorter events, 0.0 us)
Async XLA Ops:
  7.2 93.0 %all-reduce.2.cloned.1.call-start = ((), (), s32[]{:S(2)}) async-start(), calls=%async_computation | async-start | bytes 1048576 | tf_op jit(solution)/shard_map/psum | solution.py:42
  9.8 15.2 %copy-start = (bf16[8,250,512]{2,0,1:T(8,128)(2,1)S(1)}, bf16[8,250,512]{2,0,1:T(8,128)(2,1)}, u32[]{:S(2)}) copy-start(bf16[8,250,512]{2,0,1:T(8,128)(2,1)} %param.5) | copy-start | bytes 6144004
  12.2 89.7 %copy-start.1 = (bf16[250,512]{1,0:T(8,128)(2,1)S(1)}, bf16[250,512]{1,0:T(8,128)(2,1)}, u32[]{:S(2)}) copy-start(bf16[250,512]{1,0:T(8,128)(2,1)} %param.6) | copy-start | bytes 768004
  25.0 78.2 %copy-start.2 = (f32[250]{0:T(256)S(1)}, f32[250]{0:T(256)}, u32[]{:S(2)}) copy-start(f32[250]{0:T(256)} %param.8) | copy-start | bytes 3004
  25.0 78.2 %copy-start.3 = (f32[250]{0:T(256)S(1)}, f32[250]{0:T(256)}, u32[]{:S(2)}) copy-start(f32[250]{0:T(256)} %param.7) | copy-start | bytes 3004
Sparse Core Ops, SparseCore 0:
  27.4 72.7 all-reduce.1
where the time goes:
time: 112 us
  waiting for transfers between devices  48.4 us (43%)
  blocking collectives  34.8 us (31%)
  between operations  16.5 us (15%)
  other arithmetic  10.7 us (10%)
  local copies, waits for them, and re-layouts  1.39 us (1%)
    psum x1, waiting for transfers between devices, per_device(): totals, moments = lax.psum((totals, moments), 'path')  48.3 us
    psum x1, blocking collectives, per_device(): totals, moments = lax.psum((totals, moments), 'path')  22 us
    pmin x1, blocking collectives, per_device(): payoff = lax.pmin(local_min, 'dim')  12.8 us
    reduce_min x1, other arithmetic, per_device(): local_min = jnp.min(level, axis=1)  2.37 us
  transfers between devices with their start and end apart: 1, of which 1 were waited for; matrix products, arithmetic and copies ran while one was open for 1% of the time, Pallas kernels for 0%

commit v1 on v0

--- a/solution.py
+++ b/solution.py
@@ -1,6 +1,10 @@
+import functools
+
 import jax
 import jax.numpy as jnp
 from jax import lax
+from jax.experimental import pallas as pl
+from jax.experimental.pallas import tpu as pltpu
 from jax.sharding import PartitionSpec as P
 
 drift = 0.02
@@ -11,6 +15,11 @@
 value_high = 0.4
 value_low = 0.7
 
+LANES = 128
+HALF = LANES // 2
+EXTRA = 8
+F32 = jnp.float32
+
 
 def driver_of(value):
     slope = jnp.clip((value - value_high) / (value_low - value_high), 0.0, 1.0)
@@ -18,24 +27,27 @@
     return -(1.0 - delta) * quota * value - rate_free * value
 
 
-def per_device(inner_noise, outer_noise, start, vol, times):
+def is_power(n):
+    return n > 0 and n & (n - 1) == 0
+
+
+def general(inner_noise, outer_noise, start, vol, times):
     paths_here = inner_noise.shape[0]
     points = times.shape[0]
     groups = lax.axis_size("path")
     inner_total = paths_here * groups
     owned = points // groups
     tau = 1.0 - times
-    outer = outer_noise.astype(jnp.float32)
+    outer = outer_noise.astype(F32)
     mean_rate = (drift - 0.5 * vol * vol)[:, None]
     outer_state = start[:, None] * jnp.exp(
         mean_rate * times[None, :] + vol[:, None] * jnp.sqrt(times)[None, :] * outer
     )
-    shock = inner_noise.astype(jnp.float32)
+    shock = inner_noise.astype(F32)
     level = outer_state[None] * jnp.exp(
         (mean_rate * tau[None, :])[None] + (vol[:, None] * jnp.sqrt(tau)[None, :])[None] * shock
     )
-    local_min = jnp.min(level, axis=1)
-    payoff = lax.pmin(local_min, "dim")
+    payoff = lax.pmin(jnp.min(level, axis=1), "dim")
     totals = jnp.sum(payoff, axis=0)
     moments = jnp.sum(payoff[:, None, :] * shock, axis=0)
     start_index = lax.axis_index("path") * owned
@@ -55,6 +67,260 @@
     return (jnp.reshape(root_value, (1,)), root_grad, own_value, own_grad)
 
 
+def row_tiles(rows):
+    return [(r, min(16, rows - r)) for r in range(0, rows, 16)]
+
+
+def as_columns(row, rows):
+    full = -(-rows // LANES) * LANES
+    row = jnp.concatenate([row, jnp.ones((1, full - rows), F32)], axis=1)
+    return jnp.transpose(jnp.broadcast_to(row, (8, full)))[:, 0:1]
+
+
+def swap_halves(block):
+    return pltpu.roll(block, HALF, 1)
+
+
+def low_lanes(shape):
+    return lax.broadcasted_iota(jnp.int32, shape, 1) < HALF
+
+
+def pack_low(top, bottom):
+    return jnp.where(low_lanes(top.shape), top, swap_halves(bottom))
+
+
+def pack_high(top, bottom):
+    return jnp.where(low_lanes(top.shape), swap_halves(top), bottom)
+
+
+def minima_kernel(noise_hbm, outer_ref, start_ref, vol_ref, times_ref, out_ref, noise_v, sems):
+    paths, rows, points = noise_hbm.shape
+    copies = [
+        pltpu.make_async_copy(noise_hbm.at[k], noise_v.at[k], sems.at[k]) for k in range(paths)
+    ]
+    for c in copies:
+        c.start()
+    vol_row = vol_ref[...]
+    base = as_columns(jnp.log(start_ref[...]) + (drift - 0.5 * vol_row * vol_row), rows)
+    vol = as_columns(vol_row, rows)
+    times = times_ref[...]
+    root_times = jnp.sqrt(times)
+    root_tau = jnp.sqrt(1.0 - times)
+    for c in copies:
+        c.wait()
+    low = None
+    for r, n in row_tiles(rows):
+        v = vol[r : r + n]
+        a = base[r : r + n] + (v * root_times) * outer_ref[r : r + n, :].astype(F32)
+        b = v * root_tau
+        here = []
+        for k in range(paths):
+            level = a + b * noise_v[k, r : r + n, :].astype(F32)
+            if n == 16:
+                here.append(jnp.minimum(level[0:8], level[8:16]))
+            else:
+                least = jnp.min(level, axis=0, keepdims=True)
+                here.append(jnp.broadcast_to(least, (8, points)))
+        low = here if low is None else [jnp.minimum(p, q) for p, q in zip(low, here)]
+    for k in range(paths):
+        out_ref[k : k + 1, :] = jnp.min(low[k], axis=0, keepdims=True)
+
+
+def moments_kernel(
+    zs, l0, l1, l2, l3, noise_ref, times_ref, send_far, keep_far, send_near, keep_near, pay, term
+):
+    paths, rows, points = noise_ref.shape
+    me = lax.axis_index("path")
+    z = me // 2
+    first = me % 2 == 0
+    payoff = jnp.exp(jnp.minimum(jnp.minimum(l0[...], l1[...]), jnp.minimum(l2[...], l3[...])))
+    pay[...] = payoff
+    totals = jnp.sum(payoff, axis=0, keepdims=True)
+    half = zs // 2
+    for step in range(zs):
+        s = zs - 1 - step
+        send, keep = (send_far, keep_far) if s >= half else (send_near, keep_near)
+        place = (step if s >= half else step - half) * LANES
+        columns = pl.ds(pl.multiple_of((z ^ s) * LANES, LANES), LANES)
+        weights = [pay[k : k + 1, columns] for k in range(paths)]
+        root_tau = jnp.sqrt(1.0 - times_ref[0:1, columns])
+
+        def tile(r):
+            n = min(16, rows - r)
+            if n <= 0:
+                return jnp.zeros((16, LANES), F32)
+            total = weights[0] * noise_ref[0, r : r + n, columns].astype(F32)
+            for k in range(1, paths):
+                total = total + weights[k] * noise_ref[k, r : r + n, columns].astype(F32)
+            if n < 16:
+                total = jnp.concatenate([total, jnp.zeros((16 - n, LANES), F32)], axis=0)
+            return total
+
+        for r in range(0, LANES, 16):
+            top, bottom = tile(r), tile(LANES + r)
+            low, high = pack_low(top, bottom), pack_high(top, bottom)
+            send[place + r : place + r + 16, :] = jnp.where(first, high, low)
+            keep[place + r : place + r + 16, :] = jnp.where(first, low, high)
+            for at, part in ((r, top), (LANES + r, bottom)):
+                if step == 0:
+                    term[at : at + 16, :] = root_tau * part
+                else:
+                    term[at : at + 16, :] += root_tau * part
+    tail = half * LANES
+    extras = [totals[:, c : c + LANES] for c in range(0, points, LANES)]
+    for r in (0, LANES):
+        extras.append(jnp.sum(jnp.transpose(term[r : r + LANES, :]), axis=0, keepdims=True))
+    extras.append(jnp.zeros((EXTRA - len(extras), LANES), F32))
+    extras = jnp.concatenate(extras, axis=0)
+    send_far[tail : tail + EXTRA, :] = extras
+    keep_far[tail : tail + EXTRA, :] = extras
+
+
+def scale_kernel(inner_total, outer_ref, start_ref, vol_ref, times_ref, out_ref):
+    rows = outer_ref.shape[0]
+    me = lax.axis_index("path")
+    z = me // 2
+    first = me % 2 == 0
+    columns = pl.ds(pl.multiple_of(z * LANES, LANES), LANES)
+
+    def pack(top, bottom):
+        return jnp.where(first, pack_low(top, bottom), pack_high(top, bottom))
+
+    vol = as_columns(vol_ref[...], rows)
+    start = as_columns(start_ref[...], rows)
+    spare = jnp.zeros((2 * LANES - rows, LANES), F32)
+    outer = outer_ref[:, columns].astype(F32)
+    outer = pack(outer[0:LANES], jnp.concatenate([outer[LANES:rows], spare], axis=0))
+    times = times_ref[0:1, columns]
+    times = pack(times, times)
+    side = low_lanes((LANES, LANES))
+    vol = jnp.where(side, vol[0:LANES], vol[LANES:])
+    start = jnp.where(side, start[0:LANES], start[LANES:])
+    state = start * jnp.exp((drift - 0.5 * vol * vol) * times + vol * jnp.sqrt(times) * outer)
+    out_ref[...] = 1.0 / (inner_total * vol * state * jnp.sqrt(1.0 - times))
+
+
+def final_kernel(
+    inner_total, n_parts, own_ref, extra_ref, scale_ref, outer_ref, start_ref, vol_ref, times_ref, *rest
+):
+    parts, (value_ref, grad_ref, point_ref, point_grad_ref) = rest[:n_parts], rest[n_parts:]
+    rows, points = outer_ref.shape
+    me = lax.axis_index("path")
+    first = me % 2 == 0
+    moments = own_ref[...]
+    extra = extra_ref[...]
+    for part in parts:
+        moments = moments + part[0:LANES, :]
+        extra = extra + part[LANES : LANES + EXTRA, :]
+    grad = moments * scale_ref[...]
+    point_grad_ref[0:LANES, :] = grad[:, 0:HALF]
+    point_grad_ref[LANES:rows, :] = swap_halves(grad)[0 : rows - LANES, 0:HALF]
+    blocks = points // LANES
+    totals = jnp.concatenate([extra[c : c + 1, :] for c in range(blocks)], axis=1)
+    inner_term = jnp.concatenate([extra[blocks : blocks + 1, :], extra[blocks + 1 : blocks + 2, :]], axis=1)
+    values = totals / inner_total
+    driver = driver_of(values)
+    value_ref[...] = jnp.sum(totals, axis=1, keepdims=True) / (points * inner_total) + (
+        jnp.sum(driver, axis=1, keepdims=True) / points
+    )
+    own = extra[0:1, :]
+    for c in range(1, blocks):
+        own = jnp.where(me // 2 == c, extra[c : c + 1, :], own)
+    own = jnp.where(first, own, swap_halves(own)) / inner_total
+    point_ref[...] = own[:, 0:HALF]
+    root_times = jnp.sqrt(times_ref[...])
+    weight = totals * root_times / inner_total + driver / root_times
+    outer_term = lax.dot_general(
+        jnp.broadcast_to(weight, (8, points)),
+        outer_ref[...].astype(F32),
+        (((1,), (1,)), ((), ())),
+        precision=lax.Precision.HIGHEST,
+        preferred_element_type=F32,
+    )[0:1, :]
+    grad_ref[...] = (inner_term[:, 0:rows] / inner_total + outer_term) / (
+        points * vol_ref[...] * start_ref[...]
+    )
+
+
+def paired(inner_noise, outer_noise, start, vol, times):
+    paths, rows, points = inner_noise.shape
+    groups, dims = lax.axis_size("path"), lax.axis_size("dim")
+    inner_total = paths * groups
+    zs = groups // 2
+    half = zs // 2
+    start_row, vol_row, times_row = start[None, :], vol[None, :], times[None, :]
+    limit = pltpu.CompilerParams(vmem_limit_bytes=16 * 1024 * 1024)
+
+    lows = pl.pallas_call(
+        minima_kernel,
+        out_shape=jax.ShapeDtypeStruct((paths, points), F32),
+        in_specs=[pl.BlockSpec(memory_space=pl.ANY)] + [pl.BlockSpec()] * 4,
+        scratch_shapes=[
+            pltpu.VMEM((paths, rows, points), inner_noise.dtype),
+            pltpu.SemaphoreType.DMA((paths,)),
+        ],
+        compiler_params=limit,
+        name="minima",
+    )(inner_noise, outer_noise, start_row, vol_row, times_row)
+
+    others = [
+        lax.ppermute(lows, "dim", [(i, i ^ s) for i in range(dims)]) for s in range(1, dims)
+    ]
+    shapes = [half * LANES + EXTRA] * 2 + [half * LANES] * 2
+    send_far, keep_far, send_near, keep_near = pl.pallas_call(
+        functools.partial(moments_kernel, zs),
+        out_shape=[jax.ShapeDtypeStruct((n, LANES), F32) for n in shapes],
+        scratch_shapes=[pltpu.VMEM((paths, points), F32), pltpu.VMEM((2 * LANES, LANES), F32)],
+        compiler_params=limit,
+        name="moments",
+    )(lows, *others, inner_noise, times_row)
+
+    swap = [(i, i ^ 1) for i in range(groups)]
+    far = keep_far + lax.ppermute(send_far, "path", swap)
+    near = keep_near + lax.ppermute(send_near, "path", swap)
+    scale = pl.pallas_call(
+        functools.partial(scale_kernel, inner_total),
+        out_shape=jax.ShapeDtypeStruct((LANES, LANES), F32),
+        compiler_params=limit,
+        name="scale",
+    )(outer_noise, start_row, vol_row, times_row)
+    extra = far[half * LANES :]
+    arrived = []
+    for step in range(zs - 1):
+        s = zs - 1 - step
+        held, at = (far, step) if s >= half else (near, step - half)
+        message = jnp.concatenate([held[at * LANES : (at + 1) * LANES], extra], axis=0)
+        arrived.append(lax.ppermute(message, "path", [(i, i ^ (2 * s)) for i in range(groups)]))
+    own = near[(half - 1) * LANES :]
+
+    value, grad, point, point_grad = pl.pallas_call(
+        functools.partial(final_kernel, inner_total, len(arrived)),
+        out_shape=[
+            jax.ShapeDtypeStruct((1, 1), F32),
+            jax.ShapeDtypeStruct((1, rows), F32),
+            jax.ShapeDtypeStruct((1, points // groups), F32),
+            jax.ShapeDtypeStruct((rows, points // groups), F32),
+        ],
+        compiler_params=limit,
+        name="final",
+    )(own, extra, scale, outer_noise, start_row, vol_row, times_row, *arrived)
+    return value.reshape(1), grad.reshape(rows), point.reshape(points // groups), point_grad
+
+
+def per_device(inner_noise, outer_noise, start, vol, times):
+    rows, points = outer_noise.shape
+    groups, dims = lax.axis_size("path"), lax.axis_size("dim")
+    fits = (
+        2 * points == LANES * groups
+        and LANES < rows <= 2 * LANES
+        and is_power(groups)
+        and groups >= 4
+        and dims == 4
+        and points // LANES + 2 <= EXTRA
+    )
+    return (paired if fits else general)(inner_noise, outer_noise, start, vol, times)
+
+
 def solution(mesh):
     in_specs = (P("path", "dim", None), P("dim", None), P("dim"), P("dim"), P())
     out_specs = (P(), P("dim"), P("path"), P("dim", "path"))

time: 112 us -> 30.7 us (0.27)
  blocking collectives: 34.8 us -> 0 us
  waiting for transfers between devices: 48.4 us -> 13.8 us
  between operations: 16.5 us -> 0.77 us
  other arithmetic: 10.7 us -> 0.05 us
  starting transfers between devices: 0.04 us -> 9.7 us
  Pallas kernels: 0 us -> 3.21 us
  local copies, waits for them, and re-layouts: 1.39 us -> 3.04 us
    psum x1 -> x0, waiting for transfers between devices: 48.3 us -> none  [per_device(): totals, moments = lax.psum((totals, moments), 'path')]
    psum x1 -> x0, blocking collectives: 22 us -> none  [per_device(): totals, moments = lax.psum((totals, moments), 'path')]
    ppermute x0 -> x8, waiting for transfers between devices: none -> 13.8 us  [the longest x3 4.32 us: paired(): lax.ppermute(message, 'path', [(i, i ^ 2 * s) for i in range(groups)])]
    pmin x1 -> x0, blocking collectives: 12.8 us -> none  [per_device(): payoff = lax.pmin(local_min, 'dim')]
    ppermute x0 -> x8, starting transfers between devices: none -> 9.7 us  [the longest x3 4.45 us: paired(): lax.ppermute(message, 'path', [(i, i ^ 2 * s) for i in range(groups)])]
    reduce_sum x4 -> x0, other arithmetic: 4.11 us -> none  [the longest x1 2.16 us: per_device(): moments = jnp.sum(payoff[:, None, :] * shock, axis=0)]
    pallas_call x0 -> x4, Pallas kernels: none -> 3.21 us  [the longest x1 1.14 us: paired(): pl.pallas_call(minima_kernel, out_shape=jax.ShapeDtypeStruct((paths, poin...]
    reduce_min x1 -> x0, other arithmetic: 2.37 us -> none  [per_device(): local_min = jnp.min(level, axis=1)]
  transfers between devices with their start and end apart: 1 -> 8, of which waited for: 1 -> 6; matrix products, arithmetic and copies ran while one was open for 1% -> 0% of each run, Pallas kernels for 0% -> 1%
where the time goes in v1:
time: 30.7 us; the launch traced here: 30.6 us
  waiting for transfers between devices  13.8 us (45%)
  starting transfers between devices  9.7 us (32%)
  Pallas kernels  3.21 us (10%)
  local copies, waits for them, and re-layouts  3.04 us (10%)
  between operations  0.77 us (3%)
    ppermute x3, starting transfers between devices, paired(): lax.ppermute(message, 'path', [(i, i ^ 2 * s) for i in range(groups)])  4.45 us
    ppermute x3, waiting for transfers between devices, paired(): lax.ppermute(message, 'path', [(i, i ^ 2 * s) for i in range(groups)])  4.32 us
    ppermute x1, waiting for transfers between devices, paired(): near = keep_near + lax.ppermute(send_near, 'path', swap)  4.31 us
    ppermute x3, starting transfers between devices, paired(): lax.ppermute(lows, 'dim', [(i, i ^ s) for i in range(dims)])  3.15 us
    ppermute x3, waiting for transfers between devices, paired(): lax.ppermute(lows, 'dim', [(i, i ^ s) for i in range(dims)])  3.09 us
    unnamed x10, local copies, waits for them, and re-layouts  3.01 us
    ppermute x1, waiting for transfers between devices, paired(): far = keep_far + lax.ppermute(send_far, 'path', swap)  2.09 us
    ppermute x1, starting transfers between devices, paired(): near = keep_near + lax.ppermute(send_near, 'path', swap)  1.62 us
  transfers between devices with their start and end apart: 8, of which 6 were waited for; matrix products, arithmetic and copies ran while one was open for 0% of the time, Pallas kernels for 1%

profile of v1, /device:TPU:0, one launch (start us, length us, event | category | flops | bytes accessed | tf_op | source)
XLA Modules:
  0.0 30.6 jit_solution(5079295701726655150)
XLA Ops:
  0.6 0.0 copy-start.1
  0.6 0.0 copy-start.2
  0.7 0.0 copy-start.3
  0.7 0.0 copy-start
  0.7 2.3 %copy.9.noise_hbm.noise_ref = bf16[8,250,512]{2,1,0:T(8,128)(2,1)S(1)} copy(bf16[8,250,512]{2,0,1:T(8,128)(2,1)} %param.5) | data formatting | bytes 4096000 | tf_op args[0]
  3.0 0.0 copy-done.1
  3.0 0.0 copy-done.2
  3.0 0.0 copy-done.3
  3.0 0.0 copy-done
  3.0 1.1 %minima.1.l0 = f32[8,512]{1,0:T(8,128)S(1)} custom-call(bf16[8,250,512]{2,1,0:T(8,128)(2,1)S(1)} %copy.9.noise_hbm.noise_ref, bf16[250,512]{1,0:T(8,128)(2,1)S(1)} %copy-done, f32[1,250]{1,0:T(1,128)S(1)} %bitcast.10, f32[1,250]{1,0:T(1,128)S(1)} %bitcast.13, f32[1,512]{1,0:T(1,128)S(1)} %bitcast.6), custom_call_target="tpu_custom_call" | custom-call | tf_op jit(solution)/shard_map/minima/pallas_call | solution.py:254
  4.1 0.5 %collective-permute-start = (f32[8,512]{1,0:T(8,128)S(1)}, f32[8,512]{1,0:T(8,128)S(1)}, u32[]{:S(2)}, u32[]{:S(2)}) collective-permute-start(f32[8,512]{1,0:T(8,128)S(1)} %minima.1.l0), channel_id=1, source_target_pairs={{0,1},{1,0},{2,3},{3,2},{4,5},{5,4},{6,7},{7,6},{8,9},{9,8},{10,11... | collective-permute-start | bytes 49160 | tf_op jit(solution)/shard_map/ppermute | solution.py:267
  4.7 2.6 %collective-permute-start.1 = (f32[8,512]{1,0:T(8,128)S(1)}, f32[8,512]{1,0:T(8,128)S(1)}, u32[]{:S(2)}, u32[]{:S(2)}) collective-permute-start(f32[8,512]{1,0:T(8,128)S(1)} %minima.1.l0), channel_id=1, source_target_pairs={{0,2},{1,3},{2,0},{3,1},{4,6},{5,7},{6,4},{7,5},{8,10},{9,11},{10,... | collective-permute-start | bytes 49160 | tf_op jit(solution)/shard_map/ppermute | solution.py:267
  7.2 0.1 collective-permute-start.2
  7.3 0.0 collective-permute-done.l1
  7.3 1.6 %collective-permute-done.1.l2 = f32[8,512]{1,0:T(8,128)S(1)} collective-permute-done((f32[8,512]{1,0:T(8,128)S(1)}, f32[8,512]{1,0:T(8,128)S(1)}, u32[]{:S(2)}, u32[]{:S(2)}) %collective-permute-start.1) | collective-permute-done | bytes 16416 | tf_op jit(solution)/shard_map/ppermute | solution.py:267
  8.9 1.4 %collective-permute-done.2.l3 = f32[8,512]{1,0:T(8,128)S(1)} collective-permute-done((f32[8,512]{1,0:T(8,128)S(1)}, f32[8,512]{1,0:T(8,128)S(1)}, u32[]{:S(2)}, u32[]{:S(2)}) %collective-permute-start.2) | collective-permute-done | bytes 16416 | tf_op jit(solution)/shard_map/ppermute | solution.py:267
  10.4 0.7 %moments.1 = (f32[264,128]{1,0:T(8,128)S(1)}, f32[264,128]{1,0:T(8,128)S(1)}, f32[256,128]{1,0:T(8,128)S(1)}, f32[256,128]{1,0:T(8,128)S(1)}) custom-call(f32[8,512]{1,0:T(8,128)S(1)} %minima.1.l0, f32[8,512]{1,0:T(8,128)S(1)} %collective-permute-done.l1, f32[8,512]{1,0:T(8,128)S(1)} %collective-permute-done.1.l2, f32[8,512]{1,0:T(8,128)S(1)} %collective-permute-done.2.l3, ...), custom_call_target="tpu_custom_call" | custom-call | tf_op jit(solution)/shard_map/moments/pallas_call | solution.py:270
  11.1 1.6 %collective-permute-start.3 = (f32[256,128]{1,0:T(8,128)S(1)}, f32[256,128]{1,0:T(8,128)S(1)}, u32[]{:S(2)}, u32[]{:S(2)}) collective-permute-start(f32[256,128]{1,0:T(8,128)S(1)} %get-tuple-element.13), channel_id=1, source_target_pairs={{0,4},{4,0},{8,12},{12,8},{16,20},{20,16},{24,28},{28,24},{1,5},{5... | collective-permute-start | bytes 393224 | tf_op jit(solution)/shard_map/ppermute | solution.py:280
  12.7 0.5 %collective-permute-start.4 = (f32[264,128]{1,0:T(8,128)S(1)}, f32[264,128]{1,0:T(8,128)S(1)}, u32[]{:S(2)}, u32[]{:S(2)}) collective-permute-start(f32[264,128]{1,0:T(8,128)S(1)} %get-tuple-element.15), channel_id=1, source_target_pairs={{0,4},{4,0},{8,12},{12,8},{16,20},{20,16},{24,28},{28,24},{1,5},{5... | collective-permute-start | bytes 405512 | tf_op jit(solution)/shard_map/ppermute | solution.py:279
  13.2 4.3 %collective-permute-done.3 = f32[256,128]{1,0:T(8,128)S(1)} collective-permute-done((f32[256,128]{1,0:T(8,128)S(1)}, f32[256,128]{1,0:T(8,128)S(1)}, u32[]{:S(2)}, u32[]{:S(2)}) %collective-permute-start.3) | collective-permute-done | bytes 131104 | tf_op jit(solution)/shard_map/ppermute | solution.py:280
  17.5 2.1 %collective-permute-done.4 = f32[264,128]{1,0:T(8,128)S(1)} collective-permute-done((f32[264,128]{1,0:T(8,128)S(1)}, f32[264,128]{1,0:T(8,128)S(1)}, u32[]{:S(2)}, u32[]{:S(2)}) %collective-permute-start.4) | collective-permute-done | bytes 135200 | tf_op jit(solution)/shard_map/ppermute | solution.py:279
  19.7 3.7 %collective-permute-start.5 = (f32[136,128]{1,0:T(8,128)S(1)}, f32[136,128]{1,0:T(8,128)S(1)}, u32[]{:S(2)}, u32[]{:S(2)}) collective-permute-start(f32[136,128]{1,0:T(8,128)S(1)} %get-tuple-element.27), channel_id=1, source_target_pairs={{0,24},{4,28},{8,16},{12,20},{16,8},{20,12},{24,0},{28,4},{1,25},{... | collective-permute-start | bytes 208904 | tf_op jit(solution)/shard_map/ppermute | solution.py:293
  23.4 0.0 collective-permute-start.7
  23.4 0.8 %collective-permute-start.6 = (f32[136,128]{1,0:T(8,128)S(1)}, f32[136,128]{1,0:T(8,128)S(1)}, u32[]{:S(2)}, u32[]{:S(2)}) collective-permute-start(f32[136,128]{1,0:T(8,128)S(1)} %concatenate.12), channel_id=1, source_target_pairs={{0,16},{4,20},{8,24},{12,28},{16,0},{20,4},{24,8},{28,12},{1,17},{... | collective-permute-start | bytes 208904 | tf_op jit(solution)/shard_map/ppermute | solution.py:293
  24.2 0.3 scale.1.scale_ref
  24.4 1.6 %collective-permute-done.5.rest_0_ = f32[136,128]{1,0:T(8,128)S(1)} collective-permute-done((f32[136,128]{1,0:T(8,128)S(1)}, f32[136,128]{1,0:T(8,128)S(1)}, u32[]{:S(2)}, u32[]{:S(2)}) %collective-permute-start.5) | collective-permute-done | bytes 69664 | tf_op jit(solution)/shard_map/ppermute | solution.py:293
  26.0 2.8 %collective-permute-done.7.rest_2_ = f32[136,128]{1,0:T(8,128)S(1)} collective-permute-done((f32[136,128]{1,0:T(8,128)S(1)}, f32[136,128]{1,0:T(8,128)S(1)}, u32[]{:S(2)}, u32[]{:S(2)}) %collective-permute-start.7) | collective-permute-done | bytes 69664 | tf_op jit(solution)/shard_map/ppermute | solution.py:293
  28.8 0.0 collective-permute-done.6.rest_1_
  28.8 1.1 %final.1 = (f32[1,1]{1,0:T(1,128)}, f32[1,250]{1,0:T(1,128)}, f32[1,64]{1,0:T(1,128)}, f32[250,64]{1,0:T(8,128)S(1)}) custom-call(f32[128,128]{1,0:T(8,128)S(1)} %get-tuple-element.25.own_ref, f32[8,128]{1,0:T(8,128)S(1)} %slice.19.extra_ref, f32[128,128]{1,0:T(8,128)S(1)} %scale.1.scale_ref, bf16[250,512]{1,0:T(8,128)(2,1)S(1)} %copy-done, ...), custom_call_target="tpu_custom_call" | custom-call | tf_op jit(solution)/shard_map/final/pallas_call | solution.py:296
  29.9 0.7 %copy.11 = f32[250,64]{0,1:T(8,128)} copy(f32[250,64]{1,0:T(8,128)S(1)} %get-tuple-element.23) | data formatting | bytes 128000
  (7 shorter events, 0.1 us)
Async XLA Ops:
  0.6 2.3 %copy-start.1 = (f32[512]{0:T(512)S(1)}, f32[512]{0:T(512)}, u32[]{:S(2)}) copy-start(f32[512]{0:T(512)} %param.9) | copy-start | bytes 6148
  0.6 2.3 %copy-start.2 = (f32[250]{0:T(256)S(1)}, f32[250]{0:T(256)}, u32[]{:S(2)}) copy-start(f32[250]{0:T(256)} %param.7) | copy-start | bytes 3004
  0.7 2.3 %copy-start.3 = (f32[250]{0:T(256)S(1)}, f32[250]{0:T(256)}, u32[]{:S(2)}) copy-start(f32[250]{0:T(256)} %param.8) | copy-start | bytes 3004
  0.7 2.3 %copy-start = (bf16[250,512]{1,0:T(8,128)(2,1)S(1)}, bf16[250,512]{1,0:T(8,128)(2,1)}, u32[]{:S(2)}) copy-start(bf16[250,512]{1,0:T(8,128)(2,1)} %outer_ref.5) | copy-start | bytes 768004
  4.1 3.2 %collective-permute-start = (f32[8,512]{1,0:T(8,128)S(1)}, f32[8,512]{1,0:T(8,128)S(1)}, u32[]{:S(2)}, u32[]{:S(2)}) collective-permute-start(f32[8,512]{1,0:T(8,128)S(1)} %minima.1.l0), channel_id=1, source_target_pairs={{0,1},{1,0},{2,3},{3,2},{4,5},{5,4},{6,7},{7,6},{8,9},{9,8},{10,11... | collective-permute-start | bytes 49160 | tf_op jit(solution)/shard_map/ppermute | solution.py:267
  4.7 4.3 %collective-permute-start.1 = (f32[8,512]{1,0:T(8,128)S(1)}, f32[8,512]{1,0:T(8,128)S(1)}, u32[]{:S(2)}, u32[]{:S(2)}) collective-permute-start(f32[8,512]{1,0:T(8,128)S(1)} %minima.1.l0), channel_id=1, source_target_pairs={{0,2},{1,3},{2,0},{3,1},{4,6},{5,7},{6,4},{7,5},{8,10},{9,11},{10,... | collective-permute-start | bytes 49160 | tf_op jit(solution)/shard_map/ppermute | solution.py:267
  7.2 3.2 %collective-permute-start.2 = (f32[8,512]{1,0:T(8,128)S(1)}, f32[8,512]{1,0:T(8,128)S(1)}, u32[]{:S(2)}, u32[]{:S(2)}) collective-permute-start(f32[8,512]{1,0:T(8,128)S(1)} %minima.1.l0), channel_id=1, source_target_pairs={{0,3},{1,2},{2,1},{3,0},{4,7},{5,6},{6,5},{7,4},{8,11},{9,10},{10,... | collective-permute-start | bytes 49160 | tf_op jit(solution)/shard_map/ppermute | solution.py:267
  11.1 6.4 %collective-permute-start.3 = (f32[256,128]{1,0:T(8,128)S(1)}, f32[256,128]{1,0:T(8,128)S(1)}, u32[]{:S(2)}, u32[]{:S(2)}) collective-permute-start(f32[256,128]{1,0:T(8,128)S(1)} %get-tuple-element.13), channel_id=1, source_target_pairs={{0,4},{4,0},{8,12},{12,8},{16,20},{20,16},{24,28},{28,24},{1,5},{5... | collective-permute-start | bytes 393224 | tf_op jit(solution)/shard_map/ppermute | solution.py:280
  12.7 6.9 %collective-permute-start.4 = (f32[264,128]{1,0:T(8,128)S(1)}, f32[264,128]{1,0:T(8,128)S(1)}, u32[]{:S(2)}, u32[]{:S(2)}) collective-permute-start(f32[264,128]{1,0:T(8,128)S(1)} %get-tuple-element.15), channel_id=1, source_target_pairs={{0,4},{4,0},{8,12},{12,8},{16,20},{20,16},{24,28},{28,24},{1,5},{5... | collective-permute-start | bytes 405512 | tf_op jit(solution)/shard_map/ppermute | solution.py:279
  19.7 6.3 %collective-permute-start.5 = (f32[136,128]{1,0:T(8,128)S(1)}, f32[136,128]{1,0:T(8,128)S(1)}, u32[]{:S(2)}, u32[]{:S(2)}) collective-permute-start(f32[136,128]{1,0:T(8,128)S(1)} %get-tuple-element.27), channel_id=1, source_target_pairs={{0,24},{4,28},{8,16},{12,20},{16,8},{20,12},{24,0},{28,4},{1,25},{... | collective-permute-start | bytes 208904 | tf_op jit(solution)/shard_map/ppermute | solution.py:293
  23.4 5.4 %collective-permute-start.7 = (f32[136,128]{1,0:T(8,128)S(1)}, f32[136,128]{1,0:T(8,128)S(1)}, u32[]{:S(2)}, u32[]{:S(2)}) collective-permute-start(f32[136,128]{1,0:T(8,128)S(1)} %get-tuple-element.26), channel_id=1, source_target_pairs={{0,8},{4,12},{8,0},{12,4},{16,24},{20,28},{24,16},{28,20},{1,9},{5... | collective-permute-start | bytes 208904 | tf_op jit(solution)/shard_map/ppermute | solution.py:293
  23.4 5.4 %collective-permute-start.6 = (f32[136,128]{1,0:T(8,128)S(1)}, f32[136,128]{1,0:T(8,128)S(1)}, u32[]{:S(2)}, u32[]{:S(2)}) collective-permute-start(f32[136,128]{1,0:T(8,128)S(1)} %concatenate.12), channel_id=1, source_target_pairs={{0,16},{4,20},{8,24},{12,28},{16,0},{20,4},{24,8},{28,12},{1,17},{... | collective-permute-start | bytes 208904 | tf_op jit(solution)/shard_map/ppermute | solution.py:293

commit v2 on v1

--- a/solution.py
+++ b/solution.py
@@ -18,6 +18,8 @@
 LANES = 128
 HALF = LANES // 2
 EXTRA = 8
+CHUNKS = 4
+STEP = 8
 F32 = jnp.float32
 
 
@@ -93,37 +95,58 @@
     return jnp.where(low_lanes(top.shape), swap_halves(top), bottom)
 
 
-def minima_kernel(noise_hbm, outer_ref, start_ref, vol_ref, times_ref, out_ref, noise_v, sems):
-    paths, rows, points = noise_hbm.shape
+def minima_kernel(
+    noise_hbm, outer_hbm, start_hbm, vol_hbm, times_hbm, out_ref, noise_v,
+    outer_ref, start_ref, vol_ref, times_ref, level_v, slope_v, sems,
+):
+    rows, paths, points = noise_hbm.shape
+    cuts = [rows * c // CHUNKS // 16 * 16 for c in range(CHUNKS)] + [rows]
+    spans = list(zip(cuts[:-1], cuts[1:]))
     copies = [
-        pltpu.make_async_copy(noise_hbm.at[k], noise_v.at[k], sems.at[k]) for k in range(paths)
+        pltpu.make_async_copy(noise_hbm.at[lo:hi], noise_v.at[lo:hi], sems.at[c])
+        for c, (lo, hi) in enumerate(spans)
     ]
-    for c in copies:
+    small = [
+        pltpu.make_async_copy(src, dst, sems.at[CHUNKS + c])
+        for c, (src, dst) in enumerate(
+            [(vol_hbm, vol_ref), (start_hbm, start_ref), (times_hbm, times_ref), (outer_hbm, outer_ref)]
+        )
+    ]
+    for c in small + copies:
         c.start()
+    for c in small[:3]:
+        c.wait()
     vol_row = vol_ref[...]
     base = as_columns(jnp.log(start_ref[...]) + (drift - 0.5 * vol_row * vol_row), rows)
     vol = as_columns(vol_row, rows)
     times = times_ref[...]
     root_times = jnp.sqrt(times)
     root_tau = jnp.sqrt(1.0 - times)
-    for c in copies:
-        c.wait()
-    low = None
+    small[3].wait()
     for r, n in row_tiles(rows):
         v = vol[r : r + n]
-        a = base[r : r + n] + (v * root_times) * outer_ref[r : r + n, :].astype(F32)
-        b = v * root_tau
-        here = []
-        for k in range(paths):
-            level = a + b * noise_v[k, r : r + n, :].astype(F32)
-            if n == 16:
-                here.append(jnp.minimum(level[0:8], level[8:16]))
-            else:
-                least = jnp.min(level, axis=0, keepdims=True)
-                here.append(jnp.broadcast_to(least, (8, points)))
-        low = here if low is None else [jnp.minimum(p, q) for p, q in zip(low, here)]
-    for k in range(paths):
-        out_ref[k : k + 1, :] = jnp.min(low[k], axis=0, keepdims=True)
+        level_v[r : r + n, :] = base[r : r + n] + (v * root_times) * outer_ref[r : r + n, :].astype(F32)
+        slope_v[r : r + n, :] = v * root_tau
+
+    def level(d):
+        shock = noise_v[d].astype(F32)
+        return level_v[pl.ds(d, 1), :] + slope_v[pl.ds(d, 1), :] * shock
+
+    low = jnp.full((paths, points), jnp.inf, F32)
+    for (lo, hi), c in zip(spans, copies):
+        c.wait()
+        size = hi - lo
+        whole = size // STEP
+
+        def body(t, low, lo=lo):
+            for j in range(STEP):
+                low = jnp.minimum(low, level(lo + t * STEP + j))
+            return low
+
+        low = lax.fori_loop(0, whole, body, low)
+        for d in range(lo + whole * STEP, hi):
+            low = jnp.minimum(low, level(d))
+    out_ref[...] = low
 
 
 def moments_kernel(
@@ -213,8 +236,9 @@
         moments = moments + part[0:LANES, :]
         extra = extra + part[LANES : LANES + EXTRA, :]
     grad = moments * scale_ref[...]
-    point_grad_ref[0:LANES, :] = grad[:, 0:HALF]
-    point_grad_ref[LANES:rows, :] = swap_halves(grad)[0 : rows - LANES, 0:HALF]
+    turned = jnp.transpose(grad)
+    point_grad_ref[:, 0:LANES] = turned[0:HALF]
+    point_grad_ref[:, LANES:rows] = turned[HALF:, 0 : rows - LANES]
     blocks = points // LANES
     totals = jnp.concatenate([extra[c : c + 1, :] for c in range(blocks)], axis=1)
     inner_term = jnp.concatenate([extra[blocks : blocks + 1, :], extra[blocks + 1 : blocks + 2, :]], axis=1)
@@ -251,17 +275,29 @@
     start_row, vol_row, times_row = start[None, :], vol[None, :], times[None, :]
     limit = pltpu.CompilerParams(vmem_limit_bytes=16 * 1024 * 1024)
 
-    lows = pl.pallas_call(
+    lows, held_noise = pl.pallas_call(
         minima_kernel,
-        out_shape=jax.ShapeDtypeStruct((paths, points), F32),
-        in_specs=[pl.BlockSpec(memory_space=pl.ANY)] + [pl.BlockSpec()] * 4,
+        out_shape=(
+            pltpu.VMEM((paths, points), F32),
+            pltpu.VMEM((rows, paths, points), inner_noise.dtype),
+        ),
+        in_specs=[pl.BlockSpec(memory_space=pltpu.HBM)] * 5,
         scratch_shapes=[
-            pltpu.VMEM((paths, rows, points), inner_noise.dtype),
-            pltpu.SemaphoreType.DMA((paths,)),
+            pltpu.VMEM((rows, points), outer_noise.dtype),
+            pltpu.VMEM((1, rows), F32),
+            pltpu.VMEM((1, rows), F32),
+            pltpu.VMEM((1, points), F32),
+            pltpu.VMEM((rows, points), F32),
+            pltpu.VMEM((rows, points), F32),
+            pltpu.SemaphoreType.DMA((CHUNKS + 4,)),
         ],
         compiler_params=limit,
         name="minima",
-    )(inner_noise, outer_noise, start_row, vol_row, times_row)
+    )(*[
+        pltpu.with_memory_space_constraint(x, pltpu.HBM)
+        for x in (jnp.transpose(inner_noise, (1, 0, 2)), outer_noise, start_row, vol_row, times_row)
+    ])
+    held_noise = jnp.transpose(held_noise, (1, 0, 2))
 
     others = [
         lax.ppermute(lows, "dim", [(i, i ^ s) for i in range(dims)]) for s in range(1, dims)
@@ -273,7 +309,7 @@
         scratch_shapes=[pltpu.VMEM((paths, points), F32), pltpu.VMEM((2 * LANES, LANES), F32)],
         compiler_params=limit,
         name="moments",
-    )(lows, *others, inner_noise, times_row)
+    )(lows, *others, held_noise, times_row)
 
     swap = [(i, i ^ 1) for i in range(groups)]
     far = keep_far + lax.ppermute(send_far, "path", swap)
@@ -299,12 +335,12 @@
             jax.ShapeDtypeStruct((1, 1), F32),
             jax.ShapeDtypeStruct((1, rows), F32),
             jax.ShapeDtypeStruct((1, points // groups), F32),
-            jax.ShapeDtypeStruct((rows, points // groups), F32),
+            jax.ShapeDtypeStruct((points // groups, rows), F32),
         ],
         compiler_params=limit,
         name="final",
     )(own, extra, scale, outer_noise, start_row, vol_row, times_row, *arrived)
-    return value.reshape(1), grad.reshape(rows), point.reshape(points // groups), point_grad
+    return value.reshape(1), grad.reshape(rows), point.reshape(points // groups), jnp.transpose(point_grad)
 
 
 def per_device(inner_noise, outer_noise, start, vol, times):

time: 30.7 us -> 28.5 us (0.928)
  local copies, waits for them, and re-layouts: 3.04 us -> 0.71 us
  Pallas kernels: 3.21 us -> 4.05 us
  waiting for transfers between devices: 13.8 us -> 13.1 us
    unnamed x10 -> x8, local copies, waits for them, and re-layouts: 3.01 us -> 0.02 us
    pallas_call x1, Pallas kernels: 1.14 us -> 1.98 us  [paired(): pl.pallas_call(minima_kernel, out_shape=(pltpu.VMEM((paths, points), F32)...]
    ppermute x3, waiting for transfers between devices: 3.09 us -> 2.38 us  [paired(): lax.ppermute(lows, 'dim', [(i, i ^ s) for i in range(dims)])]
    pallas_call x0 -> x1, local copies, waits for them, and re-layouts: none -> 0.66 us  [paired(): pl.pallas_call(minima_kernel, out_shape=(pltpu.VMEM((paths, points), F32)...]
  transfers between devices with their start and end apart: 8 -> 8, of which waited for: 6 -> 6; matrix products, arithmetic and copies ran while one was open for 0% -> 2% of each run, Pallas kernels for 1% -> 1%
where the time goes in v2:
time: 28.5 us; the launch traced here: 28.3 us
  waiting for transfers between devices  13.1 us (46%)
  starting transfers between devices  9.7 us (34%)
  Pallas kernels  4.05 us (14%)
  between operations  0.74 us (3%)
  local copies, waits for them, and re-layouts  0.71 us (2%)
    ppermute x3, starting transfers between devices, paired(): lax.ppermute(message, 'path', [(i, i ^ 2 * s) for i in range(groups)])  4.45 us
    ppermute x1, waiting for transfers between devices, paired(): near = keep_near + lax.ppermute(send_near, 'path', swap)  4.31 us
    ppermute x3, waiting for transfers between devices, paired(): lax.ppermute(message, 'path', [(i, i ^ 2 * s) for i in range(groups)])  4.31 us
    ppermute x3, starting transfers between devices, paired(): lax.ppermute(lows, 'dim', [(i, i ^ s) for i in range(dims)])  3.15 us
    ppermute x3, waiting for transfers between devices, paired(): lax.ppermute(lows, 'dim', [(i, i ^ s) for i in range(dims)])  2.38 us
    ppermute x1, waiting for transfers between devices, paired(): far = keep_far + lax.ppermute(send_far, 'path', swap)  2.09 us
    pallas_call x1, Pallas kernels, paired(): pl.pallas_call(minima_kernel, out_shape=(pltpu.VMEM((paths, points), F32)...  1.98 us
    ppermute x1, starting transfers between devices, paired(): near = keep_near + lax.ppermute(send_near, 'path', swap)  1.62 us
  transfers between devices with their start and end apart: 8, of which 6 were waited for; matrix products, arithmetic and copies ran while one was open for 2% of the time, Pallas kernels for 1%

profile of v2, /device:TPU:0, one launch (start us, length us, event | category | flops | bytes accessed | tf_op | source)
XLA Modules:
  0.0 28.3 jit_solution(16250617641451451585)
XLA Ops:
  0.6 2.0 %minima.1 = (f32[8,512]{1,0:T(8,128)S(1)}, bf16[250,8,512]{2,1,0:T(8,128)(2,1)S(1)}) custom-call(bf16[250,8,512]{2,1,0:T(8,128)(2,1)} %bitcast.22, bf16[250,512]{1,0:T(8,128)(2,1)} %outer_ref.3, f32[1,250]{1,0:T(1,128)} %bitcast.16, f32[1,250]{1,0:T(1,128)} %bitcast.19, f32[1,512]{1,0:T(1,128)} %bitcast.12), custom_call_target="tpu_custom_call" | custom-call | tf_op jit(solution)/shard_map/minima/pallas_call | solution.py:278
  2.6 0.5 %collective-permute-start = (f32[8,512]{1,0:T(8,128)S(1)}, f32[8,512]{1,0:T(8,128)S(1)}, u32[]{:S(2)}, u32[]{:S(2)}) collective-permute-start(f32[8,512]{1,0:T(8,128)S(1)} %get-tuple-element.14.l0), channel_id=1, source_target_pairs={{0,1},{1,0},{2,3},{3,2},{4,5},{5,4},{6,7},{7,6},{8,9},{9,8},{10,11... | collective-permute-start | bytes 49160 | tf_op jit(solution)/shard_map/ppermute | solution.py:303
  3.1 2.6 %collective-permute-start.1 = (f32[8,512]{1,0:T(8,128)S(1)}, f32[8,512]{1,0:T(8,128)S(1)}, u32[]{:S(2)}, u32[]{:S(2)}) collective-permute-start(f32[8,512]{1,0:T(8,128)S(1)} %get-tuple-element.14.l0), channel_id=1, source_target_pairs={{0,2},{1,3},{2,0},{3,1},{4,6},{5,7},{6,4},{7,5},{8,10},{9,11},{10,... | collective-permute-start | bytes 49160 | tf_op jit(solution)/shard_map/ppermute | solution.py:303
  5.7 0.1 collective-permute-start.2
  5.8 0.0 copy-start.1
  5.8 0.7 %copy.11 = bf16[250,8,512]{2,0,1:T(8,128)(2,1)S(1)} copy(bf16[250,8,512]{2,1,0:T(8,128)(2,1)S(1)} %get-tuple-element.15) | data formatting | bytes 4096000 | tf_op jit(solution)/shard_map/minima/pallas_call | solution.py:278
  6.4 0.0 copy-start
  6.4 0.0 copy-start.2
  6.5 0.0 copy-start.3
  6.5 0.0 collective-permute-done.l1
  6.5 0.9 %collective-permute-done.1.l2 = f32[8,512]{1,0:T(8,128)S(1)} collective-permute-done((f32[8,512]{1,0:T(8,128)S(1)}, f32[8,512]{1,0:T(8,128)S(1)}, u32[]{:S(2)}, u32[]{:S(2)}) %collective-permute-start.1) | collective-permute-done | bytes 16416 | tf_op jit(solution)/shard_map/ppermute | solution.py:303
  7.4 1.4 %collective-permute-done.2.l3 = f32[8,512]{1,0:T(8,128)S(1)} collective-permute-done((f32[8,512]{1,0:T(8,128)S(1)}, f32[8,512]{1,0:T(8,128)S(1)}, u32[]{:S(2)}, u32[]{:S(2)}) %collective-permute-start.2) | collective-permute-done | bytes 16416 | tf_op jit(solution)/shard_map/ppermute | solution.py:303
  8.9 0.0 copy-done.1
  8.9 0.7 %moments.1 = (f32[264,128]{1,0:T(8,128)S(1)}, f32[264,128]{1,0:T(8,128)S(1)}, f32[256,128]{1,0:T(8,128)S(1)}, f32[256,128]{1,0:T(8,128)S(1)}) custom-call(f32[8,512]{1,0:T(8,128)S(1)} %get-tuple-element.14.l0, f32[8,512]{1,0:T(8,128)S(1)} %collective-permute-done.l1, f32[8,512]{1,0:T(8,128)S(1)} %collective-permute-done.1.l2, ...), custom_call_target="tpu_custom_call" | custom-call | tf_op jit(solution)/shard_map/moments/pallas_call | solution.py:306
  9.6 1.6 %collective-permute-start.3 = (f32[256,128]{1,0:T(8,128)S(1)}, f32[256,128]{1,0:T(8,128)S(1)}, u32[]{:S(2)}, u32[]{:S(2)}) collective-permute-start(f32[256,128]{1,0:T(8,128)S(1)} %get-tuple-element.17), channel_id=1, source_target_pairs={{0,4},{4,0},{8,12},{12,8},{16,20},{20,16},{24,28},{28,24},{1,5},{5... | collective-permute-start | bytes 393224 | tf_op jit(solution)/shard_map/ppermute | solution.py:316
  11.2 0.5 %collective-permute-start.4 = (f32[264,128]{1,0:T(8,128)S(1)}, f32[264,128]{1,0:T(8,128)S(1)}, u32[]{:S(2)}, u32[]{:S(2)}) collective-permute-start(f32[264,128]{1,0:T(8,128)S(1)} %get-tuple-element.19), channel_id=1, source_target_pairs={{0,4},{4,0},{8,12},{12,8},{16,20},{20,16},{24,28},{28,24},{1,5},{5... | collective-permute-start | bytes 405512 | tf_op jit(solution)/shard_map/ppermute | solution.py:315
  11.7 4.3 %collective-permute-done.3 = f32[256,128]{1,0:T(8,128)S(1)} collective-permute-done((f32[256,128]{1,0:T(8,128)S(1)}, f32[256,128]{1,0:T(8,128)S(1)}, u32[]{:S(2)}, u32[]{:S(2)}) %collective-permute-start.3) | collective-permute-done | bytes 131104 | tf_op jit(solution)/shard_map/ppermute | solution.py:316
  16.0 2.1 %collective-permute-done.4 = f32[264,128]{1,0:T(8,128)S(1)} collective-permute-done((f32[264,128]{1,0:T(8,128)S(1)}, f32[264,128]{1,0:T(8,128)S(1)}, u32[]{:S(2)}, u32[]{:S(2)}) %collective-permute-start.4) | collective-permute-done | bytes 135200 | tf_op jit(solution)/shard_map/ppermute | solution.py:315
  18.2 3.7 %collective-permute-start.5 = (f32[136,128]{1,0:T(8,128)S(1)}, f32[136,128]{1,0:T(8,128)S(1)}, u32[]{:S(2)}, u32[]{:S(2)}) collective-permute-start(f32[136,128]{1,0:T(8,128)S(1)} %get-tuple-element.27), channel_id=1, source_target_pairs={{0,24},{4,28},{8,16},{12,20},{16,8},{20,12},{24,0},{28,4},{1,25},{... | collective-permute-start | bytes 208904 | tf_op jit(solution)/shard_map/ppermute | solution.py:329
  21.8 0.0 collective-permute-start.7
  21.8 0.8 %collective-permute-start.6 = (f32[136,128]{1,0:T(8,128)S(1)}, f32[136,128]{1,0:T(8,128)S(1)}, u32[]{:S(2)}, u32[]{:S(2)}) collective-permute-start(f32[136,128]{1,0:T(8,128)S(1)} %concatenate.12), channel_id=1, source_target_pairs={{0,16},{4,20},{8,24},{12,28},{16,0},{20,4},{24,8},{28,12},{1,17},{... | collective-permute-start | bytes 208904 | tf_op jit(solution)/shard_map/ppermute | solution.py:329
  22.6 0.0 copy-done
  22.6 0.0 copy-done.2
  22.6 0.0 copy-done.3
  22.6 0.3 scale.1.scale_ref
  22.9 1.5 %collective-permute-done.5.rest_0_ = f32[136,128]{1,0:T(8,128)S(1)} collective-permute-done((f32[136,128]{1,0:T(8,128)S(1)}, f32[136,128]{1,0:T(8,128)S(1)}, u32[]{:S(2)}, u32[]{:S(2)}) %collective-permute-start.5) | collective-permute-done | bytes 69664 | tf_op jit(solution)/shard_map/ppermute | solution.py:329
  24.5 2.8 %collective-permute-done.7.rest_2_ = f32[136,128]{1,0:T(8,128)S(1)} collective-permute-done((f32[136,128]{1,0:T(8,128)S(1)}, f32[136,128]{1,0:T(8,128)S(1)}, u32[]{:S(2)}, u32[]{:S(2)}) %collective-permute-start.7) | collective-permute-done | bytes 69664 | tf_op jit(solution)/shard_map/ppermute | solution.py:329
  27.2 0.0 collective-permute-done.6.rest_1_
  27.2 1.1 %final.1 = (f32[1,1]{1,0:T(1,128)}, f32[1,250]{1,0:T(1,128)}, f32[1,64]{1,0:T(1,128)}, f32[64,250]{1,0:T(8,128)}) custom-call(f32[128,128]{1,0:T(8,128)S(1)} %get-tuple-element.25.own_ref, f32[8,128]{1,0:T(8,128)S(1)} %slice.19.extra_ref, f32[128,128]{1,0:T(8,128)S(1)} %scale.1.scale_ref, bf16[250,512]{1,0:T(8,128)(2,1)S(1)} %copy-done, ...), custom_call_target="tpu_custom_call" | custom-call | tf_op jit(solution)/shard_map/final/pallas_call | solution.py:332
  (7 shorter events, 0.1 us)
Async XLA Ops:
  2.6 3.9 %collective-permute-start = (f32[8,512]{1,0:T(8,128)S(1)}, f32[8,512]{1,0:T(8,128)S(1)}, u32[]{:S(2)}, u32[]{:S(2)}) collective-permute-start(f32[8,512]{1,0:T(8,128)S(1)} %get-tuple-element.14.l0), channel_id=1, source_target_pairs={{0,1},{1,0},{2,3},{3,2},{4,5},{5,4},{6,7},{7,6},{8,9},{9,8},{10,11... | collective-permute-start | bytes 49160 | tf_op jit(solution)/shard_map/ppermute | solution.py:303
  3.1 4.3 %collective-permute-start.1 = (f32[8,512]{1,0:T(8,128)S(1)}, f32[8,512]{1,0:T(8,128)S(1)}, u32[]{:S(2)}, u32[]{:S(2)}) collective-permute-start(f32[8,512]{1,0:T(8,128)S(1)} %get-tuple-element.14.l0), channel_id=1, source_target_pairs={{0,2},{1,3},{2,0},{3,1},{4,6},{5,7},{6,4},{7,5},{8,10},{9,11},{10,... | collective-permute-start | bytes 49160 | tf_op jit(solution)/shard_map/ppermute | solution.py:303
  5.7 3.2 %collective-permute-start.2 = (f32[8,512]{1,0:T(8,128)S(1)}, f32[8,512]{1,0:T(8,128)S(1)}, u32[]{:S(2)}, u32[]{:S(2)}) collective-permute-start(f32[8,512]{1,0:T(8,128)S(1)} %get-tuple-element.14.l0), channel_id=1, source_target_pairs={{0,3},{1,2},{2,1},{3,0},{4,7},{5,6},{6,5},{7,4},{8,11},{9,10},{10,... | collective-permute-start | bytes 49160 | tf_op jit(solution)/shard_map/ppermute | solution.py:303
  5.8 3.1 %copy-start.1 = (f32[512]{0:T(512)S(1)}, f32[512]{0:T(512)}, u32[]{:S(2)}) copy-start(f32[512]{0:T(512)} %param.9) | copy-start | bytes 6148
  6.4 16.2 %copy-start = (bf16[250,512]{1,0:T(8,128)(2,1)S(1)}, bf16[250,512]{1,0:T(8,128)(2,1)}, u32[]{:S(2)}) copy-start(bf16[250,512]{1,0:T(8,128)(2,1)} %outer_ref.3) | copy-start | bytes 768004
  6.4 16.2 %copy-start.2 = (f32[250]{0:T(256)S(1)}, f32[250]{0:T(256)}, u32[]{:S(2)}) copy-start(f32[250]{0:T(256)} %param.7) | copy-start | bytes 3004
  6.5 16.2 %copy-start.3 = (f32[250]{0:T(256)S(1)}, f32[250]{0:T(256)}, u32[]{:S(2)}) copy-start(f32[250]{0:T(256)} %param.8) | copy-start | bytes 3004
  9.6 6.4 %collective-permute-start.3 = (f32[256,128]{1,0:T(8,128)S(1)}, f32[256,128]{1,0:T(8,128)S(1)}, u32[]{:S(2)}, u32[]{:S(2)}) collective-permute-start(f32[256,128]{1,0:T(8,128)S(1)} %get-tuple-element.17), channel_id=1, source_target_pairs={{0,4},{4,0},{8,12},{12,8},{16,20},{20,16},{24,28},{28,24},{1,5},{5... | collective-permute-start | bytes 393224 | tf_op jit(solution)/shard_map/ppermute | solution.py:316
  11.2 6.9 %collective-permute-start.4 = (f32[264,128]{1,0:T(8,128)S(1)}, f32[264,128]{1,0:T(8,128)S(1)}, u32[]{:S(2)}, u32[]{:S(2)}) collective-permute-start(f32[264,128]{1,0:T(8,128)S(1)} %get-tuple-element.19), channel_id=1, source_target_pairs={{0,4},{4,0},{8,12},{12,8},{16,20},{20,16},{24,28},{28,24},{1,5},{5... | collective-permute-start | bytes 405512 | tf_op jit(solution)/shard_map/ppermute | solution.py:315
  18.2 6.3 %collective-permute-start.5 = (f32[136,128]{1,0:T(8,128)S(1)}, f32[136,128]{1,0:T(8,128)S(1)}, u32[]{:S(2)}, u32[]{:S(2)}) collective-permute-start(f32[136,128]{1,0:T(8,128)S(1)} %get-tuple-element.27), channel_id=1, source_target_pairs={{0,24},{4,28},{8,16},{12,20},{16,8},{20,12},{24,0},{28,4},{1,25},{... | collective-permute-start | bytes 208904 | tf_op jit(solution)/shard_map/ppermute | solution.py:329
  21.8 5.4 %collective-permute-start.7 = (f32[136,128]{1,0:T(8,128)S(1)}, f32[136,128]{1,0:T(8,128)S(1)}, u32[]{:S(2)}, u32[]{:S(2)}) collective-permute-start(f32[136,128]{1,0:T(8,128)S(1)} %get-tuple-element.26), channel_id=1, source_target_pairs={{0,8},{4,12},{8,0},{12,4},{16,24},{20,28},{24,16},{28,20},{1,9},{5... | collective-permute-start | bytes 208904 | tf_op jit(solution)/shard_map/ppermute | solution.py:329
  21.8 5.4 %collective-permute-start.6 = (f32[136,128]{1,0:T(8,128)S(1)}, f32[136,128]{1,0:T(8,128)S(1)}, u32[]{:S(2)}, u32[]{:S(2)}) collective-permute-start(f32[136,128]{1,0:T(8,128)S(1)} %concatenate.12), channel_id=1, source_target_pairs={{0,16},{4,20},{8,24},{12,28},{16,0},{20,4},{24,8},{28,12},{1,17},{... | collective-permute-start | bytes 208904 | tf_op jit(solution)/shard_map/ppermute | solution.py:329

commit v3 on v2

--- a/solution.py
+++ b/solution.py
@@ -149,9 +149,11 @@
     out_ref[...] = low
 
 
-def moments_kernel(
-    zs, l0, l1, l2, l3, noise_ref, times_ref, send_far, keep_far, send_near, keep_near, pay, term
-):
+def moments_kernel(zs, l0, l1, l2, l3, noise_ref, times_ref, *rest):
+    half = zs // 2
+    send_far, keep_far, keep_near = rest[:3]
+    send_near = rest[3 : 2 + half]
+    pay, term = rest[2 + half :]
     paths, rows, points = noise_ref.shape
     me = lax.axis_index("path")
     z = me // 2
@@ -159,14 +161,16 @@
     payoff = jnp.exp(jnp.minimum(jnp.minimum(l0[...], l1[...]), jnp.minimum(l2[...], l3[...])))
     pay[...] = payoff
     totals = jnp.sum(payoff, axis=0, keepdims=True)
-    half = zs // 2
     for step in range(zs):
         s = zs - 1 - step
-        send, keep = (send_far, keep_far) if s >= half else (send_near, keep_near)
-        place = (step if s >= half else step - half) * LANES
         columns = pl.ds(pl.multiple_of((z ^ s) * LANES, LANES), LANES)
         weights = [pay[k : k + 1, columns] for k in range(paths)]
         root_tau = jnp.sqrt(1.0 - times_ref[0:1, columns])
+        if s >= half:
+            (same, at), (other, past) = (keep_far, step * LANES), (send_far, step * LANES)
+        else:
+            near = keep_near if s == 0 else send_near[s - 1]
+            (same, at), (other, past) = (near, 0), (near, LANES)
 
         def tile(r):
             n = min(16, rows - r)
@@ -182,21 +186,21 @@
         for r in range(0, LANES, 16):
             top, bottom = tile(r), tile(LANES + r)
             low, high = pack_low(top, bottom), pack_high(top, bottom)
-            send[place + r : place + r + 16, :] = jnp.where(first, high, low)
-            keep[place + r : place + r + 16, :] = jnp.where(first, low, high)
-            for at, part in ((r, top), (LANES + r, bottom)):
+            same[at + r : at + r + 16, :] = jnp.where(first, low, high)
+            other[past + r : past + r + 16, :] = jnp.where(first, high, low)
+            for to, part in ((r, top), (LANES + r, bottom)):
                 if step == 0:
-                    term[at : at + 16, :] = root_tau * part
+                    term[to : to + 16, :] = root_tau * part
                 else:
-                    term[at : at + 16, :] += root_tau * part
-    tail = half * LANES
+                    term[to : to + 16, :] += root_tau * part
     extras = [totals[:, c : c + LANES] for c in range(0, points, LANES)]
     for r in (0, LANES):
         extras.append(jnp.sum(jnp.transpose(term[r : r + LANES, :]), axis=0, keepdims=True))
     extras.append(jnp.zeros((EXTRA - len(extras), LANES), F32))
     extras = jnp.concatenate(extras, axis=0)
-    send_far[tail : tail + EXTRA, :] = extras
-    keep_far[tail : tail + EXTRA, :] = extras
+    for ref in (send_far, keep_far, *send_near):
+        ref[ref.shape[0] - EXTRA :, :] = extras
+    keep_near[2 * LANES :, :] = jnp.zeros((EXTRA, LANES), F32)
 
 
 def scale_kernel(inner_total, outer_ref, start_ref, vol_ref, times_ref, out_ref):
@@ -224,14 +228,14 @@
 
 
 def final_kernel(
-    inner_total, n_parts, own_ref, extra_ref, scale_ref, outer_ref, start_ref, vol_ref, times_ref, *rest
+    inner_total, n_parts, near_ref, far_extra_ref, scale_ref, outer_ref, start_ref, vol_ref, times_ref, *rest
 ):
     parts, (value_ref, grad_ref, point_ref, point_grad_ref) = rest[:n_parts], rest[n_parts:]
     rows, points = outer_ref.shape
     me = lax.axis_index("path")
     first = me % 2 == 0
-    moments = own_ref[...]
-    extra = extra_ref[...]
+    moments = near_ref[0:LANES, :]
+    extra = far_extra_ref[...] + near_ref[2 * LANES : 2 * LANES + EXTRA, :]
     for part in parts:
         moments = moments + part[0:LANES, :]
         extra = extra + part[LANES : LANES + EXTRA, :]
@@ -302,32 +306,37 @@
     others = [
         lax.ppermute(lows, "dim", [(i, i ^ s) for i in range(dims)]) for s in range(1, dims)
     ]
-    shapes = [half * LANES + EXTRA] * 2 + [half * LANES] * 2
-    send_far, keep_far, send_near, keep_near = pl.pallas_call(
+    send_far, keep_far, keep_near, *send_near = pl.pallas_call(
         functools.partial(moments_kernel, zs),
-        out_shape=[jax.ShapeDtypeStruct((n, LANES), F32) for n in shapes],
+        out_shape=[jax.ShapeDtypeStruct((half * LANES + EXTRA, LANES), F32)] * 2
+        + [jax.ShapeDtypeStruct((2 * LANES + EXTRA, LANES), F32)] * half,
         scratch_shapes=[pltpu.VMEM((paths, points), F32), pltpu.VMEM((2 * LANES, LANES), F32)],
         compiler_params=limit,
         name="moments",
     )(lows, *others, held_noise, times_row)
 
-    swap = [(i, i ^ 1) for i in range(groups)]
-    far = keep_far + lax.ppermute(send_far, "path", swap)
-    near = keep_near + lax.ppermute(send_near, "path", swap)
+    def along_z(message, s):
+        return lax.ppermute(message, "path", [(i, i ^ (2 * s)) for i in range(groups)])
+
+    def along_y(message):
+        return lax.ppermute(message, "path", [(i, i ^ 1) for i in range(groups)])
+
+    far = keep_far + along_y(send_far)
+    near = keep_near
+    for s in range(1, half):
+        near = near + along_z(send_near[s - 1], s)
     scale = pl.pallas_call(
         functools.partial(scale_kernel, inner_total),
         out_shape=jax.ShapeDtypeStruct((LANES, LANES), F32),
         compiler_params=limit,
         name="scale",
     )(outer_noise, start_row, vol_row, times_row)
-    extra = far[half * LANES :]
+    far_extra = far[half * LANES :]
     arrived = []
-    for step in range(zs - 1):
-        s = zs - 1 - step
-        held, at = (far, step) if s >= half else (near, step - half)
-        message = jnp.concatenate([held[at * LANES : (at + 1) * LANES], extra], axis=0)
-        arrived.append(lax.ppermute(message, "path", [(i, i ^ (2 * s)) for i in range(groups)]))
-    own = near[(half - 1) * LANES :]
+    for step in range(half):
+        block = far[step * LANES : (step + 1) * LANES]
+        arrived.append(along_z(jnp.concatenate([block, far_extra], axis=0), zs - 1 - step))
+    arrived.append(along_y(near[LANES:]))
 
     value, grad, point, point_grad = pl.pallas_call(
         functools.partial(final_kernel, inner_total, len(arrived)),
@@ -339,7 +348,7 @@
         ],
         compiler_params=limit,
         name="final",
-    )(own, extra, scale, outer_noise, start_row, vol_row, times_row, *arrived)
+    )(near, far_extra, scale, outer_noise, start_row, vol_row, times_row, *arrived)
     return value.reshape(1), grad.reshape(rows), point.reshape(points // groups), jnp.transpose(point_grad)
 
 

time: 28.5 us -> 25.8 us (0.905)
  waiting for transfers between devices: 13.1 us -> 8.5 us
  starting transfers between devices: 9.7 us -> 11.6 us
    ppermute x5, waiting for transfers between devices: 10.7 us -> 6.12 us  [the longest x3 3.55 us: along_z(): lax.ppermute(message, 'path', [(i, i ^ 2 * s) for i in range(groups)])]
    ppermute x5, starting transfers between devices: 6.54 us -> 8.4 us  [the longest x3 5.23 us: along_z(): lax.ppermute(message, 'path', [(i, i ^ 2 * s) for i in range(groups)])]
  transfers between devices with their start and end apart: 8 -> 8, of which waited for: 6 -> 5; matrix products, arithmetic and copies ran while one was open for 2% -> 3% of each run, Pallas kernels for 1% -> 1%
where the time goes in v3:
time: 25.8 us; the launch traced here: 25.6 us
  starting transfers between devices  11.6 us (45%)
  waiting for transfers between devices  8.5 us (33%)
  Pallas kernels  4.05 us (16%)
  between operations  0.74 us (3%)
  local copies, waits for them, and re-layouts  0.71 us (3%)
    ppermute x3, starting transfers between devices, along_z(): lax.ppermute(message, 'path', [(i, i ^ 2 * s) for i in range(groups)])  5.23 us
    ppermute x3, waiting for transfers between devices, along_z(): lax.ppermute(message, 'path', [(i, i ^ 2 * s) for i in range(groups)])  3.55 us
    ppermute x2, starting transfers between devices, along_y(): return lax.ppermute(message, 'path', [(i, i ^ 1) for i in range(groups)])  3.17 us
    ppermute x3, starting transfers between devices, paired(): lax.ppermute(lows, 'dim', [(i, i ^ s) for i in range(dims)])  3.15 us
    ppermute x2, waiting for transfers between devices, along_y(): return lax.ppermute(message, 'path', [(i, i ^ 1) for i in range(groups)])  2.57 us
    ppermute x3, waiting for transfers between devices, paired(): lax.ppermute(lows, 'dim', [(i, i ^ s) for i in range(dims)])  2.38 us
    pallas_call x1, Pallas kernels, paired(): pl.pallas_call(minima_kernel, out_shape=(pltpu.VMEM((paths, points), F32)...  1.98 us
    pallas_call x1, Pallas kernels, paired(): pl.pallas_call(functools.partial(final_kernel, inner_total, len(arrived))...  1.1 us
  transfers between devices with their start and end apart: 8, of which 5 were waited for; matrix products, arithmetic and copies ran while one was open for 3% of the time, Pallas kernels for 1%

profile of v3, /device:TPU:0, one launch (start us, length us, event | category | flops | bytes accessed | tf_op | source)
XLA Modules:
  0.0 25.6 jit_solution(14714263158224319777)
XLA Ops:
  0.6 2.0 %minima.1 = (f32[8,512]{1,0:T(8,128)S(1)}, bf16[250,8,512]{2,1,0:T(8,128)(2,1)S(1)}) custom-call(bf16[250,8,512]{2,1,0:T(8,128)(2,1)} %bitcast.22, bf16[250,512]{1,0:T(8,128)(2,1)} %outer_ref.3, f32[1,250]{1,0:T(1,128)} %bitcast.16, f32[1,250]{1,0:T(1,128)} %bitcast.19, f32[1,512]{1,0:T(1,128)} %bitcast.12), custom_call_target="tpu_custom_call" | custom-call | tf_op jit(solution)/shard_map/minima/pallas_call | solution.py:282
  2.6 0.5 %collective-permute-start = (f32[8,512]{1,0:T(8,128)S(1)}, f32[8,512]{1,0:T(8,128)S(1)}, u32[]{:S(2)}, u32[]{:S(2)}) collective-permute-start(f32[8,512]{1,0:T(8,128)S(1)} %get-tuple-element.14.l0), channel_id=1, source_target_pairs={{0,1},{1,0},{2,3},{3,2},{4,5},{5,4},{6,7},{7,6},{8,9},{9,8},{10,11... | collective-permute-start | bytes 49160 | tf_op jit(solution)/shard_map/ppermute | solution.py:307
  3.1 2.6 %collective-permute-start.1 = (f32[8,512]{1,0:T(8,128)S(1)}, f32[8,512]{1,0:T(8,128)S(1)}, u32[]{:S(2)}, u32[]{:S(2)}) collective-permute-start(f32[8,512]{1,0:T(8,128)S(1)} %get-tuple-element.14.l0), channel_id=1, source_target_pairs={{0,2},{1,3},{2,0},{3,1},{4,6},{5,7},{6,4},{7,5},{8,10},{9,11},{10,... | collective-permute-start | bytes 49160 | tf_op jit(solution)/shard_map/ppermute | solution.py:307
  5.7 0.1 collective-permute-start.2
  5.8 0.0 copy-start.1
  5.8 0.7 %copy.11 = bf16[250,8,512]{2,0,1:T(8,128)(2,1)S(1)} copy(bf16[250,8,512]{2,1,0:T(8,128)(2,1)S(1)} %get-tuple-element.15) | data formatting | bytes 4096000 | tf_op jit(solution)/shard_map/minima/pallas_call | solution.py:282
  6.4 0.0 copy-start
  6.4 0.0 copy-start.2
  6.5 0.0 copy-start.3
  6.5 0.0 collective-permute-done.l1
  6.5 0.9 %collective-permute-done.1.l2 = f32[8,512]{1,0:T(8,128)S(1)} collective-permute-done((f32[8,512]{1,0:T(8,128)S(1)}, f32[8,512]{1,0:T(8,128)S(1)}, u32[]{:S(2)}, u32[]{:S(2)}) %collective-permute-start.1) | collective-permute-done | bytes 16416 | tf_op jit(solution)/shard_map/ppermute | solution.py:307
  7.4 1.4 %collective-permute-done.2.l3 = f32[8,512]{1,0:T(8,128)S(1)} collective-permute-done((f32[8,512]{1,0:T(8,128)S(1)}, f32[8,512]{1,0:T(8,128)S(1)}, u32[]{:S(2)}, u32[]{:S(2)}) %collective-permute-start.2) | collective-permute-done | bytes 16416 | tf_op jit(solution)/shard_map/ppermute | solution.py:307
  8.9 0.0 copy-done.1
  8.9 0.7 %moments.1 = (f32[264,128]{1,0:T(8,128)S(1)}, f32[264,128]{1,0:T(8,128)S(1)}, f32[264,128]{1,0:T(8,128)S(1)}, f32[264,128]{1,0:T(8,128)S(1)}) custom-call(f32[8,512]{1,0:T(8,128)S(1)} %get-tuple-element.14.l0, f32[8,512]{1,0:T(8,128)S(1)} %collective-permute-done.l1, f32[8,512]{1,0:T(8,128)S(1)} %collective-permute-done.1.l2, ...), custom_call_target="tpu_custom_call" | custom-call | tf_op jit(solution)/shard_map/moments/pallas_call | solution.py:309
  9.6 1.6 %collective-permute-start.4 = (f32[264,128]{1,0:T(8,128)S(1)}, f32[264,128]{1,0:T(8,128)S(1)}, u32[]{:S(2)}, u32[]{:S(2)}) collective-permute-start(f32[264,128]{1,0:T(8,128)S(1)} %get-tuple-element.19), channel_id=1, source_target_pairs={{0,4},{4,0},{8,12},{12,8},{16,20},{20,16},{24,28},{28,24},{1,5},{5... | collective-permute-start | bytes 405512 | tf_op jit(solution)/shard_map/ppermute | solution.py:322
  11.2 1.6 %collective-permute-start.3 = (f32[264,128]{1,0:T(8,128)S(1)}, f32[264,128]{1,0:T(8,128)S(1)}, u32[]{:S(2)}, u32[]{:S(2)}) collective-permute-start(f32[264,128]{1,0:T(8,128)S(1)} %get-tuple-element.17), channel_id=1, source_target_pairs={{0,8},{4,12},{8,0},{12,4},{16,24},{20,28},{24,16},{28,20},{1,9},{5... | collective-permute-start | bytes 405512 | tf_op jit(solution)/shard_map/ppermute | solution.py:319
  12.7 2.6 %collective-permute-done.4 = f32[264,128]{1,0:T(8,128)S(1)} collective-permute-done((f32[264,128]{1,0:T(8,128)S(1)}, f32[264,128]{1,0:T(8,128)S(1)}, u32[]{:S(2)}, u32[]{:S(2)}) %collective-permute-start.4) | collective-permute-done | bytes 135200 | tf_op jit(solution)/shard_map/ppermute | solution.py:322
  15.4 3.7 %collective-permute-start.5 = (f32[136,128]{1,0:T(8,128)S(1)}, f32[136,128]{1,0:T(8,128)S(1)}, u32[]{:S(2)}, u32[]{:S(2)}) collective-permute-start(f32[136,128]{1,0:T(8,128)S(1)} %pad_maximum_fusion), channel_id=1, source_target_pairs={{0,24},{4,28},{8,16},{12,20},{16,8},{20,12},{24,0},{28,4},{1,25},{... | collective-permute-start | bytes 208904 | tf_op jit(solution)/shard_map/ppermute | solution.py:319
  19.0 0.0 collective-permute-start.6
  19.0 0.0 collective-permute-done.3
  19.1 1.6 %collective-permute-start.7 = (f32[136,128]{1,0:T(8,128)S(1)}, f32[136,128]{1,0:T(8,128)S(1)}, u32[]{:S(2)}, u32[]{:S(2)}) collective-permute-start(f32[136,128]{1,0:T(8,128)S(1)} %slice.16), channel_id=1, source_target_pairs={{0,4},{4,0},{8,12},{12,8},{16,20},{20,16},{24,28},{28,24},{1,5},{5... | collective-permute-start | bytes 208904 | tf_op jit(solution)/shard_map/ppermute | solution.py:322
  20.7 0.0 copy-done
  20.7 0.0 copy-done.2
  20.7 0.0 copy-done.3
  20.7 0.3 %scale.1.scale_ref = f32[128,128]{1,0:T(8,128)S(1)} custom-call(bf16[250,512]{1,0:T(8,128)(2,1)S(1)} %copy-done, f32[1,250]{1,0:T(1,128)S(1)} %bitcast.17, f32[1,250]{1,0:T(1,128)S(1)} %bitcast.20, f32[1,512]{1,0:T(1,128)S(1)} %bitcast.14), custom_call_target="tpu_custom_call" | custom-call | tf_op jit(solution)/shard_map/scale/pallas_call | solution.py:328
  20.9 1.2 %collective-permute-done.5.rest_0_ = f32[136,128]{1,0:T(8,128)S(1)} collective-permute-done((f32[136,128]{1,0:T(8,128)S(1)}, f32[136,128]{1,0:T(8,128)S(1)}, u32[]{:S(2)}, u32[]{:S(2)}) %collective-permute-start.5) | collective-permute-done | bytes 69664 | tf_op jit(solution)/shard_map/ppermute | solution.py:319
  22.2 2.3 %collective-permute-done.6.rest_1_ = f32[136,128]{1,0:T(8,128)S(1)} collective-permute-done((f32[136,128]{1,0:T(8,128)S(1)}, f32[136,128]{1,0:T(8,128)S(1)}, u32[]{:S(2)}, u32[]{:S(2)}) %collective-permute-start.6) | collective-permute-done | bytes 69664 | tf_op jit(solution)/shard_map/ppermute | solution.py:319
  24.5 0.0 collective-permute-done.7.rest_2_
  24.5 1.1 %final.1 = (f32[1,1]{1,0:T(1,128)}, f32[1,250]{1,0:T(1,128)}, f32[1,64]{1,0:T(1,128)}, f32[64,250]{1,0:T(8,128)}) custom-call(f32[264,128]{1,0:T(8,128)S(1)} %add.6.near_ref, f32[8,128]{1,0:T(8,128)S(1)} %slice.14.far_extra_ref, f32[128,128]{1,0:T(8,128)S(1)} %scale.1.scale_ref, bf16[250,512]{1,0:T(8,128)(2,1)S(1)} %copy-done, f32[1,250]{1,0:T(1,128)S(1)} %bitcast.18, ...), custom_call_target="tpu_custom_call" | custom-call | tf_op jit(solution)/shard_map/final/pallas_call | solution.py:341
  (7 shorter events, 0.1 us)
Async XLA Ops:
  2.6 3.9 %collective-permute-start = (f32[8,512]{1,0:T(8,128)S(1)}, f32[8,512]{1,0:T(8,128)S(1)}, u32[]{:S(2)}, u32[]{:S(2)}) collective-permute-start(f32[8,512]{1,0:T(8,128)S(1)} %get-tuple-element.14.l0), channel_id=1, source_target_pairs={{0,1},{1,0},{2,3},{3,2},{4,5},{5,4},{6,7},{7,6},{8,9},{9,8},{10,11... | collective-permute-start | bytes 49160 | tf_op jit(solution)/shard_map/ppermute | solution.py:307
  3.1 4.3 %collective-permute-start.1 = (f32[8,512]{1,0:T(8,128)S(1)}, f32[8,512]{1,0:T(8,128)S(1)}, u32[]{:S(2)}, u32[]{:S(2)}) collective-permute-start(f32[8,512]{1,0:T(8,128)S(1)} %get-tuple-element.14.l0), channel_id=1, source_target_pairs={{0,2},{1,3},{2,0},{3,1},{4,6},{5,7},{6,4},{7,5},{8,10},{9,11},{10,... | collective-permute-start | bytes 49160 | tf_op jit(solution)/shard_map/ppermute | solution.py:307
  5.7 3.2 %collective-permute-start.2 = (f32[8,512]{1,0:T(8,128)S(1)}, f32[8,512]{1,0:T(8,128)S(1)}, u32[]{:S(2)}, u32[]{:S(2)}) collective-permute-start(f32[8,512]{1,0:T(8,128)S(1)} %get-tuple-element.14.l0), channel_id=1, source_target_pairs={{0,3},{1,2},{2,1},{3,0},{4,7},{5,6},{6,5},{7,4},{8,11},{9,10},{10,... | collective-permute-start | bytes 49160 | tf_op jit(solution)/shard_map/ppermute | solution.py:307
  5.8 3.1 %copy-start.1 = (f32[512]{0:T(512)S(1)}, f32[512]{0:T(512)}, u32[]{:S(2)}) copy-start(f32[512]{0:T(512)} %param.9) | copy-start | bytes 6148
  6.4 14.2 %copy-start = (bf16[250,512]{1,0:T(8,128)(2,1)S(1)}, bf16[250,512]{1,0:T(8,128)(2,1)}, u32[]{:S(2)}) copy-start(bf16[250,512]{1,0:T(8,128)(2,1)} %outer_ref.3) | copy-start | bytes 768004
  6.4 14.2 %copy-start.2 = (f32[250]{0:T(256)S(1)}, f32[250]{0:T(256)}, u32[]{:S(2)}) copy-start(f32[250]{0:T(256)} %param.7) | copy-start | bytes 3004
  6.5 14.2 %copy-start.3 = (f32[250]{0:T(256)S(1)}, f32[250]{0:T(256)}, u32[]{:S(2)}) copy-start(f32[250]{0:T(256)} %param.8) | copy-start | bytes 3004
  9.6 5.7 %collective-permute-start.4 = (f32[264,128]{1,0:T(8,128)S(1)}, f32[264,128]{1,0:T(8,128)S(1)}, u32[]{:S(2)}, u32[]{:S(2)}) collective-permute-start(f32[264,128]{1,0:T(8,128)S(1)} %get-tuple-element.19), channel_id=1, source_target_pairs={{0,4},{4,0},{8,12},{12,8},{16,20},{20,16},{24,28},{28,24},{1,5},{5... | collective-permute-start | bytes 405512 | tf_op jit(solution)/shard_map/ppermute | solution.py:322
  11.2 7.9 %collective-permute-start.3 = (f32[264,128]{1,0:T(8,128)S(1)}, f32[264,128]{1,0:T(8,128)S(1)}, u32[]{:S(2)}, u32[]{:S(2)}) collective-permute-start(f32[264,128]{1,0:T(8,128)S(1)} %get-tuple-element.17), channel_id=1, source_target_pairs={{0,8},{4,12},{8,0},{12,4},{16,24},{20,28},{24,16},{28,20},{1,9},{5... | collective-permute-start | bytes 405512 | tf_op jit(solution)/shard_map/ppermute | solution.py:319
  15.4 6.8 %collective-permute-start.5 = (f32[136,128]{1,0:T(8,128)S(1)}, f32[136,128]{1,0:T(8,128)S(1)}, u32[]{:S(2)}, u32[]{:S(2)}) collective-permute-start(f32[136,128]{1,0:T(8,128)S(1)} %pad_maximum_fusion), channel_id=1, source_target_pairs={{0,24},{4,28},{8,16},{12,20},{16,8},{20,12},{24,0},{28,4},{1,25},{... | collective-permute-start | bytes 208904 | tf_op jit(solution)/shard_map/ppermute | solution.py:319
  19.0 5.5 %collective-permute-start.6 = (f32[136,128]{1,0:T(8,128)S(1)}, f32[136,128]{1,0:T(8,128)S(1)}, u32[]{:S(2)}, u32[]{:S(2)}) collective-permute-start(f32[136,128]{1,0:T(8,128)S(1)} %concatenate.8), channel_id=1, source_target_pairs={{0,16},{4,20},{8,24},{12,28},{16,0},{20,4},{24,8},{28,12},{1,17},{... | collective-permute-start | bytes 208904 | tf_op jit(solution)/shard_map/ppermute | solution.py:319
  19.1 5.4 %collective-permute-start.7 = (f32[136,128]{1,0:T(8,128)S(1)}, f32[136,128]{1,0:T(8,128)S(1)}, u32[]{:S(2)}, u32[]{:S(2)}) collective-permute-start(f32[136,128]{1,0:T(8,128)S(1)} %slice.16), channel_id=1, source_target_pairs={{0,4},{4,0},{8,12},{12,8},{16,20},{20,16},{24,28},{28,24},{1,5},{5... | collective-permute-start | bytes 208904 | tf_op jit(solution)/shard_map/ppermute | solution.py:322

commit v4 on v3

--- a/solution.py
+++ b/solution.py
@@ -149,16 +149,16 @@
     out_ref[...] = low
 
 
-def moments_kernel(zs, l0, l1, l2, l3, noise_ref, times_ref, *rest):
-    half = zs // 2
+def moments_kernel(zs, far, lows_ref, last_ref, noise_ref, times_ref, *rest):
+    near = [s for s in range(1, zs) if s not in far]
     send_far, keep_far, keep_near = rest[:3]
-    send_near = rest[3 : 2 + half]
-    pay, term = rest[2 + half :]
+    send_near = rest[3 : 3 + len(near)]
+    pay, term = rest[3 + len(near) :]
     paths, rows, points = noise_ref.shape
     me = lax.axis_index("path")
     z = me // 2
     first = me % 2 == 0
-    payoff = jnp.exp(jnp.minimum(jnp.minimum(l0[...], l1[...]), jnp.minimum(l2[...], l3[...])))
+    payoff = jnp.exp(jnp.minimum(lows_ref[...], last_ref[...]))
     pay[...] = payoff
     totals = jnp.sum(payoff, axis=0, keepdims=True)
     for step in range(zs):
@@ -166,11 +166,12 @@
         columns = pl.ds(pl.multiple_of((z ^ s) * LANES, LANES), LANES)
         weights = [pay[k : k + 1, columns] for k in range(paths)]
         root_tau = jnp.sqrt(1.0 - times_ref[0:1, columns])
-        if s >= half:
-            (same, at), (other, past) = (keep_far, step * LANES), (send_far, step * LANES)
+        if s in far:
+            at = past = far.index(s) * LANES
+            same, other = keep_far, send_far
         else:
-            near = keep_near if s == 0 else send_near[s - 1]
-            (same, at), (other, past) = (near, 0), (near, LANES)
+            at, past = 0, LANES
+            same = other = keep_near if s == 0 else send_near[near.index(s)]
 
         def tile(r):
             n = min(16, rows - r)
@@ -303,17 +304,22 @@
     ])
     held_noise = jnp.transpose(held_noise, (1, 0, 2))
 
-    others = [
-        lax.ppermute(lows, "dim", [(i, i ^ s) for i in range(dims)]) for s in range(1, dims)
-    ]
+    last = None
+    for bit in [1 << n for n in range(dims.bit_length() - 1)]:
+        if last is not None:
+            lows = jnp.minimum(lows, last)
+        last = lax.ppermute(lows, "dim", [(i, i ^ bit) for i in range(dims)])
+
+    far = tuple(range(half, zs))
+    near = [s for s in range(1, zs) if s not in far]
     send_far, keep_far, keep_near, *send_near = pl.pallas_call(
-        functools.partial(moments_kernel, zs),
-        out_shape=[jax.ShapeDtypeStruct((half * LANES + EXTRA, LANES), F32)] * 2
-        + [jax.ShapeDtypeStruct((2 * LANES + EXTRA, LANES), F32)] * half,
+        functools.partial(moments_kernel, zs, far),
+        out_shape=[jax.ShapeDtypeStruct((len(far) * LANES + EXTRA, LANES), F32)] * 2
+        + [jax.ShapeDtypeStruct((2 * LANES + EXTRA, LANES), F32)] * (1 + len(near)),
         scratch_shapes=[pltpu.VMEM((paths, points), F32), pltpu.VMEM((2 * LANES, LANES), F32)],
         compiler_params=limit,
         name="moments",
-    )(lows, *others, held_noise, times_row)
+    )(lows, last, held_noise, times_row)
 
     def along_z(message, s):
         return lax.ppermute(message, "path", [(i, i ^ (2 * s)) for i in range(groups)])
@@ -321,22 +327,22 @@
     def along_y(message):
         return lax.ppermute(message, "path", [(i, i ^ 1) for i in range(groups)])
 
-    far = keep_far + along_y(send_far)
-    near = keep_near
-    for s in range(1, half):
-        near = near + along_z(send_near[s - 1], s)
+    far_sum = keep_far + along_y(send_far)
+    near_sum = keep_near
+    for s, send in zip(near, send_near):
+        near_sum = near_sum + along_z(send, s)
     scale = pl.pallas_call(
         functools.partial(scale_kernel, inner_total),
         out_shape=jax.ShapeDtypeStruct((LANES, LANES), F32),
         compiler_params=limit,
         name="scale",
     )(outer_noise, start_row, vol_row, times_row)
-    far_extra = far[half * LANES :]
+    far_extra = far_sum[len(far) * LANES :]
     arrived = []
-    for step in range(half):
-        block = far[step * LANES : (step + 1) * LANES]
-        arrived.append(along_z(jnp.concatenate([block, far_extra], axis=0), zs - 1 - step))
-    arrived.append(along_y(near[LANES:]))
+    for n, s in enumerate(far):
+        message = jnp.concatenate([far_sum[n * LANES : (n + 1) * LANES], far_extra], axis=0)
+        arrived.append(along_z(message, s))
+    arrived.append(along_y(near_sum[LANES:]))
 
     value, grad, point, point_grad = pl.pallas_call(
         functools.partial(final_kernel, inner_total, len(arrived)),
@@ -348,7 +354,7 @@
         ],
         compiler_params=limit,
         name="final",
-    )(near, far_extra, scale, outer_noise, start_row, vol_row, times_row, *arrived)
+    )(near_sum, far_extra, scale, outer_noise, start_row, vol_row, times_row, *arrived)
     return value.reshape(1), grad.reshape(rows), point.reshape(points // groups), jnp.transpose(point_grad)
 
 
@@ -360,7 +366,8 @@
         and LANES < rows <= 2 * LANES
         and is_power(groups)
         and groups >= 4
-        and dims == 4
+        and is_power(dims)
+        and dims > 1
         and points // LANES + 2 <= EXTRA
     )
     return (paired if fits else general)(inner_noise, outer_noise, start, vol, times)

time: 25.8 us -> 24.9 us (0.965)
  waiting for transfers between devices: 8.5 us -> 6.12 us
  starting transfers between devices: 11.6 us -> 13.1 us
    ppermute x2, waiting for transfers between devices: 2.57 us -> 1.42 us  [along_y(): return lax.ppermute(message, 'path', [(i, i ^ 1) for i in range(groups)])]
    ppermute x3, starting transfers between devices: 5.23 us -> 6.07 us  [along_z(): lax.ppermute(message, 'path', [(i, i ^ 2 * s) for i in range(groups)])]
    ppermute x3, waiting for transfers between devices: 3.55 us -> 2.85 us  [along_z(): lax.ppermute(message, 'path', [(i, i ^ 2 * s) for i in range(groups)])]
    ppermute x2, starting transfers between devices: 3.17 us -> 3.7 us  [along_y(): return lax.ppermute(message, 'path', [(i, i ^ 1) for i in range(groups)])]
    ppermute x3 -> x2, waiting for transfers between devices: 2.38 us -> 1.85 us  [paired(): last = lax.ppermute(lows, 'dim', [(i, i ^ bit) for i in range(dims)])]
    ppermute x3 -> x2, starting transfers between devices: 3.15 us -> 3.35 us  [paired(): last = lax.ppermute(lows, 'dim', [(i, i ^ bit) for i in range(dims)])]
  transfers between devices with their start and end apart: 8 -> 7, of which waited for: 5 -> 5; matrix products, arithmetic and copies ran while one was open for 3% -> 3% of each run, Pallas kernels for 1% -> 1%
where the time goes in v4:
time: 24.9 us; the launch traced here: 24.8 us
  starting transfers between devices  13.1 us (53%)
  waiting for transfers between devices  6.12 us (25%)
  Pallas kernels  4.04 us (16%)
  between operations  0.73 us (3%)
  local copies, waits for them, and re-layouts  0.71 us (3%)
    ppermute x3, starting transfers between devices, along_z(): lax.ppermute(message, 'path', [(i, i ^ 2 * s) for i in range(groups)])  6.07 us
    ppermute x2, starting transfers between devices, along_y(): return lax.ppermute(message, 'path', [(i, i ^ 1) for i in range(groups)])  3.7 us
    ppermute x2, starting transfers between devices, paired(): last = lax.ppermute(lows, 'dim', [(i, i ^ bit) for i in range(dims)])  3.35 us
    ppermute x3, waiting for transfers between devices, along_z(): lax.ppermute(message, 'path', [(i, i ^ 2 * s) for i in range(groups)])  2.85 us
    pallas_call x1, Pallas kernels, paired(): pl.pallas_call(minima_kernel, out_shape=(pltpu.VMEM((paths, points), F32)...  1.98 us
    ppermute x2, waiting for transfers between devices, paired(): last = lax.ppermute(lows, 'dim', [(i, i ^ bit) for i in range(dims)])  1.85 us
    ppermute x2, waiting for transfers between devices, along_y(): return lax.ppermute(message, 'path', [(i, i ^ 1) for i in range(groups)])  1.42 us
    pallas_call x1, Pallas kernels, paired(): pl.pallas_call(functools.partial(final_kernel, inner_total, len(arrived))...  1.1 us
  transfers between devices with their start and end apart: 7, of which 5 were waited for; matrix products, arithmetic and copies ran while one was open for 3% of the time, Pallas kernels for 1%

profile of v4, /device:TPU:0, one launch (start us, length us, event | category | flops | bytes accessed | tf_op | source)
XLA Modules:
  0.0 24.8 jit_solution(14580883181723904121)
XLA Ops:
  0.6 2.0 %minima.1 = (f32[8,512]{1,0:T(8,128)S(1)}, bf16[250,8,512]{2,1,0:T(8,128)(2,1)S(1)}) custom-call(bf16[250,8,512]{2,1,0:T(8,128)(2,1)} %bitcast.22, bf16[250,512]{1,0:T(8,128)(2,1)} %outer_ref.3, f32[1,250]{1,0:T(1,128)} %bitcast.16, f32[1,250]{1,0:T(1,128)} %bitcast.19, f32[1,512]{1,0:T(1,128)} %bitcast.12), custom_call_target="tpu_custom_call" | custom-call | tf_op jit(solution)/shard_map/minima/pallas_call | solution.py:283
  2.6 0.5 %collective-permute-start = (f32[8,512]{1,0:T(8,128)S(1)}, f32[8,512]{1,0:T(8,128)S(1)}, u32[]{:S(2)}, u32[]{:S(2)}) collective-permute-start(f32[8,512]{1,0:T(8,128)S(1)} %get-tuple-element.14), channel_id=1, source_target_pairs={{0,1},{1,0},{2,3},{3,2},{4,5},{5,4},{6,7},{7,6},{8,9},{9,8},{10,11... | collective-permute-start | bytes 49160 | tf_op jit(solution)/shard_map/ppermute | solution.py:311
  3.1 0.8 %collective-permute-done = f32[8,512]{1,0:T(8,128)S(1)} collective-permute-done((f32[8,512]{1,0:T(8,128)S(1)}, f32[8,512]{1,0:T(8,128)S(1)}, u32[]{:S(2)}, u32[]{:S(2)}) %collective-permute-start) | collective-permute-done | bytes 16416 | tf_op jit(solution)/shard_map/ppermute | solution.py:311
  4.0 2.8 %collective-permute-start.1 = (f32[8,512]{1,0:T(8,128)S(1)}, f32[8,512]{1,0:T(8,128)S(1)}, u32[]{:S(2)}, u32[]{:S(2)}) collective-permute-start(f32[8,512]{1,0:T(8,128)S(1)} %min.3.lows_ref), channel_id=1, source_target_pairs={{0,2},{1,3},{2,0},{3,1},{4,6},{5,7},{6,4},{7,5},{8,10},{9,11},{10,... | collective-permute-start | bytes 49160 | tf_op jit(solution)/shard_map/ppermute | solution.py:311
  6.8 0.0 copy-start.1
  6.8 0.7 %copy.11 = bf16[250,8,512]{2,0,1:T(8,128)(2,1)S(1)} copy(bf16[250,8,512]{2,1,0:T(8,128)(2,1)S(1)} %get-tuple-element.15) | data formatting | bytes 4096000 | tf_op jit(solution)/shard_map/minima/pallas_call | solution.py:283
  7.5 0.0 copy-start
  7.5 0.0 copy-start.2
  7.5 0.0 copy-start.3
  7.5 1.0 %collective-permute-done.1.last_ref = f32[8,512]{1,0:T(8,128)S(1)} collective-permute-done((f32[8,512]{1,0:T(8,128)S(1)}, f32[8,512]{1,0:T(8,128)S(1)}, u32[]{:S(2)}, u32[]{:S(2)}) %collective-permute-start.1) | collective-permute-done | bytes 16416 | tf_op jit(solution)/shard_map/ppermute | solution.py:311
  8.5 0.0 copy-done.1
  8.5 0.7 %moments.1 = (f32[264,128]{1,0:T(8,128)S(1)}, f32[264,128]{1,0:T(8,128)S(1)}, f32[264,128]{1,0:T(8,128)S(1)}, f32[264,128]{1,0:T(8,128)S(1)}) custom-call(f32[8,512]{1,0:T(8,128)S(1)} %min.3.lows_ref, f32[8,512]{1,0:T(8,128)S(1)} %collective-permute-done.1.last_ref, bf16[8,250,512]{2,1,0:T(8,128)(2,1)S(1)} %bitcast.11, f32[1,512]{1,0:T(1,128)S(1)} %bitcast.13), custom_call_target="tpu_custom_call" | custom-call | tf_op jit(solution)/shard_map/moments/pallas_call | solution.py:315
  9.2 2.1 %collective-permute-start.3 = (f32[264,128]{1,0:T(8,128)S(1)}, f32[264,128]{1,0:T(8,128)S(1)}, u32[]{:S(2)}, u32[]{:S(2)}) collective-permute-start(f32[264,128]{1,0:T(8,128)S(1)} %get-tuple-element.19), channel_id=1, source_target_pairs={{0,4},{4,0},{8,12},{12,8},{16,20},{20,16},{24,28},{28,24},{1,5},{5... | collective-permute-start | bytes 405512 | tf_op jit(solution)/shard_map/ppermute | solution.py:328
  11.4 1.6 %collective-permute-start.2 = (f32[264,128]{1,0:T(8,128)S(1)}, f32[264,128]{1,0:T(8,128)S(1)}, u32[]{:S(2)}, u32[]{:S(2)}) collective-permute-start(f32[264,128]{1,0:T(8,128)S(1)} %get-tuple-element.17), channel_id=1, source_target_pairs={{0,8},{4,12},{8,0},{12,4},{16,24},{20,28},{24,16},{28,20},{1,9},{5... | collective-permute-start | bytes 405512 | tf_op jit(solution)/shard_map/ppermute | solution.py:325
  12.9 1.4 %collective-permute-done.3 = f32[264,128]{1,0:T(8,128)S(1)} collective-permute-done((f32[264,128]{1,0:T(8,128)S(1)}, f32[264,128]{1,0:T(8,128)S(1)}, u32[]{:S(2)}, u32[]{:S(2)}) %collective-permute-start.3) | collective-permute-done | bytes 135200 | tf_op jit(solution)/shard_map/ppermute | solution.py:328
  14.4 3.1 %collective-permute-start.4 = (f32[136,128]{1,0:T(8,128)S(1)}, f32[136,128]{1,0:T(8,128)S(1)}, u32[]{:S(2)}, u32[]{:S(2)}) collective-permute-start(f32[136,128]{1,0:T(8,128)S(1)} %pad_maximum_fusion), channel_id=1, source_target_pairs={{0,16},{4,20},{8,24},{12,28},{16,0},{20,4},{24,8},{28,12},{1,17},{... | collective-permute-start | bytes 208904 | tf_op jit(solution)/shard_map/ppermute | solution.py:325
  17.6 1.4 %collective-permute-start.5 = (f32[136,128]{1,0:T(8,128)S(1)}, f32[136,128]{1,0:T(8,128)S(1)}, u32[]{:S(2)}, u32[]{:S(2)}) collective-permute-start(f32[136,128]{1,0:T(8,128)S(1)} %concatenate.8), channel_id=1, source_target_pairs={{0,24},{4,28},{8,16},{12,20},{16,8},{20,12},{24,0},{28,4},{1,25},{... | collective-permute-start | bytes 208904 | tf_op jit(solution)/shard_map/ppermute | solution.py:325
  18.9 0.0 collective-permute-done.2
  19.0 1.6 %collective-permute-start.6 = (f32[136,128]{1,0:T(8,128)S(1)}, f32[136,128]{1,0:T(8,128)S(1)}, u32[]{:S(2)}, u32[]{:S(2)}) collective-permute-start(f32[136,128]{1,0:T(8,128)S(1)} %slice.16), channel_id=1, source_target_pairs={{0,4},{4,0},{8,12},{12,8},{16,20},{20,16},{24,28},{28,24},{1,5},{5... | collective-permute-start | bytes 208904 | tf_op jit(solution)/shard_map/ppermute | solution.py:328
  20.5 0.0 copy-done
  20.5 0.0 copy-done.2
  20.5 0.0 copy-done.3
  20.6 0.3 %scale.1.scale_ref = f32[128,128]{1,0:T(8,128)S(1)} custom-call(bf16[250,512]{1,0:T(8,128)(2,1)S(1)} %copy-done, f32[1,250]{1,0:T(1,128)S(1)} %bitcast.17, f32[1,250]{1,0:T(1,128)S(1)} %bitcast.20, f32[1,512]{1,0:T(1,128)S(1)} %bitcast.14), custom_call_target="tpu_custom_call" | custom-call | tf_op jit(solution)/shard_map/scale/pallas_call | solution.py:334
  20.8 0.9 %collective-permute-done.4.rest_0_ = f32[136,128]{1,0:T(8,128)S(1)} collective-permute-done((f32[136,128]{1,0:T(8,128)S(1)}, f32[136,128]{1,0:T(8,128)S(1)}, u32[]{:S(2)}, u32[]{:S(2)}) %collective-permute-start.4) | collective-permute-done | bytes 69664 | tf_op jit(solution)/shard_map/ppermute | solution.py:325
  21.7 1.9 %collective-permute-done.5.rest_1_ = f32[136,128]{1,0:T(8,128)S(1)} collective-permute-done((f32[136,128]{1,0:T(8,128)S(1)}, f32[136,128]{1,0:T(8,128)S(1)}, u32[]{:S(2)}, u32[]{:S(2)}) %collective-permute-start.5) | collective-permute-done | bytes 69664 | tf_op jit(solution)/shard_map/ppermute | solution.py:325
  23.7 0.0 collective-permute-done.6.rest_2_
  23.7 1.1 %final.1 = (f32[1,1]{1,0:T(1,128)}, f32[1,250]{1,0:T(1,128)}, f32[1,64]{1,0:T(1,128)}, f32[64,250]{1,0:T(8,128)}) custom-call(f32[264,128]{1,0:T(8,128)S(1)} %add.6.near_ref, f32[8,128]{1,0:T(8,128)S(1)} %slice.14.far_extra_ref, f32[128,128]{1,0:T(8,128)S(1)} %scale.1.scale_ref, bf16[250,512]{1,0:T(8,128)(2,1)S(1)} %copy-done, f32[1,250]{1,0:T(1,128)S(1)} %bitcast.18, ...), custom_call_target="tpu_custom_call" | custom-call | tf_op jit(solution)/shard_map/final/pallas_call | solution.py:347
  (8 shorter events, 0.1 us)
Async XLA Ops:
  2.6 1.4 %collective-permute-start = (f32[8,512]{1,0:T(8,128)S(1)}, f32[8,512]{1,0:T(8,128)S(1)}, u32[]{:S(2)}, u32[]{:S(2)}) collective-permute-start(f32[8,512]{1,0:T(8,128)S(1)} %get-tuple-element.14), channel_id=1, source_target_pairs={{0,1},{1,0},{2,3},{3,2},{4,5},{5,4},{6,7},{7,6},{8,9},{9,8},{10,11... | collective-permute-start | bytes 49160 | tf_op jit(solution)/shard_map/ppermute | solution.py:311
  4.0 4.5 %collective-permute-start.1 = (f32[8,512]{1,0:T(8,128)S(1)}, f32[8,512]{1,0:T(8,128)S(1)}, u32[]{:S(2)}, u32[]{:S(2)}) collective-permute-start(f32[8,512]{1,0:T(8,128)S(1)} %min.3.lows_ref), channel_id=1, source_target_pairs={{0,2},{1,3},{2,0},{3,1},{4,6},{5,7},{6,4},{7,5},{8,10},{9,11},{10,... | collective-permute-start | bytes 49160 | tf_op jit(solution)/shard_map/ppermute | solution.py:311
  6.8 1.7 %copy-start.1 = (f32[512]{0:T(512)S(1)}, f32[512]{0:T(512)}, u32[]{:S(2)}) copy-start(f32[512]{0:T(512)} %param.9) | copy-start | bytes 6148
  7.5 13.1 %copy-start = (bf16[250,512]{1,0:T(8,128)(2,1)S(1)}, bf16[250,512]{1,0:T(8,128)(2,1)}, u32[]{:S(2)}) copy-start(bf16[250,512]{1,0:T(8,128)(2,1)} %outer_ref.3) | copy-start | bytes 768004
  7.5 13.1 %copy-start.2 = (f32[250]{0:T(256)S(1)}, f32[250]{0:T(256)}, u32[]{:S(2)}) copy-start(f32[250]{0:T(256)} %param.7) | copy-start | bytes 3004
  7.5 13.0 %copy-start.3 = (f32[250]{0:T(256)S(1)}, f32[250]{0:T(256)}, u32[]{:S(2)}) copy-start(f32[250]{0:T(256)} %param.8) | copy-start | bytes 3004
  9.2 5.1 %collective-permute-start.3 = (f32[264,128]{1,0:T(8,128)S(1)}, f32[264,128]{1,0:T(8,128)S(1)}, u32[]{:S(2)}, u32[]{:S(2)}) collective-permute-start(f32[264,128]{1,0:T(8,128)S(1)} %get-tuple-element.19), channel_id=1, source_target_pairs={{0,4},{4,0},{8,12},{12,8},{16,20},{20,16},{24,28},{28,24},{1,5},{5... | collective-permute-start | bytes 405512 | tf_op jit(solution)/shard_map/ppermute | solution.py:328
  11.4 7.6 %collective-permute-start.2 = (f32[264,128]{1,0:T(8,128)S(1)}, f32[264,128]{1,0:T(8,128)S(1)}, u32[]{:S(2)}, u32[]{:S(2)}) collective-permute-start(f32[264,128]{1,0:T(8,128)S(1)} %get-tuple-element.17), channel_id=1, source_target_pairs={{0,8},{4,12},{8,0},{12,4},{16,24},{20,28},{24,16},{28,20},{1,9},{5... | collective-permute-start | bytes 405512 | tf_op jit(solution)/shard_map/ppermute | solution.py:325
  14.4 7.3 %collective-permute-start.4 = (f32[136,128]{1,0:T(8,128)S(1)}, f32[136,128]{1,0:T(8,128)S(1)}, u32[]{:S(2)}, u32[]{:S(2)}) collective-permute-start(f32[136,128]{1,0:T(8,128)S(1)} %pad_maximum_fusion), channel_id=1, source_target_pairs={{0,16},{4,20},{8,24},{12,28},{16,0},{20,4},{24,8},{28,12},{1,17},{... | collective-permute-start | bytes 208904 | tf_op jit(solution)/shard_map/ppermute | solution.py:325
  17.6 6.1 %collective-permute-start.5 = (f32[136,128]{1,0:T(8,128)S(1)}, f32[136,128]{1,0:T(8,128)S(1)}, u32[]{:S(2)}, u32[]{:S(2)}) collective-permute-start(f32[136,128]{1,0:T(8,128)S(1)} %concatenate.8), channel_id=1, source_target_pairs={{0,24},{4,28},{8,16},{12,20},{16,8},{20,12},{24,0},{28,4},{1,25},{... | collective-permute-start | bytes 208904 | tf_op jit(solution)/shard_map/ppermute | solution.py:325
  19.0 4.7 %collective-permute-start.6 = (f32[136,128]{1,0:T(8,128)S(1)}, f32[136,128]{1,0:T(8,128)S(1)}, u32[]{:S(2)}, u32[]{:S(2)}) collective-permute-start(f32[136,128]{1,0:T(8,128)S(1)} %slice.16), channel_id=1, source_target_pairs={{0,4},{4,0},{8,12},{12,8},{16,20},{20,16},{24,28},{28,24},{1,5},{5... | collective-permute-start | bytes 208904 | tf_op jit(solution)/shard_map/ppermute | solution.py:328

commit v5 on v4

--- a/solution.py
+++ b/solution.py
@@ -19,7 +19,7 @@
 HALF = LANES // 2
 EXTRA = 8
 CHUNKS = 4
-STEP = 8
+STEP = 16
 F32 = jnp.float32
 
 
@@ -97,7 +97,7 @@
 
 def minima_kernel(
     noise_hbm, outer_hbm, start_hbm, vol_hbm, times_hbm, out_ref, noise_v,
-    outer_ref, start_ref, vol_ref, times_ref, level_v, slope_v, sems,
+    outer_ref, start_ref, vol_ref, times_ref, vol_s, level_v, sems,
 ):
     rows, paths, points = noise_hbm.shape
     cuts = [rows * c // CHUNKS // 16 * 16 for c in range(CHUNKS)] + [rows]
@@ -109,28 +109,33 @@
     small = [
         pltpu.make_async_copy(src, dst, sems.at[CHUNKS + c])
         for c, (src, dst) in enumerate(
-            [(vol_hbm, vol_ref), (start_hbm, start_ref), (times_hbm, times_ref), (outer_hbm, outer_ref)]
+            [
+                (vol_hbm, vol_ref),
+                (start_hbm, start_ref),
+                (times_hbm, times_ref),
+                (vol_hbm, vol_s),
+                (outer_hbm, outer_ref),
+            ]
         )
     ]
     for c in small + copies:
         c.start()
-    for c in small[:3]:
+    for c in small[:4]:
         c.wait()
     vol_row = vol_ref[...]
     base = as_columns(jnp.log(start_ref[...]) + (drift - 0.5 * vol_row * vol_row), rows)
     vol = as_columns(vol_row, rows)
     times = times_ref[...]
-    root_times = jnp.sqrt(times)
     root_tau = jnp.sqrt(1.0 - times)
-    small[3].wait()
+    inverse = 1.0 / root_tau
+    ratio = jnp.sqrt(times) * inverse
+    small[4].wait()
     for r, n in row_tiles(rows):
-        v = vol[r : r + n]
-        level_v[r : r + n, :] = base[r : r + n] + (v * root_times) * outer_ref[r : r + n, :].astype(F32)
-        slope_v[r : r + n, :] = v * root_tau
+        drifted = base[r : r + n] * inverse
+        level_v[r : r + n, :] = drifted + (vol[r : r + n] * ratio) * outer_ref[r : r + n, :].astype(F32)
 
     def level(d):
-        shock = noise_v[d].astype(F32)
-        return level_v[pl.ds(d, 1), :] + slope_v[pl.ds(d, 1), :] * shock
+        return level_v[pl.ds(d, 1), :] + vol_s[0, d] * noise_v[d].astype(F32)
 
     low = jnp.full((paths, points), jnp.inf, F32)
     for (lo, hi), c in zip(spans, copies):
@@ -146,58 +151,83 @@
         low = lax.fori_loop(0, whole, body, low)
         for d in range(lo + whole * STEP, hi):
             low = jnp.minimum(low, level(d))
-    out_ref[...] = low
-
-
-def moments_kernel(zs, far, lows_ref, last_ref, noise_ref, times_ref, *rest):
+    out_ref[...] = low * root_tau
+
+
+def split(value):
+    parts = []
+    for _ in range(3):
+        part = value.astype(jnp.bfloat16)
+        value = value - part.astype(F32)
+        parts.append(part)
+    return parts
+
+
+def parts_kernel(zs, noise_ref, out_ref):
+    paths, rows, points = noise_ref.shape
+    me = lax.axis_index("path")
+    z, y = me // 2, me % 2
+    for s in range(zs):
+        columns = pl.ds(pl.multiple_of((z ^ s) * LANES, LANES), LANES)
+
+        def tile(k, r):
+            n = min(16, rows - r)
+            if n <= 0:
+                return jnp.zeros((16, LANES), F32)
+            part = noise_ref[k, r : r + n, columns].astype(F32)
+            if n < 16:
+                part = jnp.concatenate([part, jnp.zeros((16 - n, LANES), F32)], axis=0)
+            return part
+
+        for k in range(paths):
+            for r in range(0, LANES, 16):
+                top, bottom = tile(k, r), tile(k, LANES + r)
+                out_ref[k, 2 * s + y, r : r + 16, :] = pack_low(top, bottom)
+                out_ref[k, 2 * s + 1 - y, r : r + 16, :] = pack_high(top, bottom)
+
+
+def moments_kernel(zs, far, lows_ref, last_ref, parts_ref, times_ref, *rest):
     near = [s for s in range(1, zs) if s not in far]
     send_far, keep_far, keep_near = rest[:3]
     send_near = rest[3 : 3 + len(near)]
     pay, term = rest[3 + len(near) :]
-    paths, rows, points = noise_ref.shape
+    paths, points = lows_ref.shape
     me = lax.axis_index("path")
     z = me // 2
     first = me % 2 == 0
     payoff = jnp.exp(jnp.minimum(lows_ref[...], last_ref[...]))
     pay[...] = payoff
     totals = jnp.sum(payoff, axis=0, keepdims=True)
-    for step in range(zs):
-        s = zs - 1 - step
+    for s in range(zs):
         columns = pl.ds(pl.multiple_of((z ^ s) * LANES, LANES), LANES)
-        weights = [pay[k : k + 1, columns] for k in range(paths)]
-        root_tau = jnp.sqrt(1.0 - times_ref[0:1, columns])
+        both = jnp.concatenate([pay[:, columns], jnp.sqrt(1.0 - times_ref[0:1, columns])], axis=0)
+        low, high = pack_low(both, both), pack_high(both, both)
         if s in far:
             at = past = far.index(s) * LANES
             same, other = keep_far, send_far
         else:
             at, past = 0, LANES
             same = other = keep_near if s == 0 else send_near[near.index(s)]
-
-        def tile(r):
-            n = min(16, rows - r)
-            if n <= 0:
-                return jnp.zeros((16, LANES), F32)
-            total = weights[0] * noise_ref[0, r : r + n, columns].astype(F32)
-            for k in range(1, paths):
-                total = total + weights[k] * noise_ref[k, r : r + n, columns].astype(F32)
-            if n < 16:
-                total = jnp.concatenate([total, jnp.zeros((16 - n, LANES), F32)], axis=0)
-            return total
-
-        for r in range(0, LANES, 16):
-            top, bottom = tile(r), tile(LANES + r)
-            low, high = pack_low(top, bottom), pack_high(top, bottom)
-            same[at + r : at + r + 16, :] = jnp.where(first, low, high)
-            other[past + r : past + r + 16, :] = jnp.where(first, high, low)
-            for to, part in ((r, top), (LANES + r, bottom)):
-                if step == 0:
-                    term[to : to + 16, :] = root_tau * part
+        for half, (ref, place) in enumerate(((same, at), (other, past))):
+            rows = jnp.where(first, low, high) if half == 0 else jnp.where(first, high, low)
+            weights = [jnp.broadcast_to(rows[k : k + 1], (8, LANES)) for k in range(paths + 1)]
+            for r in range(0, LANES, 8):
+                total = weights[0] * parts_ref[0, 2 * s + half, r : r + 8, :]
+                for k in range(1, paths):
+                    total = total + weights[k] * parts_ref[k, 2 * s + half, r : r + 8, :]
+                ref[place + r : place + r + 8, :] = total
+                if s == 0 and half == 0:
+                    term[r : r + 8, :] = weights[paths] * total
                 else:
-                    term[to : to + 16, :] += root_tau * part
+                    term[r : r + 8, :] += weights[paths] * total
     extras = [totals[:, c : c + LANES] for c in range(0, points, LANES)]
-    for r in (0, LANES):
-        extras.append(jnp.sum(jnp.transpose(term[r : r + LANES, :]), axis=0, keepdims=True))
-    extras.append(jnp.zeros((EXTRA - len(extras), LANES), F32))
+    side = lax.broadcasted_iota(jnp.int32, (16, LANES), 1) // HALF
+    picks = (lax.broadcasted_iota(jnp.int32, (16, LANES), 0) == side).astype(F32).astype(jnp.bfloat16)
+    sums = sum(
+        lax.dot_general(picks, part, (((1,), (1,)), ((), ())), preferred_element_type=F32)
+        for part in split(term[...])
+    )
+    extras.append(sums[0 : EXTRA - len(extras), :])
     extras = jnp.concatenate(extras, axis=0)
     for ref in (send_far, keep_far, *send_near):
         ref[ref.shape[0] - EXTRA :, :] = extras
@@ -259,13 +289,15 @@
     point_ref[...] = own[:, 0:HALF]
     root_times = jnp.sqrt(times_ref[...])
     weight = totals * root_times / inner_total + driver / root_times
-    outer_term = lax.dot_general(
-        jnp.broadcast_to(weight, (8, points)),
-        outer_ref[...].astype(F32),
-        (((1,), (1,)), ((), ())),
-        precision=lax.Precision.HIGHEST,
-        preferred_element_type=F32,
-    )[0:1, :]
+    parts_of = [part.astype(F32) for part in split(weight)]
+    weights = jnp.concatenate(parts_of + [jnp.zeros((13, points), F32)], axis=0).astype(jnp.bfloat16)
+    outer_term = jnp.sum(
+        lax.dot_general(
+            weights, outer_ref[...], (((1,), (1,)), ((), ())), preferred_element_type=F32
+        ),
+        axis=0,
+        keepdims=True,
+    )
     grad_ref[...] = (inner_term[:, 0:rows] / inner_total + outer_term) / (
         points * vol_ref[...] * start_ref[...]
     )
@@ -292,9 +324,9 @@
             pltpu.VMEM((1, rows), F32),
             pltpu.VMEM((1, rows), F32),
             pltpu.VMEM((1, points), F32),
+            pltpu.SMEM((1, rows), F32),
             pltpu.VMEM((rows, points), F32),
-            pltpu.VMEM((rows, points), F32),
-            pltpu.SemaphoreType.DMA((CHUNKS + 4,)),
+            pltpu.SemaphoreType.DMA((CHUNKS + 5,)),
         ],
         compiler_params=limit,
         name="minima",
@@ -310,16 +342,26 @@
             lows = jnp.minimum(lows, last)
         last = lax.ppermute(lows, "dim", [(i, i ^ bit) for i in range(dims)])
 
+    parts = pl.pallas_call(
+        functools.partial(parts_kernel, zs),
+        out_shape=pltpu.VMEM((paths, 2 * zs, LANES, LANES), F32),
+        compiler_params=limit,
+        cost_estimate=pl.CostEstimate(
+            flops=paths * rows * points, bytes_accessed=6 * paths * rows * points, transcendentals=0
+        ),
+        name="parts",
+    )(held_noise)
+
     far = tuple(range(half, zs))
     near = [s for s in range(1, zs) if s not in far]
     send_far, keep_far, keep_near, *send_near = pl.pallas_call(
         functools.partial(moments_kernel, zs, far),
-        out_shape=[jax.ShapeDtypeStruct((len(far) * LANES + EXTRA, LANES), F32)] * 2
-        + [jax.ShapeDtypeStruct((2 * LANES + EXTRA, LANES), F32)] * (1 + len(near)),
-        scratch_shapes=[pltpu.VMEM((paths, points), F32), pltpu.VMEM((2 * LANES, LANES), F32)],
+        out_shape=[pltpu.VMEM((len(far) * LANES + EXTRA, LANES), F32)] * 2
+        + [pltpu.VMEM((2 * LANES + EXTRA, LANES), F32)] * (1 + len(near)),
+        scratch_shapes=[pltpu.VMEM((paths, points), F32), pltpu.VMEM((LANES, LANES), F32)],
         compiler_params=limit,
         name="moments",
-    )(lows, last, held_noise, times_row)
+    )(lows, last, parts, times_row)
 
     def along_z(message, s):
         return lax.ppermute(message, "path", [(i, i ^ (2 * s)) for i in range(groups)])
@@ -333,7 +375,7 @@
         near_sum = near_sum + along_z(send, s)
     scale = pl.pallas_call(
         functools.partial(scale_kernel, inner_total),
-        out_shape=jax.ShapeDtypeStruct((LANES, LANES), F32),
+        out_shape=pltpu.VMEM((LANES, LANES), F32),
         compiler_params=limit,
         name="scale",
     )(outer_noise, start_row, vol_row, times_row)

time: 24.9 us -> 24.5 us (0.984)
  waiting for transfers between devices: 6.12 us -> 5.47 us
  Pallas kernels: 4.04 us -> 4.32 us
    ppermute x2, waiting for transfers between devices: 1.85 us -> 1.09 us  [paired(): last = lax.ppermute(lows, 'dim', [(i, i ^ bit) for i in range(dims)])]
    pallas_call x2 -> x3, Pallas kernels: 0.96 us -> 1.61 us  [the longest x1 0.75 us: paired(): pl.pallas_call(functools.partial(parts_kernel, zs), out_shape=pltpu.VMEM(...]
    pallas_call x1, Pallas kernels: 1.1 us -> 0.8 us  [paired(): pl.pallas_call(functools.partial(final_kernel, inner_total, len(arrived))...]
  transfers between devices with their start and end apart: 7 -> 7, of which waited for: 5 -> 5; matrix products, arithmetic and copies ran while one was open for 3% -> 3% of each run, Pallas kernels for 1% -> 4%
where the time goes in v5:
time: 24.5 us; the launch traced here: 24.3 us
  starting transfers between devices  13 us (53%)
  waiting for transfers between devices  5.47 us (22%)
  Pallas kernels  4.32 us (18%)
  between operations  0.74 us (3%)
  local copies, waits for them, and re-layouts  0.71 us (3%)
    ppermute x3, starting transfers between devices, along_z(): lax.ppermute(message, 'path', [(i, i ^ 2 * s) for i in range(groups)])  5.97 us
    ppermute x2, starting transfers between devices, along_y(): return lax.ppermute(message, 'path', [(i, i ^ 1) for i in range(groups)])  3.68 us
    ppermute x2, starting transfers between devices, paired(): last = lax.ppermute(lows, 'dim', [(i, i ^ bit) for i in range(dims)])  3.35 us
    ppermute x3, waiting for transfers between devices, along_z(): lax.ppermute(message, 'path', [(i, i ^ 2 * s) for i in range(groups)])  2.86 us
    pallas_call x1, Pallas kernels, paired(): pl.pallas_call(minima_kernel, out_shape=(pltpu.VMEM((paths, points), F32)...  1.92 us
    ppermute x2, waiting for transfers between devices, along_y(): return lax.ppermute(message, 'path', [(i, i ^ 1) for i in range(groups)])  1.52 us
    ppermute x2, waiting for transfers between devices, paired(): last = lax.ppermute(lows, 'dim', [(i, i ^ bit) for i in range(dims)])  1.09 us
    pallas_call x1, Pallas kernels, paired(): pl.pallas_call(functools.partial(final_kernel, inner_total, len(arrived))...  0.8 us
  transfers between devices with their start and end apart: 7, of which 5 were waited for; matrix products, arithmetic and copies ran while one was open for 3% of the time, Pallas kernels for 4%

profile of v5, /device:TPU:0, one launch (start us, length us, event | category | flops | bytes accessed | tf_op | source)
XLA Modules:
  0.0 24.3 jit_solution(8605255687304383333)
XLA Ops:
  0.6 1.9 %minima.1 = (f32[8,512]{1,0:T(8,128)S(1)}, bf16[250,8,512]{2,1,0:T(8,128)(2,1)S(1)}) custom-call(bf16[250,8,512]{2,1,0:T(8,128)(2,1)} %bitcast.22, bf16[250,512]{1,0:T(8,128)(2,1)} %outer_ref.3, f32[1,250]{1,0:T(1,128)} %bitcast.16, f32[1,250]{1,0:T(1,128)} %bitcast.19, f32[1,512]{1,0:T(1,128)} %bitcast.12), custom_call_target="tpu_custom_call" | custom-call | tf_op jit(solution)/shard_map/minima/pallas_call | solution.py:315
  2.6 0.5 %collective-permute-start = (f32[8,512]{1,0:T(8,128)S(1)}, f32[8,512]{1,0:T(8,128)S(1)}, u32[]{:S(2)}, u32[]{:S(2)}) collective-permute-start(f32[8,512]{1,0:T(8,128)S(1)} %get-tuple-element.14), channel_id=1, source_target_pairs={{0,1},{1,0},{2,3},{3,2},{4,5},{5,4},{6,7},{7,6},{8,9},{9,8},{10,11... | collective-permute-start | bytes 49160 | tf_op jit(solution)/shard_map/ppermute | solution.py:343
  3.1 0.8 %collective-permute-done = f32[8,512]{1,0:T(8,128)S(1)} collective-permute-done((f32[8,512]{1,0:T(8,128)S(1)}, f32[8,512]{1,0:T(8,128)S(1)}, u32[]{:S(2)}, u32[]{:S(2)}) %collective-permute-start) | collective-permute-done | bytes 16416 | tf_op jit(solution)/shard_map/ppermute | solution.py:343
  3.9 2.8 %collective-permute-start.1 = (f32[8,512]{1,0:T(8,128)S(1)}, f32[8,512]{1,0:T(8,128)S(1)}, u32[]{:S(2)}, u32[]{:S(2)}) collective-permute-start(f32[8,512]{1,0:T(8,128)S(1)} %min.3.lows_ref), channel_id=1, source_target_pairs={{0,2},{1,3},{2,0},{3,1},{4,6},{5,7},{6,4},{7,5},{8,10},{9,11},{10,... | collective-permute-start | bytes 49160 | tf_op jit(solution)/shard_map/ppermute | solution.py:343
  6.7 0.7 %copy.11 = bf16[250,8,512]{2,0,1:T(8,128)(2,1)S(1)} copy(bf16[250,8,512]{2,1,0:T(8,128)(2,1)S(1)} %get-tuple-element.15) | data formatting | bytes 4096000 | tf_op jit(solution)/shard_map/minima/pallas_call | solution.py:315
  7.4 0.0 copy-start.1
  7.4 0.7 %parts.1.parts_ref = f32[8,8,128,128]{3,2,1,0:T(8,128)S(1)} custom-call(bf16[8,250,512]{2,1,0:T(8,128)(2,1)S(1)} %bitcast.11), custom_call_target="tpu_custom_call" | custom-call | flops 1024000 | bytes 6144000 | tf_op jit(solution)/shard_map/parts/pallas_call | solution.py:345
  8.2 0.0 copy-start
  8.2 0.0 copy-start.2
  8.2 0.0 copy-start.3
  8.2 0.2 %collective-permute-done.1.last_ref = f32[8,512]{1,0:T(8,128)S(1)} collective-permute-done((f32[8,512]{1,0:T(8,128)S(1)}, f32[8,512]{1,0:T(8,128)S(1)}, u32[]{:S(2)}, u32[]{:S(2)}) %collective-permute-start.1) | collective-permute-done | bytes 16416 | tf_op jit(solution)/shard_map/ppermute | solution.py:343
  8.5 0.0 copy-done.1
  8.5 0.6 %moments.1 = (f32[264,128]{1,0:T(8,128)S(1)}, f32[264,128]{1,0:T(8,128)S(1)}, f32[264,128]{1,0:T(8,128)S(1)}, f32[264,128]{1,0:T(8,128)S(1)}) custom-call(f32[8,512]{1,0:T(8,128)S(1)} %min.3.lows_ref, f32[8,512]{1,0:T(8,128)S(1)} %collective-permute-done.1.last_ref, f32[8,8,128,128]{3,2,1,0:T(8,128)S(1)} %parts.1.parts_ref, f32[1,512]{1,0:T(1,128)S(1)} %bitcast.13), custom_call_target="tpu_custom_call" | custom-call | tf_op jit(solution)/shard_map/moments/pallas_call | solution.py:357
  9.1 2.1 %collective-permute-start.3 = (f32[264,128]{1,0:T(8,128)S(1)}, f32[264,128]{1,0:T(8,128)S(1)}, u32[]{:S(2)}, u32[]{:S(2)}) collective-permute-start(f32[264,128]{1,0:T(8,128)S(1)} %get-tuple-element.19), channel_id=1, source_target_pairs={{0,4},{4,0},{8,12},{12,8},{16,20},{20,16},{24,28},{28,24},{1,5},{5... | collective-permute-start | bytes 405512 | tf_op jit(solution)/shard_map/ppermute | solution.py:370
  11.2 1.6 %collective-permute-start.2 = (f32[264,128]{1,0:T(8,128)S(1)}, f32[264,128]{1,0:T(8,128)S(1)}, u32[]{:S(2)}, u32[]{:S(2)}) collective-permute-start(f32[264,128]{1,0:T(8,128)S(1)} %get-tuple-element.17), channel_id=1, source_target_pairs={{0,8},{4,12},{8,0},{12,4},{16,24},{20,28},{24,16},{28,20},{1,9},{5... | collective-permute-start | bytes 405512 | tf_op jit(solution)/shard_map/ppermute | solution.py:367
  12.7 1.5 %collective-permute-done.3 = f32[264,128]{1,0:T(8,128)S(1)} collective-permute-done((f32[264,128]{1,0:T(8,128)S(1)}, f32[264,128]{1,0:T(8,128)S(1)}, u32[]{:S(2)}, u32[]{:S(2)}) %collective-permute-start.3) | collective-permute-done | bytes 135200 | tf_op jit(solution)/shard_map/ppermute | solution.py:370
  14.3 3.0 %collective-permute-start.4 = (f32[136,128]{1,0:T(8,128)S(1)}, f32[136,128]{1,0:T(8,128)S(1)}, u32[]{:S(2)}, u32[]{:S(2)}) collective-permute-start(f32[136,128]{1,0:T(8,128)S(1)} %pad_maximum_fusion), channel_id=1, source_target_pairs={{0,16},{4,20},{8,24},{12,28},{16,0},{20,4},{24,8},{28,12},{1,17},{... | collective-permute-start | bytes 208904 | tf_op jit(solution)/shard_map/ppermute | solution.py:367
  17.4 1.3 %collective-permute-start.5 = (f32[136,128]{1,0:T(8,128)S(1)}, f32[136,128]{1,0:T(8,128)S(1)}, u32[]{:S(2)}, u32[]{:S(2)}) collective-permute-start(f32[136,128]{1,0:T(8,128)S(1)} %concatenate.8), channel_id=1, source_target_pairs={{0,24},{4,28},{8,16},{12,20},{16,8},{20,12},{24,0},{28,4},{1,25},{... | collective-permute-start | bytes 208904 | tf_op jit(solution)/shard_map/ppermute | solution.py:367
  18.7 0.0 collective-permute-done.2
  18.8 1.6 %collective-permute-start.6 = (f32[136,128]{1,0:T(8,128)S(1)}, f32[136,128]{1,0:T(8,128)S(1)}, u32[]{:S(2)}, u32[]{:S(2)}) collective-permute-start(f32[136,128]{1,0:T(8,128)S(1)} %slice.16), channel_id=1, source_target_pairs={{0,4},{4,0},{8,12},{12,8},{16,20},{20,16},{24,28},{28,24},{1,5},{5... | collective-permute-start | bytes 208904 | tf_op jit(solution)/shard_map/ppermute | solution.py:370
  20.4 0.0 copy-done
  20.4 0.0 copy-done.2
  20.4 0.0 copy-done.3
  20.4 0.3 %scale.1.scale_ref = f32[128,128]{1,0:T(8,128)S(1)} custom-call(bf16[250,512]{1,0:T(8,128)(2,1)S(1)} %copy-done, f32[1,250]{1,0:T(1,128)S(1)} %bitcast.17, f32[1,250]{1,0:T(1,128)S(1)} %bitcast.20, f32[1,512]{1,0:T(1,128)S(1)} %bitcast.14), custom_call_target="tpu_custom_call" | custom-call | tf_op jit(solution)/shard_map/scale/pallas_call | solution.py:376
  20.6 1.0 %collective-permute-done.4.rest_0_ = f32[136,128]{1,0:T(8,128)S(1)} collective-permute-done((f32[136,128]{1,0:T(8,128)S(1)}, f32[136,128]{1,0:T(8,128)S(1)}, u32[]{:S(2)}, u32[]{:S(2)}) %collective-permute-start.4) | collective-permute-done | bytes 69664 | tf_op jit(solution)/shard_map/ppermute | solution.py:367
  21.7 1.8 %collective-permute-done.5.rest_1_ = f32[136,128]{1,0:T(8,128)S(1)} collective-permute-done((f32[136,128]{1,0:T(8,128)S(1)}, f32[136,128]{1,0:T(8,128)S(1)}, u32[]{:S(2)}, u32[]{:S(2)}) %collective-permute-start.5) | collective-permute-done | bytes 69664 | tf_op jit(solution)/shard_map/ppermute | solution.py:367
  23.5 0.0 collective-permute-done.6.rest_2_
  23.5 0.8 %final.1 = (f32[1,1]{1,0:T(1,128)}, f32[1,250]{1,0:T(1,128)}, f32[1,64]{1,0:T(1,128)}, f32[64,250]{1,0:T(8,128)}) custom-call(f32[264,128]{1,0:T(8,128)S(1)} %add.6.near_ref, f32[8,128]{1,0:T(8,128)S(1)} %slice.14.far_extra_ref, f32[128,128]{1,0:T(8,128)S(1)} %scale.1.scale_ref, bf16[250,512]{1,0:T(8,128)(2,1)S(1)} %copy-done, f32[1,250]{1,0:T(1,128)S(1)} %bitcast.18, ...), custom_call_target="tpu_custom_call" | custom-call | tf_op jit(solution)/shard_map/final/pallas_call | solution.py:389
  (8 shorter events, 0.1 us)
Async XLA Ops:
  2.6 1.4 %collective-permute-start = (f32[8,512]{1,0:T(8,128)S(1)}, f32[8,512]{1,0:T(8,128)S(1)}, u32[]{:S(2)}, u32[]{:S(2)}) collective-permute-start(f32[8,512]{1,0:T(8,128)S(1)} %get-tuple-element.14), channel_id=1, source_target_pairs={{0,1},{1,0},{2,3},{3,2},{4,5},{5,4},{6,7},{7,6},{8,9},{9,8},{10,11... | collective-permute-start | bytes 49160 | tf_op jit(solution)/shard_map/ppermute | solution.py:343
  3.9 4.5 %collective-permute-start.1 = (f32[8,512]{1,0:T(8,128)S(1)}, f32[8,512]{1,0:T(8,128)S(1)}, u32[]{:S(2)}, u32[]{:S(2)}) collective-permute-start(f32[8,512]{1,0:T(8,128)S(1)} %min.3.lows_ref), channel_id=1, source_target_pairs={{0,2},{1,3},{2,0},{3,1},{4,6},{5,7},{6,4},{7,5},{8,10},{9,11},{10,... | collective-permute-start | bytes 49160 | tf_op jit(solution)/shard_map/ppermute | solution.py:343
  7.4 1.1 %copy-start.1 = (f32[512]{0:T(512)S(1)}, f32[512]{0:T(512)}, u32[]{:S(2)}) copy-start(f32[512]{0:T(512)} %param.9) | copy-start | bytes 6148
  8.2 12.2 %copy-start = (bf16[250,512]{1,0:T(8,128)(2,1)S(1)}, bf16[250,512]{1,0:T(8,128)(2,1)}, u32[]{:S(2)}) copy-start(bf16[250,512]{1,0:T(8,128)(2,1)} %outer_ref.3) | copy-start | bytes 768004
  8.2 12.2 %copy-start.2 = (f32[250]{0:T(256)S(1)}, f32[250]{0:T(256)}, u32[]{:S(2)}) copy-start(f32[250]{0:T(256)} %param.7) | copy-start | bytes 3004
  8.2 12.2 %copy-start.3 = (f32[250]{0:T(256)S(1)}, f32[250]{0:T(256)}, u32[]{:S(2)}) copy-start(f32[250]{0:T(256)} %param.8) | copy-start | bytes 3004
  9.1 5.2 %collective-permute-start.3 = (f32[264,128]{1,0:T(8,128)S(1)}, f32[264,128]{1,0:T(8,128)S(1)}, u32[]{:S(2)}, u32[]{:S(2)}) collective-permute-start(f32[264,128]{1,0:T(8,128)S(1)} %get-tuple-element.19), channel_id=1, source_target_pairs={{0,4},{4,0},{8,12},{12,8},{16,20},{20,16},{24,28},{28,24},{1,5},{5... | collective-permute-start | bytes 405512 | tf_op jit(solution)/shard_map/ppermute | solution.py:370
  11.2 7.6 %collective-permute-start.2 = (f32[264,128]{1,0:T(8,128)S(1)}, f32[264,128]{1,0:T(8,128)S(1)}, u32[]{:S(2)}, u32[]{:S(2)}) collective-permute-start(f32[264,128]{1,0:T(8,128)S(1)} %get-tuple-element.17), channel_id=1, source_target_pairs={{0,8},{4,12},{8,0},{12,4},{16,24},{20,28},{24,16},{28,20},{1,9},{5... | collective-permute-start | bytes 405512 | tf_op jit(solution)/shard_map/ppermute | solution.py:367
  14.3 7.3 %collective-permute-start.4 = (f32[136,128]{1,0:T(8,128)S(1)}, f32[136,128]{1,0:T(8,128)S(1)}, u32[]{:S(2)}, u32[]{:S(2)}) collective-permute-start(f32[136,128]{1,0:T(8,128)S(1)} %pad_maximum_fusion), channel_id=1, source_target_pairs={{0,16},{4,20},{8,24},{12,28},{16,0},{20,4},{24,8},{28,12},{1,17},{... | collective-permute-start | bytes 208904 | tf_op jit(solution)/shard_map/ppermute | solution.py:367
  17.4 6.1 %collective-permute-start.5 = (f32[136,128]{1,0:T(8,128)S(1)}, f32[136,128]{1,0:T(8,128)S(1)}, u32[]{:S(2)}, u32[]{:S(2)}) collective-permute-start(f32[136,128]{1,0:T(8,128)S(1)} %concatenate.8), channel_id=1, source_target_pairs={{0,24},{4,28},{8,16},{12,20},{16,8},{20,12},{24,0},{28,4},{1,25},{... | collective-permute-start | bytes 208904 | tf_op jit(solution)/shard_map/ppermute | solution.py:367
  18.8 4.7 %collective-permute-start.6 = (f32[136,128]{1,0:T(8,128)S(1)}, f32[136,128]{1,0:T(8,128)S(1)}, u32[]{:S(2)}, u32[]{:S(2)}) collective-permute-start(f32[136,128]{1,0:T(8,128)S(1)} %slice.16), channel_id=1, source_target_pairs={{0,4},{4,0},{8,12},{12,8},{16,20},{20,16},{24,28},{28,24},{1,5},{5... | collective-permute-start | bytes 208904 | tf_op jit(solution)/shard_map/ppermute | solution.py:370

commit v6 on v5

--- a/solution.py
+++ b/solution.py
@@ -163,12 +163,23 @@
     return parts
 
 
+def owner(z, step, zs):
+    half = zs // 2
+    if step < half:
+        return z ^ step
+    turn = step - half
+    up, down = half + (z + turn) % half, (z - half + turn + 1) % half
+    if isinstance(z, int):
+        return up if z < half else down
+    return jnp.where(z < half, up, down)
+
+
 def parts_kernel(zs, noise_ref, out_ref):
     paths, rows, points = noise_ref.shape
     me = lax.axis_index("path")
     z, y = me // 2, me % 2
     for s in range(zs):
-        columns = pl.ds(pl.multiple_of((z ^ s) * LANES, LANES), LANES)
+        columns = pl.ds(pl.multiple_of(owner(z, s, zs) * LANES, LANES), LANES)
 
         def tile(k, r):
             n = min(16, rows - r)
@@ -186,11 +197,11 @@
                 out_ref[k, 2 * s + 1 - y, r : r + 16, :] = pack_high(top, bottom)
 
 
-def moments_kernel(zs, far, lows_ref, last_ref, parts_ref, times_ref, *rest):
-    near = [s for s in range(1, zs) if s not in far]
+def moments_kernel(zs, lows_ref, last_ref, parts_ref, times_ref, *rest):
+    half = zs // 2
     send_far, keep_far, keep_near = rest[:3]
-    send_near = rest[3 : 3 + len(near)]
-    pay, term = rest[3 + len(near) :]
+    send_near = rest[3 : 2 + half]
+    pay, term = rest[2 + half :]
     paths, points = lows_ref.shape
     me = lax.axis_index("path")
     z = me // 2
@@ -199,30 +210,30 @@
     pay[...] = payoff
     totals = jnp.sum(payoff, axis=0, keepdims=True)
     for s in range(zs):
-        columns = pl.ds(pl.multiple_of((z ^ s) * LANES, LANES), LANES)
+        columns = pl.ds(pl.multiple_of(owner(z, s, zs) * LANES, LANES), LANES)
         both = jnp.concatenate([pay[:, columns], jnp.sqrt(1.0 - times_ref[0:1, columns])], axis=0)
         low, high = pack_low(both, both), pack_high(both, both)
-        if s in far:
-            at = past = far.index(s) * LANES
+        if s >= half:
+            at = past = (s - half) * LANES
             same, other = keep_far, send_far
         else:
             at, past = 0, LANES
-            same = other = keep_near if s == 0 else send_near[near.index(s)]
-        for half, (ref, place) in enumerate(((same, at), (other, past))):
-            rows = jnp.where(first, low, high) if half == 0 else jnp.where(first, high, low)
+            same = other = keep_near if s == 0 else send_near[s - 1]
+        for side, (ref, place) in enumerate(((same, at), (other, past))):
+            rows = jnp.where(first, low, high) if side == 0 else jnp.where(first, high, low)
             weights = [jnp.broadcast_to(rows[k : k + 1], (8, LANES)) for k in range(paths + 1)]
             for r in range(0, LANES, 8):
-                total = weights[0] * parts_ref[0, 2 * s + half, r : r + 8, :]
+                total = weights[0] * parts_ref[0, 2 * s + side, r : r + 8, :]
                 for k in range(1, paths):
-                    total = total + weights[k] * parts_ref[k, 2 * s + half, r : r + 8, :]
+                    total = total + weights[k] * parts_ref[k, 2 * s + side, r : r + 8, :]
                 ref[place + r : place + r + 8, :] = total
-                if s == 0 and half == 0:
+                if s == 0 and side == 0:
                     term[r : r + 8, :] = weights[paths] * total
                 else:
                     term[r : r + 8, :] += weights[paths] * total
     extras = [totals[:, c : c + LANES] for c in range(0, points, LANES)]
-    side = lax.broadcasted_iota(jnp.int32, (16, LANES), 1) // HALF
-    picks = (lax.broadcasted_iota(jnp.int32, (16, LANES), 0) == side).astype(F32).astype(jnp.bfloat16)
+    lanes_of = lax.broadcasted_iota(jnp.int32, (16, LANES), 1) // HALF
+    picks = (lax.broadcasted_iota(jnp.int32, (16, LANES), 0) == lanes_of).astype(F32).astype(jnp.bfloat16)
     sums = sum(
         lax.dot_general(picks, part, (((1,), (1,)), ((), ())), preferred_element_type=F32)
         for part in split(term[...])
@@ -352,38 +363,37 @@
         name="parts",
     )(held_noise)
 
-    far = tuple(range(half, zs))
-    near = [s for s in range(1, zs) if s not in far]
     send_far, keep_far, keep_near, *send_near = pl.pallas_call(
-        functools.partial(moments_kernel, zs, far),
-        out_shape=[pltpu.VMEM((len(far) * LANES + EXTRA, LANES), F32)] * 2
-        + [pltpu.VMEM((2 * LANES + EXTRA, LANES), F32)] * (1 + len(near)),
+        functools.partial(moments_kernel, zs),
+        out_shape=[pltpu.VMEM((half * LANES + EXTRA, LANES), F32)] * 2
+        + [pltpu.VMEM((2 * LANES + EXTRA, LANES), F32)] * half,
         scratch_shapes=[pltpu.VMEM((paths, points), F32), pltpu.VMEM((LANES, LANES), F32)],
         compiler_params=limit,
         name="moments",
     )(lows, last, parts, times_row)
 
-    def along_z(message, s):
-        return lax.ppermute(message, "path", [(i, i ^ (2 * s)) for i in range(groups)])
+    def along_z(message, step):
+        route = [(i, 2 * owner(i // 2, step, zs) + i % 2) for i in range(groups)]
+        return lax.ppermute(message, "path", route)
 
     def along_y(message):
         return lax.ppermute(message, "path", [(i, i ^ 1) for i in range(groups)])
 
     far_sum = keep_far + along_y(send_far)
     near_sum = keep_near
-    for s, send in zip(near, send_near):
-        near_sum = near_sum + along_z(send, s)
+    for step in range(1, half):
+        near_sum = near_sum + along_z(send_near[step - 1], step)
     scale = pl.pallas_call(
         functools.partial(scale_kernel, inner_total),
         out_shape=pltpu.VMEM((LANES, LANES), F32),
         compiler_params=limit,
         name="scale",
     )(outer_noise, start_row, vol_row, times_row)
-    far_extra = far_sum[len(far) * LANES :]
+    far_extra = far_sum[half * LANES :]
     arrived = []
-    for n, s in enumerate(far):
+    for n in range(half):
         message = jnp.concatenate([far_sum[n * LANES : (n + 1) * LANES], far_extra], axis=0)
-        arrived.append(along_z(message, s))
+        arrived.append(along_z(message, half + n))
     arrived.append(along_y(near_sum[LANES:]))
 
     value, grad, point, point_grad = pl.pallas_call(

time: 24.5 us -> 23.8 us (0.971)
  waiting for transfers between devices: 5.47 us -> 4.96 us
    ppermute x3, waiting for transfers between devices: 2.86 us -> 2.07 us  [along_z(): return lax.ppermute(message, 'path', route)]
    ppermute x3, starting transfers between devices: 5.97 us -> 5.69 us  [along_z(): return lax.ppermute(message, 'path', route)]
    ppermute x2, waiting for transfers between devices: 1.52 us -> 1.81 us  [along_y(): return lax.ppermute(message, 'path', [(i, i ^ 1) for i in range(groups)])]
  transfers between devices with their start and end apart: 7 -> 7, of which waited for: 5 -> 6; matrix products, arithmetic and copies ran while one was open for 3% -> 3% of each run, Pallas kernels for 4% -> 4%
where the time goes in v6:
time: 23.8 us; the launch traced here: 23.7 us
  starting transfers between devices  12.9 us (54%)
  waiting for transfers between devices  4.96 us (21%)
  Pallas kernels  4.32 us (18%)
  between operations  0.74 us (3%)
  local copies, waits for them, and re-layouts  0.71 us (3%)
    ppermute x3, starting transfers between devices, along_z(): return lax.ppermute(message, 'path', route)  5.69 us
    ppermute x2, starting transfers between devices, along_y(): return lax.ppermute(message, 'path', [(i, i ^ 1) for i in range(groups)])  3.84 us
    ppermute x2, starting transfers between devices, paired(): last = lax.ppermute(lows, 'dim', [(i, i ^ bit) for i in range(dims)])  3.35 us
    ppermute x3, waiting for transfers between devices, along_z(): return lax.ppermute(message, 'path', route)  2.07 us
    pallas_call x1, Pallas kernels, paired(): pl.pallas_call(minima_kernel, out_shape=(pltpu.VMEM((paths, points), F32)...  1.92 us
    ppermute x2, waiting for transfers between devices, along_y(): return lax.ppermute(message, 'path', [(i, i ^ 1) for i in range(groups)])  1.81 us
    ppermute x2, waiting for transfers between devices, paired(): last = lax.ppermute(lows, 'dim', [(i, i ^ bit) for i in range(dims)])  1.08 us
    pallas_call x1, Pallas kernels, paired(): pl.pallas_call(functools.partial(final_kernel, inner_total, len(arrived))...  0.8 us
  transfers between devices with their start and end apart: 7, of which 6 were waited for; matrix products, arithmetic and copies ran while one was open for 3% of the time, Pallas kernels for 4%

profile of v6, /device:TPU:0, one launch (start us, length us, event | category | flops | bytes accessed | tf_op | source)
XLA Modules:
  0.0 23.7 jit_solution(15600277622060115443)
XLA Ops:
  0.6 1.9 %minima.1 = (f32[8,512]{1,0:T(8,128)S(1)}, bf16[250,8,512]{2,1,0:T(8,128)(2,1)S(1)}) custom-call(bf16[250,8,512]{2,1,0:T(8,128)(2,1)} %bitcast.22, bf16[250,512]{1,0:T(8,128)(2,1)} %outer_ref.3, f32[1,250]{1,0:T(1,128)} %bitcast.16, f32[1,250]{1,0:T(1,128)} %bitcast.19, f32[1,512]{1,0:T(1,128)} %bitcast.12), custom_call_target="tpu_custom_call" | custom-call | tf_op jit(solution)/shard_map/minima/pallas_call | solution.py:326
  2.6 0.5 %collective-permute-start = (f32[8,512]{1,0:T(8,128)S(1)}, f32[8,512]{1,0:T(8,128)S(1)}, u32[]{:S(2)}, u32[]{:S(2)}) collective-permute-start(f32[8,512]{1,0:T(8,128)S(1)} %get-tuple-element.14), channel_id=1, source_target_pairs={{0,1},{1,0},{2,3},{3,2},{4,5},{5,4},{6,7},{7,6},{8,9},{9,8},{10,11... | collective-permute-start | bytes 49160 | tf_op jit(solution)/shard_map/ppermute | solution.py:354
  3.1 0.8 %collective-permute-done = f32[8,512]{1,0:T(8,128)S(1)} collective-permute-done((f32[8,512]{1,0:T(8,128)S(1)}, f32[8,512]{1,0:T(8,128)S(1)}, u32[]{:S(2)}, u32[]{:S(2)}) %collective-permute-start) | collective-permute-done | bytes 16416 | tf_op jit(solution)/shard_map/ppermute | solution.py:354
  3.9 2.8 %collective-permute-start.1 = (f32[8,512]{1,0:T(8,128)S(1)}, f32[8,512]{1,0:T(8,128)S(1)}, u32[]{:S(2)}, u32[]{:S(2)}) collective-permute-start(f32[8,512]{1,0:T(8,128)S(1)} %min.3.lows_ref), channel_id=1, source_target_pairs={{0,2},{1,3},{2,0},{3,1},{4,6},{5,7},{6,4},{7,5},{8,10},{9,11},{10,... | collective-permute-start | bytes 49160 | tf_op jit(solution)/shard_map/ppermute | solution.py:354
  6.7 0.7 %copy.11 = bf16[250,8,512]{2,0,1:T(8,128)(2,1)S(1)} copy(bf16[250,8,512]{2,1,0:T(8,128)(2,1)S(1)} %get-tuple-element.15) | data formatting | bytes 4096000 | tf_op jit(solution)/shard_map/minima/pallas_call | solution.py:326
  7.4 0.0 copy-start.1
  7.4 0.7 %parts.1.parts_ref = f32[8,8,128,128]{3,2,1,0:T(8,128)S(1)} custom-call(bf16[8,250,512]{2,1,0:T(8,128)(2,1)S(1)} %bitcast.11), custom_call_target="tpu_custom_call" | custom-call | flops 1024000 | bytes 6144000 | tf_op jit(solution)/shard_map/parts/pallas_call | solution.py:356
  8.2 0.0 copy-start
  8.2 0.0 copy-start.2
  8.2 0.0 copy-start.3
  8.2 0.2 %collective-permute-done.1.last_ref = f32[8,512]{1,0:T(8,128)S(1)} collective-permute-done((f32[8,512]{1,0:T(8,128)S(1)}, f32[8,512]{1,0:T(8,128)S(1)}, u32[]{:S(2)}, u32[]{:S(2)}) %collective-permute-start.1) | collective-permute-done | bytes 16416 | tf_op jit(solution)/shard_map/ppermute | solution.py:354
  8.5 0.0 copy-done.1
  8.5 0.6 %moments.1 = (f32[264,128]{1,0:T(8,128)S(1)}, f32[264,128]{1,0:T(8,128)S(1)}, f32[264,128]{1,0:T(8,128)S(1)}, f32[264,128]{1,0:T(8,128)S(1)}) custom-call(f32[8,512]{1,0:T(8,128)S(1)} %min.3.lows_ref, f32[8,512]{1,0:T(8,128)S(1)} %collective-permute-done.1.last_ref, f32[8,8,128,128]{3,2,1,0:T(8,128)S(1)} %parts.1.parts_ref, f32[1,512]{1,0:T(1,128)S(1)} %bitcast.13), custom_call_target="tpu_custom_call" | custom-call | tf_op jit(solution)/shard_map/moments/pallas_call | solution.py:366
  9.1 2.1 %collective-permute-start.3 = (f32[264,128]{1,0:T(8,128)S(1)}, f32[264,128]{1,0:T(8,128)S(1)}, u32[]{:S(2)}, u32[]{:S(2)}) collective-permute-start(f32[264,128]{1,0:T(8,128)S(1)} %get-tuple-element.19), channel_id=1, source_target_pairs={{0,4},{4,0},{8,12},{12,8},{16,20},{20,16},{24,28},{28,24},{1,5},{5... | collective-permute-start | bytes 405512 | tf_op jit(solution)/shard_map/ppermute | solution.py:380
  11.2 1.6 %collective-permute-start.2 = (f32[264,128]{1,0:T(8,128)S(1)}, f32[264,128]{1,0:T(8,128)S(1)}, u32[]{:S(2)}, u32[]{:S(2)}) collective-permute-start(f32[264,128]{1,0:T(8,128)S(1)} %get-tuple-element.17), channel_id=1, source_target_pairs={{0,8},{4,12},{8,0},{12,4},{16,24},{20,28},{24,16},{28,20},{1,9},{5... | collective-permute-start | bytes 405512 | tf_op jit(solution)/shard_map/ppermute | solution.py:377
  12.7 1.5 %collective-permute-done.3 = f32[264,128]{1,0:T(8,128)S(1)} collective-permute-done((f32[264,128]{1,0:T(8,128)S(1)}, f32[264,128]{1,0:T(8,128)S(1)}, u32[]{:S(2)}, u32[]{:S(2)}) %collective-permute-start.3) | collective-permute-done | bytes 135200 | tf_op jit(solution)/shard_map/ppermute | solution.py:380
  14.3 3.0 %collective-permute-start.4 = (f32[136,128]{1,0:T(8,128)S(1)}, f32[136,128]{1,0:T(8,128)S(1)}, u32[]{:S(2)}, u32[]{:S(2)}) collective-permute-start(f32[136,128]{1,0:T(8,128)S(1)} %pad_maximum_fusion), channel_id=1, source_target_pairs={{0,16},{4,20},{8,24},{12,28},{16,8},{20,12},{24,0},{28,4},{1,17},{... | collective-permute-start | bytes 208904 | tf_op jit(solution)/shard_map/ppermute | solution.py:377
  17.4 1.1 %collective-permute-start.5 = (f32[136,128]{1,0:T(8,128)S(1)}, f32[136,128]{1,0:T(8,128)S(1)}, u32[]{:S(2)}, u32[]{:S(2)}) collective-permute-start(f32[136,128]{1,0:T(8,128)S(1)} %concatenate.8), channel_id=1, source_target_pairs={{0,24},{4,28},{8,16},{12,20},{16,0},{20,4},{24,8},{28,12},{1,25},{... | collective-permute-start | bytes 208904 | tf_op jit(solution)/shard_map/ppermute | solution.py:377
  18.4 0.0 collective-permute-done.2
  18.5 1.7 %collective-permute-start.6 = (f32[136,128]{1,0:T(8,128)S(1)}, f32[136,128]{1,0:T(8,128)S(1)}, u32[]{:S(2)}, u32[]{:S(2)}) collective-permute-start(f32[136,128]{1,0:T(8,128)S(1)} %slice.16), channel_id=1, source_target_pairs={{0,4},{4,0},{8,12},{12,8},{16,20},{20,16},{24,28},{28,24},{1,5},{5... | collective-permute-start | bytes 208904 | tf_op jit(solution)/shard_map/ppermute | solution.py:380
  20.2 0.0 copy-done
  20.2 0.0 copy-done.2
  20.2 0.0 copy-done.3
  20.2 0.3 %scale.1.scale_ref = f32[128,128]{1,0:T(8,128)S(1)} custom-call(bf16[250,512]{1,0:T(8,128)(2,1)S(1)} %copy-done, f32[1,250]{1,0:T(1,128)S(1)} %bitcast.17, f32[1,250]{1,0:T(1,128)S(1)} %bitcast.20, f32[1,512]{1,0:T(1,128)S(1)} %bitcast.14), custom_call_target="tpu_custom_call" | custom-call | tf_op jit(solution)/shard_map/scale/pallas_call | solution.py:386
  20.5 0.7 %collective-permute-done.4.rest_0_ = f32[136,128]{1,0:T(8,128)S(1)} collective-permute-done((f32[136,128]{1,0:T(8,128)S(1)}, f32[136,128]{1,0:T(8,128)S(1)}, u32[]{:S(2)}, u32[]{:S(2)}) %collective-permute-start.4) | collective-permute-done | bytes 69664 | tf_op jit(solution)/shard_map/ppermute | solution.py:377
  21.2 1.4 %collective-permute-done.5.rest_1_ = f32[136,128]{1,0:T(8,128)S(1)} collective-permute-done((f32[136,128]{1,0:T(8,128)S(1)}, f32[136,128]{1,0:T(8,128)S(1)}, u32[]{:S(2)}, u32[]{:S(2)}) %collective-permute-start.5) | collective-permute-done | bytes 69664 | tf_op jit(solution)/shard_map/ppermute | solution.py:377
  22.6 0.3 %collective-permute-done.6.rest_2_ = f32[136,128]{1,0:T(8,128)S(1)} collective-permute-done((f32[136,128]{1,0:T(8,128)S(1)}, f32[136,128]{1,0:T(8,128)S(1)}, u32[]{:S(2)}, u32[]{:S(2)}) %collective-permute-start.6) | collective-permute-done | bytes 69664 | tf_op jit(solution)/shard_map/ppermute | solution.py:380
  22.9 0.8 %final.1 = (f32[1,1]{1,0:T(1,128)}, f32[1,250]{1,0:T(1,128)}, f32[1,64]{1,0:T(1,128)}, f32[64,250]{1,0:T(8,128)}) custom-call(f32[264,128]{1,0:T(8,128)S(1)} %add.6.near_ref, f32[8,128]{1,0:T(8,128)S(1)} %slice.14.far_extra_ref, f32[128,128]{1,0:T(8,128)S(1)} %scale.1.scale_ref, bf16[250,512]{1,0:T(8,128)(2,1)S(1)} %copy-done, f32[1,250]{1,0:T(1,128)S(1)} %bitcast.18, ...), custom_call_target="tpu_custom_call" | custom-call | tf_op jit(solution)/shard_map/final/pallas_call | solution.py:399
  (8 shorter events, 0.1 us)
Async XLA Ops:
  2.6 1.4 %collective-permute-start = (f32[8,512]{1,0:T(8,128)S(1)}, f32[8,512]{1,0:T(8,128)S(1)}, u32[]{:S(2)}, u32[]{:S(2)}) collective-permute-start(f32[8,512]{1,0:T(8,128)S(1)} %get-tuple-element.14), channel_id=1, source_target_pairs={{0,1},{1,0},{2,3},{3,2},{4,5},{5,4},{6,7},{7,6},{8,9},{9,8},{10,11... | collective-permute-start | bytes 49160 | tf_op jit(solution)/shard_map/ppermute | solution.py:354
  3.9 4.5 %collective-permute-start.1 = (f32[8,512]{1,0:T(8,128)S(1)}, f32[8,512]{1,0:T(8,128)S(1)}, u32[]{:S(2)}, u32[]{:S(2)}) collective-permute-start(f32[8,512]{1,0:T(8,128)S(1)} %min.3.lows_ref), channel_id=1, source_target_pairs={{0,2},{1,3},{2,0},{3,1},{4,6},{5,7},{6,4},{7,5},{8,10},{9,11},{10,... | collective-permute-start | bytes 49160 | tf_op jit(solution)/shard_map/ppermute | solution.py:354
  7.4 1.1 %copy-start.1 = (f32[512]{0:T(512)S(1)}, f32[512]{0:T(512)}, u32[]{:S(2)}) copy-start(f32[512]{0:T(512)} %param.9) | copy-start | bytes 6148
  8.2 12.1 %copy-start = (bf16[250,512]{1,0:T(8,128)(2,1)S(1)}, bf16[250,512]{1,0:T(8,128)(2,1)}, u32[]{:S(2)}) copy-start(bf16[250,512]{1,0:T(8,128)(2,1)} %outer_ref.3) | copy-start | bytes 768004
  8.2 12.0 %copy-start.2 = (f32[250]{0:T(256)S(1)}, f32[250]{0:T(256)}, u32[]{:S(2)}) copy-start(f32[250]{0:T(256)} %param.7) | copy-start | bytes 3004
  8.2 12.0 %copy-start.3 = (f32[250]{0:T(256)S(1)}, f32[250]{0:T(256)}, u32[]{:S(2)}) copy-start(f32[250]{0:T(256)} %param.8) | copy-start | bytes 3004
  9.1 5.2 %collective-permute-start.3 = (f32[264,128]{1,0:T(8,128)S(1)}, f32[264,128]{1,0:T(8,128)S(1)}, u32[]{:S(2)}, u32[]{:S(2)}) collective-permute-start(f32[264,128]{1,0:T(8,128)S(1)} %get-tuple-element.19), channel_id=1, source_target_pairs={{0,4},{4,0},{8,12},{12,8},{16,20},{20,16},{24,28},{28,24},{1,5},{5... | collective-permute-start | bytes 405512 | tf_op jit(solution)/shard_map/ppermute | solution.py:380
  11.2 7.3 %collective-permute-start.2 = (f32[264,128]{1,0:T(8,128)S(1)}, f32[264,128]{1,0:T(8,128)S(1)}, u32[]{:S(2)}, u32[]{:S(2)}) collective-permute-start(f32[264,128]{1,0:T(8,128)S(1)} %get-tuple-element.17), channel_id=1, source_target_pairs={{0,8},{4,12},{8,0},{12,4},{16,24},{20,28},{24,16},{28,20},{1,9},{5... | collective-permute-start | bytes 405512 | tf_op jit(solution)/shard_map/ppermute | solution.py:377
  14.3 6.8 %collective-permute-start.4 = (f32[136,128]{1,0:T(8,128)S(1)}, f32[136,128]{1,0:T(8,128)S(1)}, u32[]{:S(2)}, u32[]{:S(2)}) collective-permute-start(f32[136,128]{1,0:T(8,128)S(1)} %pad_maximum_fusion), channel_id=1, source_target_pairs={{0,16},{4,20},{8,24},{12,28},{16,8},{20,12},{24,0},{28,4},{1,17},{... | collective-permute-start | bytes 208904 | tf_op jit(solution)/shard_map/ppermute | solution.py:377
  17.4 5.2 %collective-permute-start.5 = (f32[136,128]{1,0:T(8,128)S(1)}, f32[136,128]{1,0:T(8,128)S(1)}, u32[]{:S(2)}, u32[]{:S(2)}) collective-permute-start(f32[136,128]{1,0:T(8,128)S(1)} %concatenate.8), channel_id=1, source_target_pairs={{0,24},{4,28},{8,16},{12,20},{16,0},{20,4},{24,8},{28,12},{1,25},{... | collective-permute-start | bytes 208904 | tf_op jit(solution)/shard_map/ppermute | solution.py:377
  18.5 4.4 %collective-permute-start.6 = (f32[136,128]{1,0:T(8,128)S(1)}, f32[136,128]{1,0:T(8,128)S(1)}, u32[]{:S(2)}, u32[]{:S(2)}) collective-permute-start(f32[136,128]{1,0:T(8,128)S(1)} %slice.16), channel_id=1, source_target_pairs={{0,4},{4,0},{8,12},{12,8},{16,20},{20,16},{24,28},{28,24},{1,5},{5... | collective-permute-start | bytes 208904 | tf_op jit(solution)/shard_map/ppermute | solution.py:380

commit v7 on v6

--- a/solution.py
+++ b/solution.py
@@ -18,7 +18,7 @@
 LANES = 128
 HALF = LANES // 2
 EXTRA = 8
-CHUNKS = 4
+CHUNKS = 8
 STEP = 16
 F32 = jnp.float32
 
@@ -197,16 +197,17 @@
                 out_ref[k, 2 * s + 1 - y, r : r + 16, :] = pack_high(top, bottom)
 
 
-def moments_kernel(zs, lows_ref, last_ref, parts_ref, times_ref, *rest):
+def moments_kernel(zs, n_lows, *refs):
     half = zs // 2
+    lows, (parts_ref, times_ref, *rest) = refs[:n_lows], refs[n_lows:]
     send_far, keep_far, keep_near = rest[:3]
     send_near = rest[3 : 2 + half]
     pay, term = rest[2 + half :]
-    paths, points = lows_ref.shape
+    paths, points = lows[0].shape
     me = lax.axis_index("path")
     z = me // 2
     first = me % 2 == 0
-    payoff = jnp.exp(jnp.minimum(lows_ref[...], last_ref[...]))
+    payoff = jnp.exp(functools.reduce(jnp.minimum, [low[...] for low in lows]))
     pay[...] = payoff
     totals = jnp.sum(payoff, axis=0, keepdims=True)
     for s in range(zs):
@@ -347,11 +348,10 @@
     ])
     held_noise = jnp.transpose(held_noise, (1, 0, 2))
 
-    last = None
-    for bit in [1 << n for n in range(dims.bit_length() - 1)]:
-        if last is not None:
-            lows = jnp.minimum(lows, last)
-        last = lax.ppermute(lows, "dim", [(i, i ^ bit) for i in range(dims)])
+    others = [
+        lax.ppermute(lows, "dim", [(i, i ^ s) for i in range(dims)])
+        for s in sorted(range(1, dims), key=lambda s: (s < 2, s))
+    ]
 
     parts = pl.pallas_call(
         functools.partial(parts_kernel, zs),
@@ -364,13 +364,13 @@
     )(held_noise)
 
     send_far, keep_far, keep_near, *send_near = pl.pallas_call(
-        functools.partial(moments_kernel, zs),
+        functools.partial(moments_kernel, zs, dims),
         out_shape=[pltpu.VMEM((half * LANES + EXTRA, LANES), F32)] * 2
         + [pltpu.VMEM((2 * LANES + EXTRA, LANES), F32)] * half,
         scratch_shapes=[pltpu.VMEM((paths, points), F32), pltpu.VMEM((LANES, LANES), F32)],
         compiler_params=limit,
         name="moments",
-    )(lows, last, parts, times_row)
+    )(lows, *others, parts, times_row)
 
     def along_z(message, step):
         route = [(i, 2 * owner(i // 2, step, zs) + i % 2) for i in range(groups)]

time: 23.8 us -> 23.8 us (level)
  starting transfers between devices: 12.9 us -> 11.8 us
  waiting for transfers between devices: 4.96 us -> 5.96 us
    ppermute x2, starting transfers between devices: 3.84 us -> 3.15 us  [along_y(): return lax.ppermute(message, 'path', [(i, i ^ 1) for i in range(groups)])]
    ppermute x2, waiting for transfers between devices: 1.81 us -> 2.28 us  [along_y(): return lax.ppermute(message, 'path', [(i, i ^ 1) for i in range(groups)])]
    ppermute x2 -> x3, waiting for transfers between devices: 1.08 us -> 1.5 us  [paired(): lax.ppermute(lows, 'dim', [(i, i ^ s) for i in range(dims)])]
    ppermute x2 -> x3, starting transfers between devices: 3.35 us -> 3.2 us  [paired(): lax.ppermute(lows, 'dim', [(i, i ^ s) for i in range(dims)])]
  transfers between devices with their start and end apart: 7 -> 8, of which waited for: 6 -> 6; matrix products, arithmetic and copies ran while one was open for 3% -> 3% of each run, Pallas kernels for 4% -> 4%
where the time goes in v7:
time: 23.8 us; the launch traced here: 23.6 us
  starting transfers between devices  11.8 us (50%)
  waiting for transfers between devices  5.96 us (25%)
  Pallas kernels  4.36 us (18%)
  between operations  0.74 us (3%)
  local copies, waits for them, and re-layouts  0.71 us (3%)
    ppermute x3, starting transfers between devices, along_z(): return lax.ppermute(message, 'path', route)  5.45 us
    ppermute x3, starting transfers between devices, paired(): lax.ppermute(lows, 'dim', [(i, i ^ s) for i in range(dims)])  3.2 us
    ppermute x2, starting transfers between devices, along_y(): return lax.ppermute(message, 'path', [(i, i ^ 1) for i in range(groups)])  3.15 us
    ppermute x2, waiting for transfers between devices, along_y(): return lax.ppermute(message, 'path', [(i, i ^ 1) for i in range(groups)])  2.28 us
    ppermute x3, waiting for transfers between devices, along_z(): return lax.ppermute(message, 'path', route)  2.18 us
    pallas_call x1, Pallas kernels, paired(): pl.pallas_call(minima_kernel, out_shape=(pltpu.VMEM((paths, points), F32)...  1.95 us
    ppermute x3, waiting for transfers between devices, paired(): lax.ppermute(lows, 'dim', [(i, i ^ s) for i in range(dims)])  1.5 us
    pallas_call x1, Pallas kernels, paired(): pl.pallas_call(functools.partial(final_kernel, inner_total, len(arrived))...  0.8 us
  transfers between devices with their start and end apart: 8, of which 6 were waited for; matrix products, arithmetic and copies ran while one was open for 3% of the time, Pallas kernels for 4%

profile of v7, /device:TPU:0, one launch (start us, length us, event | category | flops | bytes accessed | tf_op | source)
XLA Modules:
  0.0 23.6 jit_solution(2808234071410653769)
XLA Ops:
  0.6 1.9 %minima.1 = (f32[8,512]{1,0:T(8,128)S(1)}, bf16[250,8,512]{2,1,0:T(8,128)(2,1)S(1)}) custom-call(bf16[250,8,512]{2,1,0:T(8,128)(2,1)} %bitcast.22, bf16[250,512]{1,0:T(8,128)(2,1)} %outer_ref.3, f32[1,250]{1,0:T(1,128)} %bitcast.16, f32[1,250]{1,0:T(1,128)} %bitcast.19, f32[1,512]{1,0:T(1,128)} %bitcast.12), custom_call_target="tpu_custom_call" | custom-call | tf_op jit(solution)/shard_map/minima/pallas_call | solution.py:327
  2.6 3.0 %collective-permute-start = (f32[8,512]{1,0:T(8,128)S(1)}, f32[8,512]{1,0:T(8,128)S(1)}, u32[]{:S(2)}, u32[]{:S(2)}) collective-permute-start(f32[8,512]{1,0:T(8,128)S(1)} %get-tuple-element.14.refs_0_), channel_id=1, source_target_pairs={{0,2},{1,3},{2,0},{3,1},{4,6},{5,7},{6,4},{7,5},{8,10},{9,11},{10,... | collective-permute-start | bytes 49160 | tf_op jit(solution)/shard_map/ppermute | solution.py:352
  5.6 0.0 collective-permute-start.1
  5.6 0.2 collective-permute-start.2
  5.8 0.7 %copy.11 = bf16[250,8,512]{2,0,1:T(8,128)(2,1)S(1)} copy(bf16[250,8,512]{2,1,0:T(8,128)(2,1)S(1)} %get-tuple-element.15) | data formatting | bytes 4096000 | tf_op jit(solution)/shard_map/minima/pallas_call | solution.py:327
  6.5 0.0 copy-start.1
  6.5 0.7 %parts.1.refs_4_ = f32[8,8,128,128]{3,2,1,0:T(8,128)S(1)} custom-call(bf16[8,250,512]{2,1,0:T(8,128)(2,1)S(1)} %bitcast.11), custom_call_target="tpu_custom_call" | custom-call | flops 1024000 | bytes 6144000 | tf_op jit(solution)/shard_map/parts/pallas_call | solution.py:356
  7.2 0.0 copy-start
  7.2 0.0 copy-start.2
  7.2 0.0 copy-start.3
  7.3 0.1 collective-permute-done.refs_1_
  7.3 1.4 %collective-permute-done.1.refs_2_ = f32[8,512]{1,0:T(8,128)S(1)} collective-permute-done((f32[8,512]{1,0:T(8,128)S(1)}, f32[8,512]{1,0:T(8,128)S(1)}, u32[]{:S(2)}, u32[]{:S(2)}) %collective-permute-start.1) | collective-permute-done | bytes 16416 | tf_op jit(solution)/shard_map/ppermute | solution.py:352
  8.8 0.0 collective-permute-done.2.refs_3_
  8.8 0.0 copy-done.1
  8.8 0.6 %moments.1 = (f32[264,128]{1,0:T(8,128)S(1)}, f32[264,128]{1,0:T(8,128)S(1)}, f32[264,128]{1,0:T(8,128)S(1)}, f32[264,128]{1,0:T(8,128)S(1)}) custom-call(f32[8,512]{1,0:T(8,128)S(1)} %get-tuple-element.14.refs_0_, f32[8,512]{1,0:T(8,128)S(1)} %collective-permute-done.refs_1_, f32[8,512]{1,0:T(8,128)S(1)} %collective-permute-done.1.refs_2_, ...), custom_call_target="tpu_custom_call" | custom-call | tf_op jit(solution)/shard_map/moments/pallas_call | solution.py:366
  9.4 1.6 %collective-permute-start.4 = (f32[264,128]{1,0:T(8,128)S(1)}, f32[264,128]{1,0:T(8,128)S(1)}, u32[]{:S(2)}, u32[]{:S(2)}) collective-permute-start(f32[264,128]{1,0:T(8,128)S(1)} %get-tuple-element.19), channel_id=1, source_target_pairs={{0,4},{4,0},{8,12},{12,8},{16,20},{20,16},{24,28},{28,24},{1,5},{5... | collective-permute-start | bytes 405512 | tf_op jit(solution)/shard_map/ppermute | solution.py:380
  10.9 1.6 %collective-permute-start.3 = (f32[264,128]{1,0:T(8,128)S(1)}, f32[264,128]{1,0:T(8,128)S(1)}, u32[]{:S(2)}, u32[]{:S(2)}) collective-permute-start(f32[264,128]{1,0:T(8,128)S(1)} %get-tuple-element.17), channel_id=1, source_target_pairs={{0,8},{4,12},{8,0},{12,4},{16,24},{20,28},{24,16},{28,20},{1,9},{5... | collective-permute-start | bytes 405512 | tf_op jit(solution)/shard_map/ppermute | solution.py:377
  12.5 1.9 %collective-permute-done.4 = f32[264,128]{1,0:T(8,128)S(1)} collective-permute-done((f32[264,128]{1,0:T(8,128)S(1)}, f32[264,128]{1,0:T(8,128)S(1)}, u32[]{:S(2)}, u32[]{:S(2)}) %collective-permute-start.4) | collective-permute-done | bytes 135200 | tf_op jit(solution)/shard_map/ppermute | solution.py:380
  14.5 2.6 %collective-permute-start.5 = (f32[136,128]{1,0:T(8,128)S(1)}, f32[136,128]{1,0:T(8,128)S(1)}, u32[]{:S(2)}, u32[]{:S(2)}) collective-permute-start(f32[136,128]{1,0:T(8,128)S(1)} %pad_maximum_fusion), channel_id=1, source_target_pairs={{0,16},{4,20},{8,24},{12,28},{16,8},{20,12},{24,0},{28,4},{1,17},{... | collective-permute-start | bytes 208904 | tf_op jit(solution)/shard_map/ppermute | solution.py:377
  17.2 1.2 %collective-permute-start.6 = (f32[136,128]{1,0:T(8,128)S(1)}, f32[136,128]{1,0:T(8,128)S(1)}, u32[]{:S(2)}, u32[]{:S(2)}) collective-permute-start(f32[136,128]{1,0:T(8,128)S(1)} %concatenate.8), channel_id=1, source_target_pairs={{0,24},{4,28},{8,16},{12,20},{16,0},{20,4},{24,8},{28,12},{1,25},{... | collective-permute-start | bytes 208904 | tf_op jit(solution)/shard_map/ppermute | solution.py:377
  18.4 0.0 collective-permute-done.3
  18.4 1.6 %collective-permute-start.7 = (f32[136,128]{1,0:T(8,128)S(1)}, f32[136,128]{1,0:T(8,128)S(1)}, u32[]{:S(2)}, u32[]{:S(2)}) collective-permute-start(f32[136,128]{1,0:T(8,128)S(1)} %slice.16), channel_id=1, source_target_pairs={{0,4},{4,0},{8,12},{12,8},{16,20},{20,16},{24,28},{28,24},{1,5},{5... | collective-permute-start | bytes 208904 | tf_op jit(solution)/shard_map/ppermute | solution.py:380
  20.0 0.0 copy-done
  20.0 0.0 copy-done.2
  20.0 0.0 copy-done.3
  20.0 0.3 %scale.1.scale_ref = f32[128,128]{1,0:T(8,128)S(1)} custom-call(bf16[250,512]{1,0:T(8,128)(2,1)S(1)} %copy-done, f32[1,250]{1,0:T(1,128)S(1)} %bitcast.17, f32[1,250]{1,0:T(1,128)S(1)} %bitcast.20, f32[1,512]{1,0:T(1,128)S(1)} %bitcast.14), custom_call_target="tpu_custom_call" | custom-call | tf_op jit(solution)/shard_map/scale/pallas_call | solution.py:386
  20.3 1.1 %collective-permute-done.5.rest_0_ = f32[136,128]{1,0:T(8,128)S(1)} collective-permute-done((f32[136,128]{1,0:T(8,128)S(1)}, f32[136,128]{1,0:T(8,128)S(1)}, u32[]{:S(2)}, u32[]{:S(2)}) %collective-permute-start.5) | collective-permute-done | bytes 69664 | tf_op jit(solution)/shard_map/ppermute | solution.py:377
  21.4 1.1 %collective-permute-done.6.rest_1_ = f32[136,128]{1,0:T(8,128)S(1)} collective-permute-done((f32[136,128]{1,0:T(8,128)S(1)}, f32[136,128]{1,0:T(8,128)S(1)}, u32[]{:S(2)}, u32[]{:S(2)}) %collective-permute-start.6) | collective-permute-done | bytes 69664 | tf_op jit(solution)/shard_map/ppermute | solution.py:377
  22.5 0.3 %collective-permute-done.7.rest_2_ = f32[136,128]{1,0:T(8,128)S(1)} collective-permute-done((f32[136,128]{1,0:T(8,128)S(1)}, f32[136,128]{1,0:T(8,128)S(1)}, u32[]{:S(2)}, u32[]{:S(2)}) %collective-permute-start.7) | collective-permute-done | bytes 69664 | tf_op jit(solution)/shard_map/ppermute | solution.py:380
  22.8 0.8 %final.1 = (f32[1,1]{1,0:T(1,128)}, f32[1,250]{1,0:T(1,128)}, f32[1,64]{1,0:T(1,128)}, f32[64,250]{1,0:T(8,128)}) custom-call(f32[264,128]{1,0:T(8,128)S(1)} %add.6.near_ref, f32[8,128]{1,0:T(8,128)S(1)} %slice.14.far_extra_ref, f32[128,128]{1,0:T(8,128)S(1)} %scale.1.scale_ref, bf16[250,512]{1,0:T(8,128)(2,1)S(1)} %copy-done, f32[1,250]{1,0:T(1,128)S(1)} %bitcast.18, ...), custom_call_target="tpu_custom_call" | custom-call | tf_op jit(solution)/shard_map/final/pallas_call | solution.py:399
  (7 shorter events, 0.1 us)
Async XLA Ops:
  2.6 4.7 %collective-permute-start = (f32[8,512]{1,0:T(8,128)S(1)}, f32[8,512]{1,0:T(8,128)S(1)}, u32[]{:S(2)}, u32[]{:S(2)}) collective-permute-start(f32[8,512]{1,0:T(8,128)S(1)} %get-tuple-element.14.refs_0_), channel_id=1, source_target_pairs={{0,2},{1,3},{2,0},{3,1},{4,6},{5,7},{6,4},{7,5},{8,10},{9,11},{10,... | collective-permute-start | bytes 49160 | tf_op jit(solution)/shard_map/ppermute | solution.py:352
  5.6 3.2 %collective-permute-start.1 = (f32[8,512]{1,0:T(8,128)S(1)}, f32[8,512]{1,0:T(8,128)S(1)}, u32[]{:S(2)}, u32[]{:S(2)}) collective-permute-start(f32[8,512]{1,0:T(8,128)S(1)} %get-tuple-element.14.refs_0_), channel_id=1, source_target_pairs={{0,3},{1,2},{2,1},{3,0},{4,7},{5,6},{6,5},{7,4},{8,11},{9,10},{10,... | collective-permute-start | bytes 49160 | tf_op jit(solution)/shard_map/ppermute | solution.py:352
  5.6 3.2 %collective-permute-start.2 = (f32[8,512]{1,0:T(8,128)S(1)}, f32[8,512]{1,0:T(8,128)S(1)}, u32[]{:S(2)}, u32[]{:S(2)}) collective-permute-start(f32[8,512]{1,0:T(8,128)S(1)} %get-tuple-element.14.refs_0_), channel_id=1, source_target_pairs={{0,1},{1,0},{2,3},{3,2},{4,5},{5,4},{6,7},{7,6},{8,9},{9,8},{10,11... | collective-permute-start | bytes 49160 | tf_op jit(solution)/shard_map/ppermute | solution.py:352
  6.5 2.3 %copy-start.1 = (f32[512]{0:T(512)S(1)}, f32[512]{0:T(512)}, u32[]{:S(2)}) copy-start(f32[512]{0:T(512)} %param.9) | copy-start | bytes 6148
  7.2 12.8 %copy-start = (bf16[250,512]{1,0:T(8,128)(2,1)S(1)}, bf16[250,512]{1,0:T(8,128)(2,1)}, u32[]{:S(2)}) copy-start(bf16[250,512]{1,0:T(8,128)(2,1)} %outer_ref.3) | copy-start | bytes 768004
  7.2 12.8 %copy-start.2 = (f32[250]{0:T(256)S(1)}, f32[250]{0:T(256)}, u32[]{:S(2)}) copy-start(f32[250]{0:T(256)} %param.7) | copy-start | bytes 3004
  7.2 12.8 %copy-start.3 = (f32[250]{0:T(256)S(1)}, f32[250]{0:T(256)}, u32[]{:S(2)}) copy-start(f32[250]{0:T(256)} %param.8) | copy-start | bytes 3004
  9.4 5.1 %collective-permute-start.4 = (f32[264,128]{1,0:T(8,128)S(1)}, f32[264,128]{1,0:T(8,128)S(1)}, u32[]{:S(2)}, u32[]{:S(2)}) collective-permute-start(f32[264,128]{1,0:T(8,128)S(1)} %get-tuple-element.19), channel_id=1, source_target_pairs={{0,4},{4,0},{8,12},{12,8},{16,20},{20,16},{24,28},{28,24},{1,5},{5... | collective-permute-start | bytes 405512 | tf_op jit(solution)/shard_map/ppermute | solution.py:380
  10.9 7.5 %collective-permute-start.3 = (f32[264,128]{1,0:T(8,128)S(1)}, f32[264,128]{1,0:T(8,128)S(1)}, u32[]{:S(2)}, u32[]{:S(2)}) collective-permute-start(f32[264,128]{1,0:T(8,128)S(1)} %get-tuple-element.17), channel_id=1, source_target_pairs={{0,8},{4,12},{8,0},{12,4},{16,24},{20,28},{24,16},{28,20},{1,9},{5... | collective-permute-start | bytes 405512 | tf_op jit(solution)/shard_map/ppermute | solution.py:377
  14.5 6.8 %collective-permute-start.5 = (f32[136,128]{1,0:T(8,128)S(1)}, f32[136,128]{1,0:T(8,128)S(1)}, u32[]{:S(2)}, u32[]{:S(2)}) collective-permute-start(f32[136,128]{1,0:T(8,128)S(1)} %pad_maximum_fusion), channel_id=1, source_target_pairs={{0,16},{4,20},{8,24},{12,28},{16,8},{20,12},{24,0},{28,4},{1,17},{... | collective-permute-start | bytes 208904 | tf_op jit(solution)/shard_map/ppermute | solution.py:377
  17.2 5.3 %collective-permute-start.6 = (f32[136,128]{1,0:T(8,128)S(1)}, f32[136,128]{1,0:T(8,128)S(1)}, u32[]{:S(2)}, u32[]{:S(2)}) collective-permute-start(f32[136,128]{1,0:T(8,128)S(1)} %concatenate.8), channel_id=1, source_target_pairs={{0,24},{4,28},{8,16},{12,20},{16,0},{20,4},{24,8},{28,12},{1,25},{... | collective-permute-start | bytes 208904 | tf_op jit(solution)/shard_map/ppermute | solution.py:377
  18.4 4.4 %collective-permute-start.7 = (f32[136,128]{1,0:T(8,128)S(1)}, f32[136,128]{1,0:T(8,128)S(1)}, u32[]{:S(2)}, u32[]{:S(2)}) collective-permute-start(f32[136,128]{1,0:T(8,128)S(1)} %slice.16), channel_id=1, source_target_pairs={{0,4},{4,0},{8,12},{12,8},{16,20},{20,16},{24,28},{28,24},{1,5},{5... | collective-permute-start | bytes 208904 | tf_op jit(solution)/shard_map/ppermute | solution.py:380

commit v8 on v7

--- a/solution.py
+++ b/solution.py
@@ -246,6 +246,15 @@
     keep_near[2 * LANES :, :] = jnp.zeros((EXTRA, LANES), F32)
 
 
+def join_kernel(keep_ref, got_ref, *messages):
+    tail = keep_ref.shape[0] - EXTRA
+    extras = keep_ref[tail:, :] + got_ref[tail:, :]
+    for n, ref in enumerate(messages):
+        block = slice(n * LANES, (n + 1) * LANES)
+        ref[0:LANES, :] = keep_ref[block, :] + got_ref[block, :]
+        ref[LANES:, :] = extras
+
+
 def scale_kernel(inner_total, outer_ref, start_ref, vol_ref, times_ref, out_ref):
     rows = outer_ref.shape[0]
     me = lax.axis_index("path")
@@ -379,7 +388,12 @@
     def along_y(message):
         return lax.ppermute(message, "path", [(i, i ^ 1) for i in range(groups)])
 
-    far_sum = keep_far + along_y(send_far)
+    messages = pl.pallas_call(
+        join_kernel,
+        out_shape=[pltpu.VMEM((LANES + EXTRA, LANES), F32)] * half,
+        compiler_params=limit,
+        name="join",
+    )(keep_far, along_y(send_far))
     near_sum = keep_near
     for step in range(1, half):
         near_sum = near_sum + along_z(send_near[step - 1], step)
@@ -389,11 +403,8 @@
         compiler_params=limit,
         name="scale",
     )(outer_noise, start_row, vol_row, times_row)
-    far_extra = far_sum[half * LANES :]
-    arrived = []
-    for n in range(half):
-        message = jnp.concatenate([far_sum[n * LANES : (n + 1) * LANES], far_extra], axis=0)
-        arrived.append(along_z(message, half + n))
+    far_extra = messages[0][LANES:]
+    arrived = [along_z(message, half + n) for n, message in enumerate(messages)]
     arrived.append(along_y(near_sum[LANES:]))
 
     value, grad, point, point_grad = pl.pallas_call(

time: 23.8 us -> 23.7 us (level)
  no operation moved by 1% of the time
where the time goes in v8:
time: 23.7 us; the launch traced here: 23.6 us
  starting transfers between devices  11.8 us (50%)
  waiting for transfers between devices  5.95 us (25%)
  Pallas kernels  4.38 us (18%)
  between operations  0.72 us (3%)
  local copies, waits for them, and re-layouts  0.7 us (3%)
    ppermute x3, starting transfers between devices, along_z(): return lax.ppermute(message, 'path', route)  5.45 us
    ppermute x3, starting transfers between devices, paired(): lax.ppermute(lows, 'dim', [(i, i ^ s) for i in range(dims)])  3.2 us
    ppermute x2, starting transfers between devices, along_y(): return lax.ppermute(message, 'path', [(i, i ^ 1) for i in range(groups)])  3.15 us
    ppermute x2, waiting for transfers between devices, along_y(): return lax.ppermute(message, 'path', [(i, i ^ 1) for i in range(groups)])  2.27 us
    ppermute x3, waiting for transfers between devices, along_z(): return lax.ppermute(message, 'path', route)  2.18 us
    pallas_call x1, Pallas kernels, paired(): pl.pallas_call(minima_kernel, out_shape=(pltpu.VMEM((paths, points), F32)...  1.95 us
    ppermute x3, waiting for transfers between devices, paired(): lax.ppermute(lows, 'dim', [(i, i ^ s) for i in range(dims)])  1.5 us
    pallas_call x1, Pallas kernels, paired(): pl.pallas_call(functools.partial(final_kernel, inner_total, len(arrived))...  0.8 us
  transfers between devices with their start and end apart: 8, of which 6 were waited for; matrix products, arithmetic and copies ran while one was open for 3% of the time, Pallas kernels for 4%

profile of v8, /device:TPU:0, one launch (start us, length us, event | category | flops | bytes accessed | tf_op | source)
XLA Modules:
  0.0 23.6 jit_solution(16204142944127380532)
XLA Ops:
  0.6 1.9 %minima.1 = (f32[8,512]{1,0:T(8,128)S(1)}, bf16[250,8,512]{2,1,0:T(8,128)(2,1)S(1)}) custom-call(bf16[250,8,512]{2,1,0:T(8,128)(2,1)} %bitcast.22, bf16[250,512]{1,0:T(8,128)(2,1)} %outer_ref.3, f32[1,250]{1,0:T(1,128)} %bitcast.16, f32[1,250]{1,0:T(1,128)} %bitcast.19, f32[1,512]{1,0:T(1,128)} %bitcast.12), custom_call_target="tpu_custom_call" | custom-call | tf_op jit(solution)/shard_map/minima/pallas_call | solution.py:336
  2.6 3.0 %collective-permute-start = (f32[8,512]{1,0:T(8,128)S(1)}, f32[8,512]{1,0:T(8,128)S(1)}, u32[]{:S(2)}, u32[]{:S(2)}) collective-permute-start(f32[8,512]{1,0:T(8,128)S(1)} %get-tuple-element.16.refs_0_), channel_id=1, source_target_pairs={{0,2},{1,3},{2,0},{3,1},{4,6},{5,7},{6,4},{7,5},{8,10},{9,11},{10,... | collective-permute-start | bytes 49160 | tf_op jit(solution)/shard_map/ppermute | solution.py:361
  5.6 0.0 collective-permute-start.1
  5.6 0.2 collective-permute-start.2
  5.8 0.7 %copy.11 = bf16[250,8,512]{2,0,1:T(8,128)(2,1)S(1)} copy(bf16[250,8,512]{2,1,0:T(8,128)(2,1)S(1)} %get-tuple-element.17) | data formatting | bytes 4096000 | tf_op jit(solution)/shard_map/minima/pallas_call | solution.py:336
  6.5 0.0 copy-start.1
  6.5 0.7 %parts.1.refs_4_ = f32[8,8,128,128]{3,2,1,0:T(8,128)S(1)} custom-call(bf16[8,250,512]{2,1,0:T(8,128)(2,1)S(1)} %bitcast.11), custom_call_target="tpu_custom_call" | custom-call | flops 1024000 | bytes 6144000 | tf_op jit(solution)/shard_map/parts/pallas_call | solution.py:365
  7.2 0.0 copy-start
  7.2 0.0 copy-start.2
  7.2 0.0 copy-start.3
  7.3 0.1 collective-permute-done.refs_1_
  7.3 1.4 %collective-permute-done.1.refs_2_ = f32[8,512]{1,0:T(8,128)S(1)} collective-permute-done((f32[8,512]{1,0:T(8,128)S(1)}, f32[8,512]{1,0:T(8,128)S(1)}, u32[]{:S(2)}, u32[]{:S(2)}) %collective-permute-start.1) | collective-permute-done | bytes 16416 | tf_op jit(solution)/shard_map/ppermute | solution.py:361
  8.8 0.0 collective-permute-done.2.refs_3_
  8.8 0.0 copy-done.1
  8.8 0.6 %moments.1 = (f32[264,128]{1,0:T(8,128)S(1)}, f32[264,128]{1,0:T(8,128)S(1)}, f32[264,128]{1,0:T(8,128)S(1)}, f32[264,128]{1,0:T(8,128)S(1)}) custom-call(f32[8,512]{1,0:T(8,128)S(1)} %get-tuple-element.16.refs_0_, f32[8,512]{1,0:T(8,128)S(1)} %collective-permute-done.refs_1_, f32[8,512]{1,0:T(8,128)S(1)} %collective-permute-done.1.refs_2_, ...), custom_call_target="tpu_custom_call" | custom-call | tf_op jit(solution)/shard_map/moments/pallas_call | solution.py:375
  9.4 1.6 %collective-permute-start.4 = (f32[264,128]{1,0:T(8,128)S(1)}, f32[264,128]{1,0:T(8,128)S(1)}, u32[]{:S(2)}, u32[]{:S(2)}) collective-permute-start(f32[264,128]{1,0:T(8,128)S(1)} %get-tuple-element.21), channel_id=1, source_target_pairs={{0,4},{4,0},{8,12},{12,8},{16,20},{20,16},{24,28},{28,24},{1,5},{5... | collective-permute-start | bytes 405512 | tf_op jit(solution)/shard_map/ppermute | solution.py:389
  10.9 1.6 %collective-permute-start.3 = (f32[264,128]{1,0:T(8,128)S(1)}, f32[264,128]{1,0:T(8,128)S(1)}, u32[]{:S(2)}, u32[]{:S(2)}) collective-permute-start(f32[264,128]{1,0:T(8,128)S(1)} %get-tuple-element.19), channel_id=1, source_target_pairs={{0,8},{4,12},{8,0},{12,4},{16,24},{20,28},{24,16},{28,20},{1,9},{5... | collective-permute-start | bytes 405512 | tf_op jit(solution)/shard_map/ppermute | solution.py:386
  12.5 1.9 %collective-permute-done.4.got_ref = f32[264,128]{1,0:T(8,128)S(1)} collective-permute-done((f32[264,128]{1,0:T(8,128)S(1)}, f32[264,128]{1,0:T(8,128)S(1)}, u32[]{:S(2)}, u32[]{:S(2)}) %collective-permute-start.4) | collective-permute-done | bytes 135200 | tf_op jit(solution)/shard_map/ppermute | solution.py:389
  14.5 2.6 %collective-permute-start.5 = (f32[136,128]{1,0:T(8,128)S(1)}, f32[136,128]{1,0:T(8,128)S(1)}, u32[]{:S(2)}, u32[]{:S(2)}) collective-permute-start(f32[136,128]{1,0:T(8,128)S(1)} %get-tuple-element.22), channel_id=1, source_target_pairs={{0,16},{4,20},{8,24},{12,28},{16,8},{20,12},{24,0},{28,4},{1,17},{... | collective-permute-start | bytes 208904 | tf_op jit(solution)/shard_map/ppermute | solution.py:386
  17.1 1.2 %collective-permute-start.6 = (f32[136,128]{1,0:T(8,128)S(1)}, f32[136,128]{1,0:T(8,128)S(1)}, u32[]{:S(2)}, u32[]{:S(2)}) collective-permute-start(f32[136,128]{1,0:T(8,128)S(1)} %get-tuple-element.23), channel_id=1, source_target_pairs={{0,24},{4,28},{8,16},{12,20},{16,0},{20,4},{24,8},{28,12},{1,25},{... | collective-permute-start | bytes 208904 | tf_op jit(solution)/shard_map/ppermute | solution.py:386
  18.4 0.0 collective-permute-done.3
  18.4 1.6 %collective-permute-start.7 = (f32[136,128]{1,0:T(8,128)S(1)}, f32[136,128]{1,0:T(8,128)S(1)}, u32[]{:S(2)}, u32[]{:S(2)}) collective-permute-start(f32[136,128]{1,0:T(8,128)S(1)} %slice.8), channel_id=1, source_target_pairs={{0,4},{4,0},{8,12},{12,8},{16,20},{20,16},{24,28},{28,24},{1,5},{5... | collective-permute-start | bytes 208904 | tf_op jit(solution)/shard_map/ppermute | solution.py:389
  20.0 0.0 copy-done
  20.0 0.0 copy-done.2
  20.0 0.0 copy-done.3
  20.0 0.3 %scale.1.scale_ref = f32[128,128]{1,0:T(8,128)S(1)} custom-call(bf16[250,512]{1,0:T(8,128)(2,1)S(1)} %copy-done, f32[1,250]{1,0:T(1,128)S(1)} %bitcast.17, f32[1,250]{1,0:T(1,128)S(1)} %bitcast.20, f32[1,512]{1,0:T(1,128)S(1)} %bitcast.14), custom_call_target="tpu_custom_call" | custom-call | tf_op jit(solution)/shard_map/scale/pallas_call | solution.py:400
  20.3 1.0 %collective-permute-done.5.rest_0_ = f32[136,128]{1,0:T(8,128)S(1)} collective-permute-done((f32[136,128]{1,0:T(8,128)S(1)}, f32[136,128]{1,0:T(8,128)S(1)}, u32[]{:S(2)}, u32[]{:S(2)}) %collective-permute-start.5) | collective-permute-done | bytes 69664 | tf_op jit(solution)/shard_map/ppermute | solution.py:386
  21.3 1.1 %collective-permute-done.6.rest_1_ = f32[136,128]{1,0:T(8,128)S(1)} collective-permute-done((f32[136,128]{1,0:T(8,128)S(1)}, f32[136,128]{1,0:T(8,128)S(1)}, u32[]{:S(2)}, u32[]{:S(2)}) %collective-permute-start.6) | collective-permute-done | bytes 69664 | tf_op jit(solution)/shard_map/ppermute | solution.py:386
  22.4 0.3 %collective-permute-done.7.rest_2_ = f32[136,128]{1,0:T(8,128)S(1)} collective-permute-done((f32[136,128]{1,0:T(8,128)S(1)}, f32[136,128]{1,0:T(8,128)S(1)}, u32[]{:S(2)}, u32[]{:S(2)}) %collective-permute-start.7) | collective-permute-done | bytes 69664 | tf_op jit(solution)/shard_map/ppermute | solution.py:389
  22.8 0.8 %final.1 = (f32[1,1]{1,0:T(1,128)}, f32[1,250]{1,0:T(1,128)}, f32[1,64]{1,0:T(1,128)}, f32[64,250]{1,0:T(8,128)}) custom-call(f32[264,128]{1,0:T(8,128)S(1)} %add.3.near_ref, f32[8,128]{1,0:T(8,128)S(1)} %slice.6.far_extra_ref, f32[128,128]{1,0:T(8,128)S(1)} %scale.1.scale_ref, bf16[250,512]{1,0:T(8,128)(2,1)S(1)} %copy-done, f32[1,250]{1,0:T(1,128)S(1)} %bitcast.18, ...), custom_call_target="tpu_custom_call" | custom-call | tf_op jit(solution)/shard_map/final/pallas_call | solution.py:410
  (4 shorter events, 0.0 us)
Async XLA Ops:
  2.6 4.7 %collective-permute-start = (f32[8,512]{1,0:T(8,128)S(1)}, f32[8,512]{1,0:T(8,128)S(1)}, u32[]{:S(2)}, u32[]{:S(2)}) collective-permute-start(f32[8,512]{1,0:T(8,128)S(1)} %get-tuple-element.16.refs_0_), channel_id=1, source_target_pairs={{0,2},{1,3},{2,0},{3,1},{4,6},{5,7},{6,4},{7,5},{8,10},{9,11},{10,... | collective-permute-start | bytes 49160 | tf_op jit(solution)/shard_map/ppermute | solution.py:361
  5.6 3.2 %collective-permute-start.1 = (f32[8,512]{1,0:T(8,128)S(1)}, f32[8,512]{1,0:T(8,128)S(1)}, u32[]{:S(2)}, u32[]{:S(2)}) collective-permute-start(f32[8,512]{1,0:T(8,128)S(1)} %get-tuple-element.16.refs_0_), channel_id=1, source_target_pairs={{0,3},{1,2},{2,1},{3,0},{4,7},{5,6},{6,5},{7,4},{8,11},{9,10},{10,... | collective-permute-start | bytes 49160 | tf_op jit(solution)/shard_map/ppermute | solution.py:361
  5.6 3.2 %collective-permute-start.2 = (f32[8,512]{1,0:T(8,128)S(1)}, f32[8,512]{1,0:T(8,128)S(1)}, u32[]{:S(2)}, u32[]{:S(2)}) collective-permute-start(f32[8,512]{1,0:T(8,128)S(1)} %get-tuple-element.16.refs_0_), channel_id=1, source_target_pairs={{0,1},{1,0},{2,3},{3,2},{4,5},{5,4},{6,7},{7,6},{8,9},{9,8},{10,11... | collective-permute-start | bytes 49160 | tf_op jit(solution)/shard_map/ppermute | solution.py:361
  6.5 2.3 %copy-start.1 = (f32[512]{0:T(512)S(1)}, f32[512]{0:T(512)}, u32[]{:S(2)}) copy-start(f32[512]{0:T(512)} %param.9) | copy-start | bytes 6148
  7.2 12.8 %copy-start = (bf16[250,512]{1,0:T(8,128)(2,1)S(1)}, bf16[250,512]{1,0:T(8,128)(2,1)}, u32[]{:S(2)}) copy-start(bf16[250,512]{1,0:T(8,128)(2,1)} %outer_ref.3) | copy-start | bytes 768004
  7.2 12.7 %copy-start.2 = (f32[250]{0:T(256)S(1)}, f32[250]{0:T(256)}, u32[]{:S(2)}) copy-start(f32[250]{0:T(256)} %param.7) | copy-start | bytes 3004
  7.2 12.7 %copy-start.3 = (f32[250]{0:T(256)S(1)}, f32[250]{0:T(256)}, u32[]{:S(2)}) copy-start(f32[250]{0:T(256)} %param.8) | copy-start | bytes 3004
  9.4 5.1 %collective-permute-start.4 = (f32[264,128]{1,0:T(8,128)S(1)}, f32[264,128]{1,0:T(8,128)S(1)}, u32[]{:S(2)}, u32[]{:S(2)}) collective-permute-start(f32[264,128]{1,0:T(8,128)S(1)} %get-tuple-element.21), channel_id=1, source_target_pairs={{0,4},{4,0},{8,12},{12,8},{16,20},{20,16},{24,28},{28,24},{1,5},{5... | collective-permute-start | bytes 405512 | tf_op jit(solution)/shard_map/ppermute | solution.py:389
  10.9 7.4 %collective-permute-start.3 = (f32[264,128]{1,0:T(8,128)S(1)}, f32[264,128]{1,0:T(8,128)S(1)}, u32[]{:S(2)}, u32[]{:S(2)}) collective-permute-start(f32[264,128]{1,0:T(8,128)S(1)} %get-tuple-element.19), channel_id=1, source_target_pairs={{0,8},{4,12},{8,0},{12,4},{16,24},{20,28},{24,16},{28,20},{1,9},{5... | collective-permute-start | bytes 405512 | tf_op jit(solution)/shard_map/ppermute | solution.py:386
  14.5 6.8 %collective-permute-start.5 = (f32[136,128]{1,0:T(8,128)S(1)}, f32[136,128]{1,0:T(8,128)S(1)}, u32[]{:S(2)}, u32[]{:S(2)}) collective-permute-start(f32[136,128]{1,0:T(8,128)S(1)} %get-tuple-element.22), channel_id=1, source_target_pairs={{0,16},{4,20},{8,24},{12,28},{16,8},{20,12},{24,0},{28,4},{1,17},{... | collective-permute-start | bytes 208904 | tf_op jit(solution)/shard_map/ppermute | solution.py:386
  17.1 5.3 %collective-permute-start.6 = (f32[136,128]{1,0:T(8,128)S(1)}, f32[136,128]{1,0:T(8,128)S(1)}, u32[]{:S(2)}, u32[]{:S(2)}) collective-permute-start(f32[136,128]{1,0:T(8,128)S(1)} %get-tuple-element.23), channel_id=1, source_target_pairs={{0,24},{4,28},{8,16},{12,20},{16,0},{20,4},{24,8},{28,12},{1,25},{... | collective-permute-start | bytes 208904 | tf_op jit(solution)/shard_map/ppermute | solution.py:386
  18.4 4.4 %collective-permute-start.7 = (f32[136,128]{1,0:T(8,128)S(1)}, f32[136,128]{1,0:T(8,128)S(1)}, u32[]{:S(2)}, u32[]{:S(2)}) collective-permute-start(f32[136,128]{1,0:T(8,128)S(1)} %slice.8), channel_id=1, source_target_pairs={{0,4},{4,0},{8,12},{12,8},{16,20},{20,16},{24,28},{28,24},{1,5},{5... | collective-permute-start | bytes 208904 | tf_op jit(solution)/shard_map/ppermute | solution.py:389

commit v9 on v8

--- a/solution.py
+++ b/solution.py
@@ -24,7 +24,7 @@
 
 
 def driver_of(value):
-    slope = jnp.clip((value - value_high) / (value_low - value_high), 0.0, 1.0)
+    slope = jnp.clip((value - value_high) * (1.0 / (value_low - value_high)), 0.0, 1.0)
     quota = gamma_high + (gamma_low - gamma_high) * slope
     return -(1.0 - delta) * quota * value - rate_free * value
 
@@ -298,18 +298,18 @@
     blocks = points // LANES
     totals = jnp.concatenate([extra[c : c + 1, :] for c in range(blocks)], axis=1)
     inner_term = jnp.concatenate([extra[blocks : blocks + 1, :], extra[blocks + 1 : blocks + 2, :]], axis=1)
-    values = totals / inner_total
+    values = totals * (1.0 / inner_total)
     driver = driver_of(values)
-    value_ref[...] = jnp.sum(totals, axis=1, keepdims=True) / (points * inner_total) + (
-        jnp.sum(driver, axis=1, keepdims=True) / points
+    value_ref[...] = jnp.sum(totals, axis=1, keepdims=True) * (1.0 / (points * inner_total)) + (
+        jnp.sum(driver, axis=1, keepdims=True) * (1.0 / points)
     )
     own = extra[0:1, :]
     for c in range(1, blocks):
         own = jnp.where(me // 2 == c, extra[c : c + 1, :], own)
-    own = jnp.where(first, own, swap_halves(own)) / inner_total
+    own = jnp.where(first, own, swap_halves(own)) * (1.0 / inner_total)
     point_ref[...] = own[:, 0:HALF]
     root_times = jnp.sqrt(times_ref[...])
-    weight = totals * root_times / inner_total + driver / root_times
+    weight = values * root_times + driver * (1.0 / root_times)
     parts_of = [part.astype(F32) for part in split(weight)]
     weights = jnp.concatenate(parts_of + [jnp.zeros((13, points), F32)], axis=0).astype(jnp.bfloat16)
     outer_term = jnp.sum(
@@ -319,9 +319,8 @@
         axis=0,
         keepdims=True,
     )
-    grad_ref[...] = (inner_term[:, 0:rows] / inner_total + outer_term) / (
-        points * vol_ref[...] * start_ref[...]
-    )
+    factor = 1.0 / (points * vol_ref[...] * start_ref[...])
+    grad_ref[...] = (inner_term[:, 0:rows] * (1.0 / inner_total) + outer_term) * factor
 
 
 def paired(inner_noise, outer_noise, start, vol, times):

time: 23.7 us -> 23.7 us (level)
  no operation moved by 1% of the time
where the time goes in v9:
time: 23.7 us; the launch traced here: 23.6 us
  starting transfers between devices  11.8 us (50%)
  waiting for transfers between devices  5.95 us (25%)
  Pallas kernels  4.37 us (18%)
  between operations  0.72 us (3%)
  local copies, waits for them, and re-layouts  0.7 us (3%)
    ppermute x3, starting transfers between devices, along_z(): return lax.ppermute(message, 'path', route)  5.45 us
    ppermute x3, starting transfers between devices, paired(): lax.ppermute(lows, 'dim', [(i, i ^ s) for i in range(dims)])  3.2 us
    ppermute x2, starting transfers between devices, along_y(): return lax.ppermute(message, 'path', [(i, i ^ 1) for i in range(groups)])  3.15 us
    ppermute x2, waiting for transfers between devices, along_y(): return lax.ppermute(message, 'path', [(i, i ^ 1) for i in range(groups)])  2.27 us
    ppermute x3, waiting for transfers between devices, along_z(): return lax.ppermute(message, 'path', route)  2.18 us
    pallas_call x1, Pallas kernels, paired(): pl.pallas_call(minima_kernel, out_shape=(pltpu.VMEM((paths, points), F32)...  1.95 us
    ppermute x3, waiting for transfers between devices, paired(): lax.ppermute(lows, 'dim', [(i, i ^ s) for i in range(dims)])  1.5 us
    pallas_call x1, Pallas kernels, paired(): pl.pallas_call(functools.partial(final_kernel, inner_total, len(arrived))...  0.79 us
  transfers between devices with their start and end apart: 8, of which 6 were waited for; matrix products, arithmetic and copies ran while one was open for 3% of the time, Pallas kernels for 4%

profile of v9, /device:TPU:0, one launch (start us, length us, event | category | flops | bytes accessed | tf_op | source)
XLA Modules:
  0.0 23.6 jit_solution(17551502125740313931)
XLA Ops:
  0.6 1.9 %minima.1 = (f32[8,512]{1,0:T(8,128)S(1)}, bf16[250,8,512]{2,1,0:T(8,128)(2,1)S(1)}) custom-call(bf16[250,8,512]{2,1,0:T(8,128)(2,1)} %bitcast.22, bf16[250,512]{1,0:T(8,128)(2,1)} %outer_ref.3, f32[1,250]{1,0:T(1,128)} %bitcast.16, f32[1,250]{1,0:T(1,128)} %bitcast.19, f32[1,512]{1,0:T(1,128)} %bitcast.12), custom_call_target="tpu_custom_call" | custom-call | tf_op jit(solution)/shard_map/minima/pallas_call | solution.py:335
  2.6 3.0 %collective-permute-start = (f32[8,512]{1,0:T(8,128)S(1)}, f32[8,512]{1,0:T(8,128)S(1)}, u32[]{:S(2)}, u32[]{:S(2)}) collective-permute-start(f32[8,512]{1,0:T(8,128)S(1)} %get-tuple-element.16.refs_0_), channel_id=1, source_target_pairs={{0,2},{1,3},{2,0},{3,1},{4,6},{5,7},{6,4},{7,5},{8,10},{9,11},{10,... | collective-permute-start | bytes 49160 | tf_op jit(solution)/shard_map/ppermute | solution.py:360
  5.6 0.0 collective-permute-start.1
  5.6 0.2 collective-permute-start.2
  5.8 0.7 %copy.11 = bf16[250,8,512]{2,0,1:T(8,128)(2,1)S(1)} copy(bf16[250,8,512]{2,1,0:T(8,128)(2,1)S(1)} %get-tuple-element.17) | data formatting | bytes 4096000 | tf_op jit(solution)/shard_map/minima/pallas_call | solution.py:335
  6.5 0.0 copy-start.1
  6.5 0.7 %parts.1.refs_4_ = f32[8,8,128,128]{3,2,1,0:T(8,128)S(1)} custom-call(bf16[8,250,512]{2,1,0:T(8,128)(2,1)S(1)} %bitcast.11), custom_call_target="tpu_custom_call" | custom-call | flops 1024000 | bytes 6144000 | tf_op jit(solution)/shard_map/parts/pallas_call | solution.py:364
  7.2 0.0 copy-start
  7.2 0.0 copy-start.2
  7.2 0.0 copy-start.3
  7.3 0.1 collective-permute-done.refs_1_
  7.3 1.4 %collective-permute-done.1.refs_2_ = f32[8,512]{1,0:T(8,128)S(1)} collective-permute-done((f32[8,512]{1,0:T(8,128)S(1)}, f32[8,512]{1,0:T(8,128)S(1)}, u32[]{:S(2)}, u32[]{:S(2)}) %collective-permute-start.1) | collective-permute-done | bytes 16416 | tf_op jit(solution)/shard_map/ppermute | solution.py:360
  8.8 0.0 collective-permute-done.2.refs_3_
  8.8 0.0 copy-done.1
  8.8 0.6 %moments.1 = (f32[264,128]{1,0:T(8,128)S(1)}, f32[264,128]{1,0:T(8,128)S(1)}, f32[264,128]{1,0:T(8,128)S(1)}, f32[264,128]{1,0:T(8,128)S(1)}) custom-call(f32[8,512]{1,0:T(8,128)S(1)} %get-tuple-element.16.refs_0_, f32[8,512]{1,0:T(8,128)S(1)} %collective-permute-done.refs_1_, f32[8,512]{1,0:T(8,128)S(1)} %collective-permute-done.1.refs_2_, ...), custom_call_target="tpu_custom_call" | custom-call | tf_op jit(solution)/shard_map/moments/pallas_call | solution.py:374
  9.4 1.6 %collective-permute-start.4 = (f32[264,128]{1,0:T(8,128)S(1)}, f32[264,128]{1,0:T(8,128)S(1)}, u32[]{:S(2)}, u32[]{:S(2)}) collective-permute-start(f32[264,128]{1,0:T(8,128)S(1)} %get-tuple-element.21), channel_id=1, source_target_pairs={{0,4},{4,0},{8,12},{12,8},{16,20},{20,16},{24,28},{28,24},{1,5},{5... | collective-permute-start | bytes 405512 | tf_op jit(solution)/shard_map/ppermute | solution.py:388
  10.9 1.6 %collective-permute-start.3 = (f32[264,128]{1,0:T(8,128)S(1)}, f32[264,128]{1,0:T(8,128)S(1)}, u32[]{:S(2)}, u32[]{:S(2)}) collective-permute-start(f32[264,128]{1,0:T(8,128)S(1)} %get-tuple-element.19), channel_id=1, source_target_pairs={{0,8},{4,12},{8,0},{12,4},{16,24},{20,28},{24,16},{28,20},{1,9},{5... | collective-permute-start | bytes 405512 | tf_op jit(solution)/shard_map/ppermute | solution.py:385
  12.5 1.9 %collective-permute-done.4.got_ref = f32[264,128]{1,0:T(8,128)S(1)} collective-permute-done((f32[264,128]{1,0:T(8,128)S(1)}, f32[264,128]{1,0:T(8,128)S(1)}, u32[]{:S(2)}, u32[]{:S(2)}) %collective-permute-start.4) | collective-permute-done | bytes 135200 | tf_op jit(solution)/shard_map/ppermute | solution.py:388
  14.5 2.6 %collective-permute-start.5 = (f32[136,128]{1,0:T(8,128)S(1)}, f32[136,128]{1,0:T(8,128)S(1)}, u32[]{:S(2)}, u32[]{:S(2)}) collective-permute-start(f32[136,128]{1,0:T(8,128)S(1)} %get-tuple-element.22), channel_id=1, source_target_pairs={{0,16},{4,20},{8,24},{12,28},{16,8},{20,12},{24,0},{28,4},{1,17},{... | collective-permute-start | bytes 208904 | tf_op jit(solution)/shard_map/ppermute | solution.py:385
  17.1 1.2 %collective-permute-start.6 = (f32[136,128]{1,0:T(8,128)S(1)}, f32[136,128]{1,0:T(8,128)S(1)}, u32[]{:S(2)}, u32[]{:S(2)}) collective-permute-start(f32[136,128]{1,0:T(8,128)S(1)} %get-tuple-element.23), channel_id=1, source_target_pairs={{0,24},{4,28},{8,16},{12,20},{16,0},{20,4},{24,8},{28,12},{1,25},{... | collective-permute-start | bytes 208904 | tf_op jit(solution)/shard_map/ppermute | solution.py:385
  18.4 0.0 collective-permute-done.3
  18.4 1.6 %collective-permute-start.7 = (f32[136,128]{1,0:T(8,128)S(1)}, f32[136,128]{1,0:T(8,128)S(1)}, u32[]{:S(2)}, u32[]{:S(2)}) collective-permute-start(f32[136,128]{1,0:T(8,128)S(1)} %slice.8), channel_id=1, source_target_pairs={{0,4},{4,0},{8,12},{12,8},{16,20},{20,16},{24,28},{28,24},{1,5},{5... | collective-permute-start | bytes 208904 | tf_op jit(solution)/shard_map/ppermute | solution.py:388
  20.0 0.0 copy-done
  20.0 0.0 copy-done.2
  20.0 0.0 copy-done.3
  20.0 0.3 %scale.1.scale_ref = f32[128,128]{1,0:T(8,128)S(1)} custom-call(bf16[250,512]{1,0:T(8,128)(2,1)S(1)} %copy-done, f32[1,250]{1,0:T(1,128)S(1)} %bitcast.17, f32[1,250]{1,0:T(1,128)S(1)} %bitcast.20, f32[1,512]{1,0:T(1,128)S(1)} %bitcast.14), custom_call_target="tpu_custom_call" | custom-call | tf_op jit(solution)/shard_map/scale/pallas_call | solution.py:399
  20.3 1.0 %collective-permute-done.5.rest_0_ = f32[136,128]{1,0:T(8,128)S(1)} collective-permute-done((f32[136,128]{1,0:T(8,128)S(1)}, f32[136,128]{1,0:T(8,128)S(1)}, u32[]{:S(2)}, u32[]{:S(2)}) %collective-permute-start.5) | collective-permute-done | bytes 69664 | tf_op jit(solution)/shard_map/ppermute | solution.py:385
  21.3 1.1 %collective-permute-done.6.rest_1_ = f32[136,128]{1,0:T(8,128)S(1)} collective-permute-done((f32[136,128]{1,0:T(8,128)S(1)}, f32[136,128]{1,0:T(8,128)S(1)}, u32[]{:S(2)}, u32[]{:S(2)}) %collective-permute-start.6) | collective-permute-done | bytes 69664 | tf_op jit(solution)/shard_map/ppermute | solution.py:385
  22.4 0.3 %collective-permute-done.7.rest_2_ = f32[136,128]{1,0:T(8,128)S(1)} collective-permute-done((f32[136,128]{1,0:T(8,128)S(1)}, f32[136,128]{1,0:T(8,128)S(1)}, u32[]{:S(2)}, u32[]{:S(2)}) %collective-permute-start.7) | collective-permute-done | bytes 69664 | tf_op jit(solution)/shard_map/ppermute | solution.py:388
  22.8 0.8 %final.1 = (f32[1,1]{1,0:T(1,128)}, f32[1,250]{1,0:T(1,128)}, f32[1,64]{1,0:T(1,128)}, f32[64,250]{1,0:T(8,128)}) custom-call(f32[264,128]{1,0:T(8,128)S(1)} %add.3.near_ref, f32[8,128]{1,0:T(8,128)S(1)} %slice.6.far_extra_ref, f32[128,128]{1,0:T(8,128)S(1)} %scale.1.scale_ref, bf16[250,512]{1,0:T(8,128)(2,1)S(1)} %copy-done, f32[1,250]{1,0:T(1,128)S(1)} %bitcast.18, ...), custom_call_target="tpu_custom_call" | custom-call | tf_op jit(solution)/shard_map/final/pallas_call | solution.py:409
  (4 shorter events, 0.0 us)
Async XLA Ops:
  2.6 4.7 %collective-permute-start = (f32[8,512]{1,0:T(8,128)S(1)}, f32[8,512]{1,0:T(8,128)S(1)}, u32[]{:S(2)}, u32[]{:S(2)}) collective-permute-start(f32[8,512]{1,0:T(8,128)S(1)} %get-tuple-element.16.refs_0_), channel_id=1, source_target_pairs={{0,2},{1,3},{2,0},{3,1},{4,6},{5,7},{6,4},{7,5},{8,10},{9,11},{10,... | collective-permute-start | bytes 49160 | tf_op jit(solution)/shard_map/ppermute | solution.py:360
  5.6 3.2 %collective-permute-start.1 = (f32[8,512]{1,0:T(8,128)S(1)}, f32[8,512]{1,0:T(8,128)S(1)}, u32[]{:S(2)}, u32[]{:S(2)}) collective-permute-start(f32[8,512]{1,0:T(8,128)S(1)} %get-tuple-element.16.refs_0_), channel_id=1, source_target_pairs={{0,3},{1,2},{2,1},{3,0},{4,7},{5,6},{6,5},{7,4},{8,11},{9,10},{10,... | collective-permute-start | bytes 49160 | tf_op jit(solution)/shard_map/ppermute | solution.py:360
  5.6 3.2 %collective-permute-start.2 = (f32[8,512]{1,0:T(8,128)S(1)}, f32[8,512]{1,0:T(8,128)S(1)}, u32[]{:S(2)}, u32[]{:S(2)}) collective-permute-start(f32[8,512]{1,0:T(8,128)S(1)} %get-tuple-element.16.refs_0_), channel_id=1, source_target_pairs={{0,1},{1,0},{2,3},{3,2},{4,5},{5,4},{6,7},{7,6},{8,9},{9,8},{10,11... | collective-permute-start | bytes 49160 | tf_op jit(solution)/shard_map/ppermute | solution.py:360
  6.5 2.3 %copy-start.1 = (f32[512]{0:T(512)S(1)}, f32[512]{0:T(512)}, u32[]{:S(2)}) copy-start(f32[512]{0:T(512)} %param.9) | copy-start | bytes 6148
  7.2 12.8 %copy-start = (bf16[250,512]{1,0:T(8,128)(2,1)S(1)}, bf16[250,512]{1,0:T(8,128)(2,1)}, u32[]{:S(2)}) copy-start(bf16[250,512]{1,0:T(8,128)(2,1)} %outer_ref.3) | copy-start | bytes 768004
  7.2 12.7 %copy-start.2 = (f32[250]{0:T(256)S(1)}, f32[250]{0:T(256)}, u32[]{:S(2)}) copy-start(f32[250]{0:T(256)} %param.7) | copy-start | bytes 3004
  7.2 12.7 %copy-start.3 = (f32[250]{0:T(256)S(1)}, f32[250]{0:T(256)}, u32[]{:S(2)}) copy-start(f32[250]{0:T(256)} %param.8) | copy-start | bytes 3004
  9.4 5.1 %collective-permute-start.4 = (f32[264,128]{1,0:T(8,128)S(1)}, f32[264,128]{1,0:T(8,128)S(1)}, u32[]{:S(2)}, u32[]{:S(2)}) collective-permute-start(f32[264,128]{1,0:T(8,128)S(1)} %get-tuple-element.21), channel_id=1, source_target_pairs={{0,4},{4,0},{8,12},{12,8},{16,20},{20,16},{24,28},{28,24},{1,5},{5... | collective-permute-start | bytes 405512 | tf_op jit(solution)/shard_map/ppermute | solution.py:388
  10.9 7.4 %collective-permute-start.3 = (f32[264,128]{1,0:T(8,128)S(1)}, f32[264,128]{1,0:T(8,128)S(1)}, u32[]{:S(2)}, u32[]{:S(2)}) collective-permute-start(f32[264,128]{1,0:T(8,128)S(1)} %get-tuple-element.19), channel_id=1, source_target_pairs={{0,8},{4,12},{8,0},{12,4},{16,24},{20,28},{24,16},{28,20},{1,9},{5... | collective-permute-start | bytes 405512 | tf_op jit(solution)/shard_map/ppermute | solution.py:385
  14.5 6.8 %collective-permute-start.5 = (f32[136,128]{1,0:T(8,128)S(1)}, f32[136,128]{1,0:T(8,128)S(1)}, u32[]{:S(2)}, u32[]{:S(2)}) collective-permute-start(f32[136,128]{1,0:T(8,128)S(1)} %get-tuple-element.22), channel_id=1, source_target_pairs={{0,16},{4,20},{8,24},{12,28},{16,8},{20,12},{24,0},{28,4},{1,17},{... | collective-permute-start | bytes 208904 | tf_op jit(solution)/shard_map/ppermute | solution.py:385
  17.1 5.3 %collective-permute-start.6 = (f32[136,128]{1,0:T(8,128)S(1)}, f32[136,128]{1,0:T(8,128)S(1)}, u32[]{:S(2)}, u32[]{:S(2)}) collective-permute-start(f32[136,128]{1,0:T(8,128)S(1)} %get-tuple-element.23), channel_id=1, source_target_pairs={{0,24},{4,28},{8,16},{12,20},{16,0},{20,4},{24,8},{28,12},{1,25},{... | collective-permute-start | bytes 208904 | tf_op jit(solution)/shard_map/ppermute | solution.py:385
  18.4 4.4 %collective-permute-start.7 = (f32[136,128]{1,0:T(8,128)S(1)}, f32[136,128]{1,0:T(8,128)S(1)}, u32[]{:S(2)}, u32[]{:S(2)}) collective-permute-start(f32[136,128]{1,0:T(8,128)S(1)} %slice.8), channel_id=1, source_target_pairs={{0,4},{4,0},{8,12},{12,8},{16,20},{20,16},{24,28},{28,24},{1,5},{5... | collective-permute-start | bytes 208904 | tf_op jit(solution)/shard_map/ppermute | solution.py:388

commit v10 on v8

--- a/solution.py
+++ b/solution.py
@@ -18,7 +18,7 @@
 LANES = 128
 HALF = LANES // 2
 EXTRA = 8
-CHUNKS = 8
+CHUNKS = 6
 STEP = 16
 F32 = jnp.float32
 

time: 23.7 us -> 23.7 us (level)
  no operation moved by 1% of the time
where the time goes in v10:
time: 23.7 us; the launch traced here: 23.5 us
  starting transfers between devices  11.8 us (50%)
  waiting for transfers between devices  5.95 us (25%)
  Pallas kernels  4.35 us (18%)
  between operations  0.72 us (3%)
  local copies, waits for them, and re-layouts  0.7 us (3%)
    ppermute x3, starting transfers between devices, along_z(): return lax.ppermute(message, 'path', route)  5.45 us
    ppermute x3, starting transfers between devices, paired(): lax.ppermute(lows, 'dim', [(i, i ^ s) for i in range(dims)])  3.2 us
    ppermute x2, starting transfers between devices, along_y(): return lax.ppermute(message, 'path', [(i, i ^ 1) for i in range(groups)])  3.15 us
    ppermute x2, waiting for transfers between devices, along_y(): return lax.ppermute(message, 'path', [(i, i ^ 1) for i in range(groups)])  2.27 us
    ppermute x3, waiting for transfers between devices, along_z(): return lax.ppermute(message, 'path', route)  2.18 us
    pallas_call x1, Pallas kernels, paired(): pl.pallas_call(minima_kernel, out_shape=(pltpu.VMEM((paths, points), F32)...  1.93 us
    ppermute x3, waiting for transfers between devices, paired(): lax.ppermute(lows, 'dim', [(i, i ^ s) for i in range(dims)])  1.5 us
    pallas_call x1, Pallas kernels, paired(): pl.pallas_call(functools.partial(final_kernel, inner_total, len(arrived))...  0.8 us
  transfers between devices with their start and end apart: 8, of which 6 were waited for; matrix products, arithmetic and copies ran while one was open for 3% of the time, Pallas kernels for 4%

profile of v10, /device:TPU:0, one launch (start us, length us, event | category | flops | bytes accessed | tf_op | source)
XLA Modules:
  0.0 23.5 jit_solution(11478463450109793476)
XLA Ops:
  0.6 1.9 %minima.1 = (f32[8,512]{1,0:T(8,128)S(1)}, bf16[250,8,512]{2,1,0:T(8,128)(2,1)S(1)}) custom-call(bf16[250,8,512]{2,1,0:T(8,128)(2,1)} %bitcast.22, bf16[250,512]{1,0:T(8,128)(2,1)} %outer_ref.3, f32[1,250]{1,0:T(1,128)} %bitcast.16, f32[1,250]{1,0:T(1,128)} %bitcast.19, f32[1,512]{1,0:T(1,128)} %bitcast.12), custom_call_target="tpu_custom_call" | custom-call | tf_op jit(solution)/shard_map/minima/pallas_call | solution.py:336
  2.6 3.0 %collective-permute-start = (f32[8,512]{1,0:T(8,128)S(1)}, f32[8,512]{1,0:T(8,128)S(1)}, u32[]{:S(2)}, u32[]{:S(2)}) collective-permute-start(f32[8,512]{1,0:T(8,128)S(1)} %get-tuple-element.16.refs_0_), channel_id=1, source_target_pairs={{0,2},{1,3},{2,0},{3,1},{4,6},{5,7},{6,4},{7,5},{8,10},{9,11},{10,... | collective-permute-start | bytes 49160 | tf_op jit(solution)/shard_map/ppermute | solution.py:361
  5.6 0.0 collective-permute-start.1
  5.6 0.2 collective-permute-start.2
  5.8 0.7 %copy.11 = bf16[250,8,512]{2,0,1:T(8,128)(2,1)S(1)} copy(bf16[250,8,512]{2,1,0:T(8,128)(2,1)S(1)} %get-tuple-element.17) | data formatting | bytes 4096000 | tf_op jit(solution)/shard_map/minima/pallas_call | solution.py:336
  6.4 0.0 copy-start.1
  6.4 0.7 %parts.1.refs_4_ = f32[8,8,128,128]{3,2,1,0:T(8,128)S(1)} custom-call(bf16[8,250,512]{2,1,0:T(8,128)(2,1)S(1)} %bitcast.11), custom_call_target="tpu_custom_call" | custom-call | flops 1024000 | bytes 6144000 | tf_op jit(solution)/shard_map/parts/pallas_call | solution.py:365
  7.2 0.0 copy-start
  7.2 0.0 copy-start.2
  7.2 0.0 copy-start.3
  7.2 0.1 collective-permute-done.refs_1_
  7.3 1.4 %collective-permute-done.1.refs_2_ = f32[8,512]{1,0:T(8,128)S(1)} collective-permute-done((f32[8,512]{1,0:T(8,128)S(1)}, f32[8,512]{1,0:T(8,128)S(1)}, u32[]{:S(2)}, u32[]{:S(2)}) %collective-permute-start.1) | collective-permute-done | bytes 16416 | tf_op jit(solution)/shard_map/ppermute | solution.py:361
  8.7 0.0 collective-permute-done.2.refs_3_
  8.7 0.0 copy-done.1
  8.7 0.6 %moments.1 = (f32[264,128]{1,0:T(8,128)S(1)}, f32[264,128]{1,0:T(8,128)S(1)}, f32[264,128]{1,0:T(8,128)S(1)}, f32[264,128]{1,0:T(8,128)S(1)}) custom-call(f32[8,512]{1,0:T(8,128)S(1)} %get-tuple-element.16.refs_0_, f32[8,512]{1,0:T(8,128)S(1)} %collective-permute-done.refs_1_, f32[8,512]{1,0:T(8,128)S(1)} %collective-permute-done.1.refs_2_, ...), custom_call_target="tpu_custom_call" | custom-call | tf_op jit(solution)/shard_map/moments/pallas_call | solution.py:375
  9.3 1.6 %collective-permute-start.4 = (f32[264,128]{1,0:T(8,128)S(1)}, f32[264,128]{1,0:T(8,128)S(1)}, u32[]{:S(2)}, u32[]{:S(2)}) collective-permute-start(f32[264,128]{1,0:T(8,128)S(1)} %get-tuple-element.21), channel_id=1, source_target_pairs={{0,4},{4,0},{8,12},{12,8},{16,20},{20,16},{24,28},{28,24},{1,5},{5... | collective-permute-start | bytes 405512 | tf_op jit(solution)/shard_map/ppermute | solution.py:389
  10.9 1.6 %collective-permute-start.3 = (f32[264,128]{1,0:T(8,128)S(1)}, f32[264,128]{1,0:T(8,128)S(1)}, u32[]{:S(2)}, u32[]{:S(2)}) collective-permute-start(f32[264,128]{1,0:T(8,128)S(1)} %get-tuple-element.19), channel_id=1, source_target_pairs={{0,8},{4,12},{8,0},{12,4},{16,24},{20,28},{24,16},{28,20},{1,9},{5... | collective-permute-start | bytes 405512 | tf_op jit(solution)/shard_map/ppermute | solution.py:386
  12.5 1.9 %collective-permute-done.4.got_ref = f32[264,128]{1,0:T(8,128)S(1)} collective-permute-done((f32[264,128]{1,0:T(8,128)S(1)}, f32[264,128]{1,0:T(8,128)S(1)}, u32[]{:S(2)}, u32[]{:S(2)}) %collective-permute-start.4) | collective-permute-done | bytes 135200 | tf_op jit(solution)/shard_map/ppermute | solution.py:389
  14.5 2.6 %collective-permute-start.5 = (f32[136,128]{1,0:T(8,128)S(1)}, f32[136,128]{1,0:T(8,128)S(1)}, u32[]{:S(2)}, u32[]{:S(2)}) collective-permute-start(f32[136,128]{1,0:T(8,128)S(1)} %get-tuple-element.22), channel_id=1, source_target_pairs={{0,16},{4,20},{8,24},{12,28},{16,8},{20,12},{24,0},{28,4},{1,17},{... | collective-permute-start | bytes 208904 | tf_op jit(solution)/shard_map/ppermute | solution.py:386
  17.1 1.2 %collective-permute-start.6 = (f32[136,128]{1,0:T(8,128)S(1)}, f32[136,128]{1,0:T(8,128)S(1)}, u32[]{:S(2)}, u32[]{:S(2)}) collective-permute-start(f32[136,128]{1,0:T(8,128)S(1)} %get-tuple-element.23), channel_id=1, source_target_pairs={{0,24},{4,28},{8,16},{12,20},{16,0},{20,4},{24,8},{28,12},{1,25},{... | collective-permute-start | bytes 208904 | tf_op jit(solution)/shard_map/ppermute | solution.py:386
  18.3 0.0 collective-permute-done.3
  18.4 1.6 %collective-permute-start.7 = (f32[136,128]{1,0:T(8,128)S(1)}, f32[136,128]{1,0:T(8,128)S(1)}, u32[]{:S(2)}, u32[]{:S(2)}) collective-permute-start(f32[136,128]{1,0:T(8,128)S(1)} %slice.8), channel_id=1, source_target_pairs={{0,4},{4,0},{8,12},{12,8},{16,20},{20,16},{24,28},{28,24},{1,5},{5... | collective-permute-start | bytes 208904 | tf_op jit(solution)/shard_map/ppermute | solution.py:389
  20.0 0.0 copy-done
  20.0 0.0 copy-done.2
  20.0 0.0 copy-done.3
  20.0 0.3 %scale.1.scale_ref = f32[128,128]{1,0:T(8,128)S(1)} custom-call(bf16[250,512]{1,0:T(8,128)(2,1)S(1)} %copy-done, f32[1,250]{1,0:T(1,128)S(1)} %bitcast.17, f32[1,250]{1,0:T(1,128)S(1)} %bitcast.20, f32[1,512]{1,0:T(1,128)S(1)} %bitcast.14), custom_call_target="tpu_custom_call" | custom-call | tf_op jit(solution)/shard_map/scale/pallas_call | solution.py:400
  20.2 1.0 %collective-permute-done.5.rest_0_ = f32[136,128]{1,0:T(8,128)S(1)} collective-permute-done((f32[136,128]{1,0:T(8,128)S(1)}, f32[136,128]{1,0:T(8,128)S(1)}, u32[]{:S(2)}, u32[]{:S(2)}) %collective-permute-start.5) | collective-permute-done | bytes 69664 | tf_op jit(solution)/shard_map/ppermute | solution.py:386
  21.3 1.1 %collective-permute-done.6.rest_1_ = f32[136,128]{1,0:T(8,128)S(1)} collective-permute-done((f32[136,128]{1,0:T(8,128)S(1)}, f32[136,128]{1,0:T(8,128)S(1)}, u32[]{:S(2)}, u32[]{:S(2)}) %collective-permute-start.6) | collective-permute-done | bytes 69664 | tf_op jit(solution)/shard_map/ppermute | solution.py:386
  22.4 0.3 %collective-permute-done.7.rest_2_ = f32[136,128]{1,0:T(8,128)S(1)} collective-permute-done((f32[136,128]{1,0:T(8,128)S(1)}, f32[136,128]{1,0:T(8,128)S(1)}, u32[]{:S(2)}, u32[]{:S(2)}) %collective-permute-start.7) | collective-permute-done | bytes 69664 | tf_op jit(solution)/shard_map/ppermute | solution.py:389
  22.7 0.8 %final.1 = (f32[1,1]{1,0:T(1,128)}, f32[1,250]{1,0:T(1,128)}, f32[1,64]{1,0:T(1,128)}, f32[64,250]{1,0:T(8,128)}) custom-call(f32[264,128]{1,0:T(8,128)S(1)} %add.3.near_ref, f32[8,128]{1,0:T(8,128)S(1)} %slice.6.far_extra_ref, f32[128,128]{1,0:T(8,128)S(1)} %scale.1.scale_ref, bf16[250,512]{1,0:T(8,128)(2,1)S(1)} %copy-done, f32[1,250]{1,0:T(1,128)S(1)} %bitcast.18, ...), custom_call_target="tpu_custom_call" | custom-call | tf_op jit(solution)/shard_map/final/pallas_call | solution.py:410
  (4 shorter events, 0.0 us)
Async XLA Ops:
  2.6 4.7 %collective-permute-start = (f32[8,512]{1,0:T(8,128)S(1)}, f32[8,512]{1,0:T(8,128)S(1)}, u32[]{:S(2)}, u32[]{:S(2)}) collective-permute-start(f32[8,512]{1,0:T(8,128)S(1)} %get-tuple-element.16.refs_0_), channel_id=1, source_target_pairs={{0,2},{1,3},{2,0},{3,1},{4,6},{5,7},{6,4},{7,5},{8,10},{9,11},{10,... | collective-permute-start | bytes 49160 | tf_op jit(solution)/shard_map/ppermute | solution.py:361
  5.6 3.2 %collective-permute-start.1 = (f32[8,512]{1,0:T(8,128)S(1)}, f32[8,512]{1,0:T(8,128)S(1)}, u32[]{:S(2)}, u32[]{:S(2)}) collective-permute-start(f32[8,512]{1,0:T(8,128)S(1)} %get-tuple-element.16.refs_0_), channel_id=1, source_target_pairs={{0,3},{1,2},{2,1},{3,0},{4,7},{5,6},{6,5},{7,4},{8,11},{9,10},{10,... | collective-permute-start | bytes 49160 | tf_op jit(solution)/shard_map/ppermute | solution.py:361
  5.6 3.2 %collective-permute-start.2 = (f32[8,512]{1,0:T(8,128)S(1)}, f32[8,512]{1,0:T(8,128)S(1)}, u32[]{:S(2)}, u32[]{:S(2)}) collective-permute-start(f32[8,512]{1,0:T(8,128)S(1)} %get-tuple-element.16.refs_0_), channel_id=1, source_target_pairs={{0,1},{1,0},{2,3},{3,2},{4,5},{5,4},{6,7},{7,6},{8,9},{9,8},{10,11... | collective-permute-start | bytes 49160 | tf_op jit(solution)/shard_map/ppermute | solution.py:361
  6.4 2.3 %copy-start.1 = (f32[512]{0:T(512)S(1)}, f32[512]{0:T(512)}, u32[]{:S(2)}) copy-start(f32[512]{0:T(512)} %param.9) | copy-start | bytes 6148
  7.2 12.8 %copy-start = (bf16[250,512]{1,0:T(8,128)(2,1)S(1)}, bf16[250,512]{1,0:T(8,128)(2,1)}, u32[]{:S(2)}) copy-start(bf16[250,512]{1,0:T(8,128)(2,1)} %outer_ref.3) | copy-start | bytes 768004
  7.2 12.7 %copy-start.2 = (f32[250]{0:T(256)S(1)}, f32[250]{0:T(256)}, u32[]{:S(2)}) copy-start(f32[250]{0:T(256)} %param.7) | copy-start | bytes 3004
  7.2 12.7 %copy-start.3 = (f32[250]{0:T(256)S(1)}, f32[250]{0:T(256)}, u32[]{:S(2)}) copy-start(f32[250]{0:T(256)} %param.8) | copy-start | bytes 3004
  9.3 5.1 %collective-permute-start.4 = (f32[264,128]{1,0:T(8,128)S(1)}, f32[264,128]{1,0:T(8,128)S(1)}, u32[]{:S(2)}, u32[]{:S(2)}) collective-permute-start(f32[264,128]{1,0:T(8,128)S(1)} %get-tuple-element.21), channel_id=1, source_target_pairs={{0,4},{4,0},{8,12},{12,8},{16,20},{20,16},{24,28},{28,24},{1,5},{5... | collective-permute-start | bytes 405512 | tf_op jit(solution)/shard_map/ppermute | solution.py:389
  10.9 7.4 %collective-permute-start.3 = (f32[264,128]{1,0:T(8,128)S(1)}, f32[264,128]{1,0:T(8,128)S(1)}, u32[]{:S(2)}, u32[]{:S(2)}) collective-permute-start(f32[264,128]{1,0:T(8,128)S(1)} %get-tuple-element.19), channel_id=1, source_target_pairs={{0,8},{4,12},{8,0},{12,4},{16,24},{20,28},{24,16},{28,20},{1,9},{5... | collective-permute-start | bytes 405512 | tf_op jit(solution)/shard_map/ppermute | solution.py:386
  14.5 6.8 %collective-permute-start.5 = (f32[136,128]{1,0:T(8,128)S(1)}, f32[136,128]{1,0:T(8,128)S(1)}, u32[]{:S(2)}, u32[]{:S(2)}) collective-permute-start(f32[136,128]{1,0:T(8,128)S(1)} %get-tuple-element.22), channel_id=1, source_target_pairs={{0,16},{4,20},{8,24},{12,28},{16,8},{20,12},{24,0},{28,4},{1,17},{... | collective-permute-start | bytes 208904 | tf_op jit(solution)/shard_map/ppermute | solution.py:386
  17.1 5.3 %collective-permute-start.6 = (f32[136,128]{1,0:T(8,128)S(1)}, f32[136,128]{1,0:T(8,128)S(1)}, u32[]{:S(2)}, u32[]{:S(2)}) collective-permute-start(f32[136,128]{1,0:T(8,128)S(1)} %get-tuple-element.23), channel_id=1, source_target_pairs={{0,24},{4,28},{8,16},{12,20},{16,0},{20,4},{24,8},{28,12},{1,25},{... | collective-permute-start | bytes 208904 | tf_op jit(solution)/shard_map/ppermute | solution.py:386
  18.4 4.4 %collective-permute-start.7 = (f32[136,128]{1,0:T(8,128)S(1)}, f32[136,128]{1,0:T(8,128)S(1)}, u32[]{:S(2)}, u32[]{:S(2)}) collective-permute-start(f32[136,128]{1,0:T(8,128)S(1)} %slice.8), channel_id=1, source_target_pairs={{0,4},{4,0},{8,12},{12,8},{16,20},{20,16},{24,28},{28,24},{1,5},{5... | collective-permute-start | bytes 208904 | tf_op jit(solution)/shard_map/ppermute | solution.py:389

commit v11 on v9

--- a/solution.py
+++ b/solution.py
@@ -18,7 +18,7 @@
 LANES = 128
 HALF = LANES // 2
 EXTRA = 8
-CHUNKS = 8
+CHUNKS = 6
 STEP = 16
 F32 = jnp.float32
 

time: 23.7 us -> 23.7 us (level)
  no operation moved by 1% of the time
where the time goes in v11:
time: 23.7 us; the launch traced here: 23.5 us
  starting transfers between devices  11.8 us (50%)
  waiting for transfers between devices  5.95 us (25%)
  Pallas kernels  4.35 us (18%)
  between operations  0.72 us (3%)
  local copies, waits for them, and re-layouts  0.7 us (3%)
    ppermute x3, starting transfers between devices, along_z(): return lax.ppermute(message, 'path', route)  5.45 us
    ppermute x3, starting transfers between devices, paired(): lax.ppermute(lows, 'dim', [(i, i ^ s) for i in range(dims)])  3.2 us
    ppermute x2, starting transfers between devices, along_y(): return lax.ppermute(message, 'path', [(i, i ^ 1) for i in range(groups)])  3.15 us
    ppermute x2, waiting for transfers between devices, along_y(): return lax.ppermute(message, 'path', [(i, i ^ 1) for i in range(groups)])  2.27 us
    ppermute x3, waiting for transfers between devices, along_z(): return lax.ppermute(message, 'path', route)  2.18 us
    pallas_call x1, Pallas kernels, paired(): pl.pallas_call(minima_kernel, out_shape=(pltpu.VMEM((paths, points), F32)...  1.93 us
    ppermute x3, waiting for transfers between devices, paired(): lax.ppermute(lows, 'dim', [(i, i ^ s) for i in range(dims)])  1.5 us
    pallas_call x1, Pallas kernels, paired(): pl.pallas_call(functools.partial(final_kernel, inner_total, len(arrived))...  0.79 us
  transfers between devices with their start and end apart: 8, of which 6 were waited for; matrix products, arithmetic and copies ran while one was open for 3% of the time, Pallas kernels for 4%

profile of v11, /device:TPU:0, one launch (start us, length us, event | category | flops | bytes accessed | tf_op | source)
XLA Modules:
  0.0 23.5 jit_solution(405510052635985052)
XLA Ops:
  0.6 1.9 %minima.1 = (f32[8,512]{1,0:T(8,128)S(1)}, bf16[250,8,512]{2,1,0:T(8,128)(2,1)S(1)}) custom-call(bf16[250,8,512]{2,1,0:T(8,128)(2,1)} %bitcast.22, bf16[250,512]{1,0:T(8,128)(2,1)} %outer_ref.3, f32[1,250]{1,0:T(1,128)} %bitcast.16, f32[1,250]{1,0:T(1,128)} %bitcast.19, f32[1,512]{1,0:T(1,128)} %bitcast.12), custom_call_target="tpu_custom_call" | custom-call | tf_op jit(solution)/shard_map/minima/pallas_call | solution.py:335
  2.6 3.0 %collective-permute-start = (f32[8,512]{1,0:T(8,128)S(1)}, f32[8,512]{1,0:T(8,128)S(1)}, u32[]{:S(2)}, u32[]{:S(2)}) collective-permute-start(f32[8,512]{1,0:T(8,128)S(1)} %get-tuple-element.16.refs_0_), channel_id=1, source_target_pairs={{0,2},{1,3},{2,0},{3,1},{4,6},{5,7},{6,4},{7,5},{8,10},{9,11},{10,... | collective-permute-start | bytes 49160 | tf_op jit(solution)/shard_map/ppermute | solution.py:360
  5.6 0.0 collective-permute-start.1
  5.6 0.2 collective-permute-start.2
  5.8 0.7 %copy.11 = bf16[250,8,512]{2,0,1:T(8,128)(2,1)S(1)} copy(bf16[250,8,512]{2,1,0:T(8,128)(2,1)S(1)} %get-tuple-element.17) | data formatting | bytes 4096000 | tf_op jit(solution)/shard_map/minima/pallas_call | solution.py:335
  6.4 0.0 copy-start.1
  6.4 0.7 %parts.1.refs_4_ = f32[8,8,128,128]{3,2,1,0:T(8,128)S(1)} custom-call(bf16[8,250,512]{2,1,0:T(8,128)(2,1)S(1)} %bitcast.11), custom_call_target="tpu_custom_call" | custom-call | flops 1024000 | bytes 6144000 | tf_op jit(solution)/shard_map/parts/pallas_call | solution.py:364
  7.2 0.0 copy-start
  7.2 0.0 copy-start.2
  7.2 0.0 copy-start.3
  7.2 0.1 collective-permute-done.refs_1_
  7.3 1.4 %collective-permute-done.1.refs_2_ = f32[8,512]{1,0:T(8,128)S(1)} collective-permute-done((f32[8,512]{1,0:T(8,128)S(1)}, f32[8,512]{1,0:T(8,128)S(1)}, u32[]{:S(2)}, u32[]{:S(2)}) %collective-permute-start.1) | collective-permute-done | bytes 16416 | tf_op jit(solution)/shard_map/ppermute | solution.py:360
  8.7 0.0 collective-permute-done.2.refs_3_
  8.7 0.0 copy-done.1
  8.7 0.6 %moments.1 = (f32[264,128]{1,0:T(8,128)S(1)}, f32[264,128]{1,0:T(8,128)S(1)}, f32[264,128]{1,0:T(8,128)S(1)}, f32[264,128]{1,0:T(8,128)S(1)}) custom-call(f32[8,512]{1,0:T(8,128)S(1)} %get-tuple-element.16.refs_0_, f32[8,512]{1,0:T(8,128)S(1)} %collective-permute-done.refs_1_, f32[8,512]{1,0:T(8,128)S(1)} %collective-permute-done.1.refs_2_, ...), custom_call_target="tpu_custom_call" | custom-call | tf_op jit(solution)/shard_map/moments/pallas_call | solution.py:374
  9.3 1.6 %collective-permute-start.4 = (f32[264,128]{1,0:T(8,128)S(1)}, f32[264,128]{1,0:T(8,128)S(1)}, u32[]{:S(2)}, u32[]{:S(2)}) collective-permute-start(f32[264,128]{1,0:T(8,128)S(1)} %get-tuple-element.21), channel_id=1, source_target_pairs={{0,4},{4,0},{8,12},{12,8},{16,20},{20,16},{24,28},{28,24},{1,5},{5... | collective-permute-start | bytes 405512 | tf_op jit(solution)/shard_map/ppermute | solution.py:388
  10.9 1.6 %collective-permute-start.3 = (f32[264,128]{1,0:T(8,128)S(1)}, f32[264,128]{1,0:T(8,128)S(1)}, u32[]{:S(2)}, u32[]{:S(2)}) collective-permute-start(f32[264,128]{1,0:T(8,128)S(1)} %get-tuple-element.19), channel_id=1, source_target_pairs={{0,8},{4,12},{8,0},{12,4},{16,24},{20,28},{24,16},{28,20},{1,9},{5... | collective-permute-start | bytes 405512 | tf_op jit(solution)/shard_map/ppermute | solution.py:385
  12.5 1.9 %collective-permute-done.4.got_ref = f32[264,128]{1,0:T(8,128)S(1)} collective-permute-done((f32[264,128]{1,0:T(8,128)S(1)}, f32[264,128]{1,0:T(8,128)S(1)}, u32[]{:S(2)}, u32[]{:S(2)}) %collective-permute-start.4) | collective-permute-done | bytes 135200 | tf_op jit(solution)/shard_map/ppermute | solution.py:388
  14.5 2.6 %collective-permute-start.5 = (f32[136,128]{1,0:T(8,128)S(1)}, f32[136,128]{1,0:T(8,128)S(1)}, u32[]{:S(2)}, u32[]{:S(2)}) collective-permute-start(f32[136,128]{1,0:T(8,128)S(1)} %get-tuple-element.22), channel_id=1, source_target_pairs={{0,16},{4,20},{8,24},{12,28},{16,8},{20,12},{24,0},{28,4},{1,17},{... | collective-permute-start | bytes 208904 | tf_op jit(solution)/shard_map/ppermute | solution.py:385
  17.1 1.2 %collective-permute-start.6 = (f32[136,128]{1,0:T(8,128)S(1)}, f32[136,128]{1,0:T(8,128)S(1)}, u32[]{:S(2)}, u32[]{:S(2)}) collective-permute-start(f32[136,128]{1,0:T(8,128)S(1)} %get-tuple-element.23), channel_id=1, source_target_pairs={{0,24},{4,28},{8,16},{12,20},{16,0},{20,4},{24,8},{28,12},{1,25},{... | collective-permute-start | bytes 208904 | tf_op jit(solution)/shard_map/ppermute | solution.py:385
  18.3 0.0 collective-permute-done.3
  18.4 1.6 %collective-permute-start.7 = (f32[136,128]{1,0:T(8,128)S(1)}, f32[136,128]{1,0:T(8,128)S(1)}, u32[]{:S(2)}, u32[]{:S(2)}) collective-permute-start(f32[136,128]{1,0:T(8,128)S(1)} %slice.8), channel_id=1, source_target_pairs={{0,4},{4,0},{8,12},{12,8},{16,20},{20,16},{24,28},{28,24},{1,5},{5... | collective-permute-start | bytes 208904 | tf_op jit(solution)/shard_map/ppermute | solution.py:388
  20.0 0.0 copy-done
  20.0 0.0 copy-done.2
  20.0 0.0 copy-done.3
  20.0 0.3 %scale.1.scale_ref = f32[128,128]{1,0:T(8,128)S(1)} custom-call(bf16[250,512]{1,0:T(8,128)(2,1)S(1)} %copy-done, f32[1,250]{1,0:T(1,128)S(1)} %bitcast.17, f32[1,250]{1,0:T(1,128)S(1)} %bitcast.20, f32[1,512]{1,0:T(1,128)S(1)} %bitcast.14), custom_call_target="tpu_custom_call" | custom-call | tf_op jit(solution)/shard_map/scale/pallas_call | solution.py:399
  20.2 1.0 %collective-permute-done.5.rest_0_ = f32[136,128]{1,0:T(8,128)S(1)} collective-permute-done((f32[136,128]{1,0:T(8,128)S(1)}, f32[136,128]{1,0:T(8,128)S(1)}, u32[]{:S(2)}, u32[]{:S(2)}) %collective-permute-start.5) | collective-permute-done | bytes 69664 | tf_op jit(solution)/shard_map/ppermute | solution.py:385
  21.3 1.1 %collective-permute-done.6.rest_1_ = f32[136,128]{1,0:T(8,128)S(1)} collective-permute-done((f32[136,128]{1,0:T(8,128)S(1)}, f32[136,128]{1,0:T(8,128)S(1)}, u32[]{:S(2)}, u32[]{:S(2)}) %collective-permute-start.6) | collective-permute-done | bytes 69664 | tf_op jit(solution)/shard_map/ppermute | solution.py:385
  22.4 0.3 %collective-permute-done.7.rest_2_ = f32[136,128]{1,0:T(8,128)S(1)} collective-permute-done((f32[136,128]{1,0:T(8,128)S(1)}, f32[136,128]{1,0:T(8,128)S(1)}, u32[]{:S(2)}, u32[]{:S(2)}) %collective-permute-start.7) | collective-permute-done | bytes 69664 | tf_op jit(solution)/shard_map/ppermute | solution.py:388
  22.7 0.8 %final.1 = (f32[1,1]{1,0:T(1,128)}, f32[1,250]{1,0:T(1,128)}, f32[1,64]{1,0:T(1,128)}, f32[64,250]{1,0:T(8,128)}) custom-call(f32[264,128]{1,0:T(8,128)S(1)} %add.3.near_ref, f32[8,128]{1,0:T(8,128)S(1)} %slice.6.far_extra_ref, f32[128,128]{1,0:T(8,128)S(1)} %scale.1.scale_ref, bf16[250,512]{1,0:T(8,128)(2,1)S(1)} %copy-done, f32[1,250]{1,0:T(1,128)S(1)} %bitcast.18, ...), custom_call_target="tpu_custom_call" | custom-call | tf_op jit(solution)/shard_map/final/pallas_call | solution.py:409
  (4 shorter events, 0.0 us)
Async XLA Ops:
  2.6 4.7 %collective-permute-start = (f32[8,512]{1,0:T(8,128)S(1)}, f32[8,512]{1,0:T(8,128)S(1)}, u32[]{:S(2)}, u32[]{:S(2)}) collective-permute-start(f32[8,512]{1,0:T(8,128)S(1)} %get-tuple-element.16.refs_0_), channel_id=1, source_target_pairs={{0,2},{1,3},{2,0},{3,1},{4,6},{5,7},{6,4},{7,5},{8,10},{9,11},{10,... | collective-permute-start | bytes 49160 | tf_op jit(solution)/shard_map/ppermute | solution.py:360
  5.6 3.2 %collective-permute-start.1 = (f32[8,512]{1,0:T(8,128)S(1)}, f32[8,512]{1,0:T(8,128)S(1)}, u32[]{:S(2)}, u32[]{:S(2)}) collective-permute-start(f32[8,512]{1,0:T(8,128)S(1)} %get-tuple-element.16.refs_0_), channel_id=1, source_target_pairs={{0,3},{1,2},{2,1},{3,0},{4,7},{5,6},{6,5},{7,4},{8,11},{9,10},{10,... | collective-permute-start | bytes 49160 | tf_op jit(solution)/shard_map/ppermute | solution.py:360
  5.6 3.2 %collective-permute-start.2 = (f32[8,512]{1,0:T(8,128)S(1)}, f32[8,512]{1,0:T(8,128)S(1)}, u32[]{:S(2)}, u32[]{:S(2)}) collective-permute-start(f32[8,512]{1,0:T(8,128)S(1)} %get-tuple-element.16.refs_0_), channel_id=1, source_target_pairs={{0,1},{1,0},{2,3},{3,2},{4,5},{5,4},{6,7},{7,6},{8,9},{9,8},{10,11... | collective-permute-start | bytes 49160 | tf_op jit(solution)/shard_map/ppermute | solution.py:360
  6.4 2.3 %copy-start.1 = (f32[512]{0:T(512)S(1)}, f32[512]{0:T(512)}, u32[]{:S(2)}) copy-start(f32[512]{0:T(512)} %param.9) | copy-start | bytes 6148
  7.2 12.8 %copy-start = (bf16[250,512]{1,0:T(8,128)(2,1)S(1)}, bf16[250,512]{1,0:T(8,128)(2,1)}, u32[]{:S(2)}) copy-start(bf16[250,512]{1,0:T(8,128)(2,1)} %outer_ref.3) | copy-start | bytes 768004
  7.2 12.7 %copy-start.2 = (f32[250]{0:T(256)S(1)}, f32[250]{0:T(256)}, u32[]{:S(2)}) copy-start(f32[250]{0:T(256)} %param.7) | copy-start | bytes 3004
  7.2 12.7 %copy-start.3 = (f32[250]{0:T(256)S(1)}, f32[250]{0:T(256)}, u32[]{:S(2)}) copy-start(f32[250]{0:T(256)} %param.8) | copy-start | bytes 3004
  9.3 5.1 %collective-permute-start.4 = (f32[264,128]{1,0:T(8,128)S(1)}, f32[264,128]{1,0:T(8,128)S(1)}, u32[]{:S(2)}, u32[]{:S(2)}) collective-permute-start(f32[264,128]{1,0:T(8,128)S(1)} %get-tuple-element.21), channel_id=1, source_target_pairs={{0,4},{4,0},{8,12},{12,8},{16,20},{20,16},{24,28},{28,24},{1,5},{5... | collective-permute-start | bytes 405512 | tf_op jit(solution)/shard_map/ppermute | solution.py:388
  10.9 7.4 %collective-permute-start.3 = (f32[264,128]{1,0:T(8,128)S(1)}, f32[264,128]{1,0:T(8,128)S(1)}, u32[]{:S(2)}, u32[]{:S(2)}) collective-permute-start(f32[264,128]{1,0:T(8,128)S(1)} %get-tuple-element.19), channel_id=1, source_target_pairs={{0,8},{4,12},{8,0},{12,4},{16,24},{20,28},{24,16},{28,20},{1,9},{5... | collective-permute-start | bytes 405512 | tf_op jit(solution)/shard_map/ppermute | solution.py:385
  14.5 6.8 %collective-permute-start.5 = (f32[136,128]{1,0:T(8,128)S(1)}, f32[136,128]{1,0:T(8,128)S(1)}, u32[]{:S(2)}, u32[]{:S(2)}) collective-permute-start(f32[136,128]{1,0:T(8,128)S(1)} %get-tuple-element.22), channel_id=1, source_target_pairs={{0,16},{4,20},{8,24},{12,28},{16,8},{20,12},{24,0},{28,4},{1,17},{... | collective-permute-start | bytes 208904 | tf_op jit(solution)/shard_map/ppermute | solution.py:385
  17.1 5.3 %collective-permute-start.6 = (f32[136,128]{1,0:T(8,128)S(1)}, f32[136,128]{1,0:T(8,128)S(1)}, u32[]{:S(2)}, u32[]{:S(2)}) collective-permute-start(f32[136,128]{1,0:T(8,128)S(1)} %get-tuple-element.23), channel_id=1, source_target_pairs={{0,24},{4,28},{8,16},{12,20},{16,0},{20,4},{24,8},{28,12},{1,25},{... | collective-permute-start | bytes 208904 | tf_op jit(solution)/shard_map/ppermute | solution.py:385
  18.4 4.4 %collective-permute-start.7 = (f32[136,128]{1,0:T(8,128)S(1)}, f32[136,128]{1,0:T(8,128)S(1)}, u32[]{:S(2)}, u32[]{:S(2)}) collective-permute-start(f32[136,128]{1,0:T(8,128)S(1)} %slice.8), channel_id=1, source_target_pairs={{0,4},{4,0},{8,12},{12,8},{16,20},{20,16},{24,28},{28,24},{1,5},{5... | collective-permute-start | bytes 208904 | tf_op jit(solution)/shard_map/ppermute | solution.py:388
